TPU v7x, 32 devices: a whole 2x2x4 slice. The times are simulated.
32 devices in a mesh: row: 4 (over x, core), col: 8 (over z, y).
Axes of the slice: x: 2, y: 2, z: 4, core: 2. Of those that a mesh axis runs over, the one named last changes fastest.
Arguments:
- covariance: float32 [8192, 8192], P('row', 'col'), may hold values from -8 to 8, as said below
- couplings: float32 [64, 9, 128, 128], P('row'), may hold values from -0.1875 to 0.1875
- block_columns: int32 [64, 9], replicated, may hold values from 0 to 63, as said below
- onsite: float32 [64], replicated, may hold values from 0.04 to 0.2
Outputs:
- new_covariance: float32 [8192, 8192], P('row', 'col')
Inputs may be any that keep to these rules, and one draw needn't show every extreme that they name: `block_columns`: each block row's 9 block columns are distinct and lie within 5 blocks of the row, counted cyclically over the 64 blocks; every row has one block column at distance 5 on each side. The covariance is skew-symmetric.
All inputs are finite; a program needn't handle non-finite values.
Results may differ from a plain program's by a relative error of at most 0.0001.
Values sent between devices are 32-bit elements; how exact they have to be, the bound alone decides.
No kernel may reach another device: no remote copies, remote signals or barrier semaphores. Data moves between devices by JAX's collectives and lax.ppermute only.
A program may use at most 256 MiB of HBM per device.

v0:
```python
import jax
import jax.numpy as jnp
from jax import lax
from jax.sharding import PartitionSpec as P

BLOCK = 128
REACH = 5


step_size = 0.25


def from_root(block, axis, holder):
    block = jnp.where(lax.axis_index(axis) == holder, block, jnp.zeros_like(block))
    return lax.psum(block, axis)


def shifted(block, axis, distance):
    devices = range(lax.axis_size(axis))
    route = [((i - distance) % len(devices), i) for i in devices]
    return lax.ppermute(block, axis, route)


def relative_positions(columns, first_block, count, total_blocks):
    own_ids = first_block + jnp.arange(count, dtype=jnp.int32)
    relative = (columns - own_ids[:, None] + total_blocks // 2) % total_blocks - total_blocks // 2
    return jnp.arange(count, dtype=jnp.int32)[:, None] + relative + REACH


def on_device(covariance, couplings, block_columns, onsite):
    tile_rows, tile_cols = covariance.shape
    row_blocks = tile_rows // BLOCK
    col_blocks = tile_cols // BLOCK
    total_blocks = block_columns.shape[0]
    reach_cells = REACH * BLOCK
    row_hops = -(-reach_cells // tile_rows)
    col_hops = -(-reach_cells // tile_cols)
    first_row = lax.axis_index("row") * row_blocks
    first_col = lax.axis_index("col") * col_blocks
    own_offset = jnp.clip(first_col - first_row, 0, row_blocks - col_blocks)
    col_root = first_col // row_blocks
    own_couplings = lax.dynamic_slice_in_dim(couplings, own_offset, col_blocks, 0)
    col_couplings = from_root(own_couplings, "row", col_root)
    row_columns = lax.dynamic_slice_in_dim(block_columns, first_row, row_blocks, 0)
    col_columns = lax.dynamic_slice_in_dim(block_columns, first_col, col_blocks, 0)
    row_positions = relative_positions(row_columns, first_row, row_blocks, total_blocks)
    col_positions = relative_positions(col_columns, first_col, col_blocks, total_blocks)
    row_gains = lax.dynamic_slice_in_dim(onsite, first_row, row_blocks, 0)
    col_gains = lax.dynamic_slice_in_dim(onsite, first_col, col_blocks, 0)
    middle = 0.5 * (covariance + covariance)
    shaped = middle.reshape(row_blocks, BLOCK, col_blocks, BLOCK)
    picked = lax.dynamic_slice_in_dim(shaped, own_offset, col_blocks, 0)
    indices = jnp.arange(col_blocks, dtype=jnp.int32)
    local_diagonal = picked[indices, :, indices, :]
    received = []
    for root_part in range(row_blocks // col_blocks):
        received.append(from_root(local_diagonal, "col", first_row // col_blocks + root_part))
    row_diagonal = jnp.concatenate(received, axis=0)
    lower_parts = []
    upper_parts = []
    for distance in range(1, row_hops + 1):
        needed = min(tile_rows, reach_cells - (distance - 1) * tile_rows)
        to_upper = middle[tile_rows - needed :]
        to_lower = middle[:needed]
        from_lower = shifted(to_upper, "row", distance)
        from_upper = shifted(to_lower, "row", -distance)
        lower_parts.insert(0, from_lower)
        upper_parts.append(from_upper)
    extended_rows = jnp.concatenate(lower_parts + [middle] + upper_parts, axis=0).reshape(
        -1, BLOCK, tile_cols
    )
    picked_rows = jnp.take(extended_rows, row_positions, axis=0)
    left_part = jnp.einsum(
        "ikab,ikbn->ian", couplings, picked_rows, precision=lax.Precision.HIGHEST
    )
    left_part = left_part + jnp.einsum(
        "iab,ibn->ian",
        row_diagonal * row_gains[:, None, None],
        middle.reshape(row_blocks, BLOCK, tile_cols),
        precision=lax.Precision.HIGHEST,
    )
    left_part = left_part.reshape(tile_rows, tile_cols)
    col_diagonal = from_root(local_diagonal, "row", col_root)
    left_parts = []
    right_parts = []
    for distance in range(1, col_hops + 1):
        needed = min(tile_cols, reach_cells - (distance - 1) * tile_cols)
        to_right = middle[:, tile_cols - needed :]
        to_left = middle[:, :needed]
        from_left = shifted(to_right, "col", distance)
        from_right = shifted(to_left, "col", -distance)
        left_parts.insert(0, from_left)
        right_parts.append(from_right)
    extended_cols = jnp.concatenate(left_parts + [middle] + right_parts, axis=1).reshape(
        tile_rows, -1, BLOCK
    )
    picked_cols = jnp.take(extended_cols, col_positions, axis=1)
    right_part = jnp.einsum(
        "nikb,ikab->nia", picked_cols, col_couplings, precision=lax.Precision.HIGHEST
    )
    right_part = right_part + jnp.einsum(
        "nib,iab->nia",
        middle.reshape(tile_rows, col_blocks, BLOCK),
        col_diagonal * col_gains[:, None, None],
        precision=lax.Precision.HIGHEST,
    )
    right_part = right_part.reshape(tile_rows, tile_cols)
    return covariance + step_size * (left_part + right_part)


def solution(mesh):
    return jax.shard_map(
        on_device,
        mesh=mesh,
        in_specs=(P("row", "col"), P("row", None, None, None), P(), P()),
        out_specs=P("row", "col"),
        check_vma=False,
    )
```

profile of v0, /device:TPU:0, one launch (start us, length us, event | category | flops | bytes accessed | tf_op | source)
XLA Modules:
  0.0 588.8 jit_solution(2562979897797401706)
XLA Ops:
  6.5 9.7 %add_multiply_fusion = (f32[2048,1024]{1,0:T(8,128)}, f32[256,8,8,128]{3,1,2,0:T(8,128)S(1)}, f32[256,8,8,128]{3,2,1,0:T(8,128)}) fusion(f32[2048,1024]{1,0:T(8,128)} %param.4), kind=kLoop, calls=%fused_computation.22 | loop fusion | flops 4194304 | bytes 33554432 | tf_op jit(solution)/shard_map/mul | solution.py:50
  16.2 2.1 copy.44
  18.6 2.7 copy.41
  21.3 2.8 gather_fusion.1
  25.4 4.7 fusion.35
  30.6 1.9 collective-permute-start.1
  32.5 5.4 dynamic-slice_select_fusion
  38.0 8.8 %fusion.36 = (f32[2048,640]{1,0:T(8,128)}, f32[2048,640]{1,0:T(8,128)}) fusion(f32[2048,1024]{1,0:T(8,128)} %get-tuple-element.17), kind=kLoop, calls=%fused_computation.63 | loop fusion | bytes 20971520 | tf_op jit(solution)/shard_map/slice | solution.py:88
  46.7 2.2 collective-permute-start.2
  48.9 3.0 collective-permute-start.3
  53.3 168.1 %all-reduce.5.cloned.1.call-done = (f32[8,128,128]{2,1,0:T(8,128)}, f32[8,128,128]{2,1,0:T(8,128)}) async-done(((f32[8,128,128]{2,1,0:T(8,128)}, f32[8,128,128]{2,1,0:T(8,128)}), (f32[8,128,128]{2,1,0:T(8,128)}, f32[8,128,128]{2,1,0:T(8,128)})) %all-reduce.5.cloned.1.call-update) | async-done | bytes 1048592 | tf_op jit(solution)/shard_map/psum | solution.py:15
  221.4 12.4 %fusion.18 = f32[16,128,1024]{2,1,0:T(8,128)} fusion(f32[16,128,1024]{2,1,0:T(8,128)} %bitcast.44, f32[8,128,128]{2,1,0:T(8,128)} %get-tuple-element.5, f32[8,128,128]{2,1,0:T(8,128)} %get-tuple-element.6, f32[16]{0:T(128)S(1)} %dynamic_slice.20), kind=kOutput, calls=%fused_computation.25 | convolution fusion | flops 3221749760 | bytes 17825856 | tf_op jit(solution)/shard_map/iab,ibn->ian/dot_general | solution.py:76
  233.8 10.0 %pad_maximum_fusion.1 = f32[3328,1024]{1,0:T(8,128)} fusion(f32[640,1024]{1,0:T(8,128)} %collective-permute-done.1, f32[2048,1024]{1,0:T(8,128)} %get-tuple-element.17, f32[640,1024]{1,0:T(8,128)} %collective-permute-done), kind=kLoop, calls=%fused_computation.13 | loop fusion | flops 6815744 | bytes 27262976 | tf_op jit(solution)/shard_map/concatenate | solution.py:69
  243.8 31.8 %gather_fusion = f32[144,128,1024]{2,1,0:T(8,128)} fusion(f32[26,128,1024]{2,1,0:T(8,128)} %bitcast.43, s32[1024]{0:T(1024)S(1)} %pad_clamp_fusion.1), kind=kCustom, calls=%fused_computation | custom fusion | bytes 150995520 | tf_op jit(solution)/shard_map/jit(_take)/gather | solution.py:72
  275.5 50.3 %all-reduce.7.cloned.1.call-done = (f32[8,128,128]{2,1,0:T(8,128)}, f32[8,9,128,128]{3,2,1,0:T(8,128)}) async-done(((f32[8,128,128]{2,1,0:T(8,128)}, f32[8,9,128,128]{3,2,1,0:T(8,128)}), (f32[8,128,128]{2,1,0:T(8,128)}, f32[8,9,128,128]{3,2,1,0:T(8,128)})) %all-reduce.7.cloned.1.call-update) | async-done | bytes 5242896 | tf_op jit(solution)/shard_map/psum | solution.py:15
  325.9 12.2 %fusion.9 = f32[8,128,2048]{2,1,0:T(8,128)} fusion(f32[256,8,8,128]{3,2,1,0:T(8,128)} %get-tuple-element.19, f32[8,128,128]{2,1,0:T(8,128)} %get-tuple-element.7, f32[8]{0:T(128)S(1)} %dynamic_slice.23), kind=kOutput, calls=%fused_computation.14 | convolution fusion | flops 3221356544 | bytes 17301536 | tf_op jit(solution)/shard_map/nib,iab->nia/dot_general | solution.py:101
  338.1 54.7 %bitcast_add_fusion = f32[16,128,1024]{2,1,0:T(8,128)} fusion(f32[16,128,1024]{2,1,0:T(8,128)S(1)} %copy-done, f32[16,9,128,128]{3,2,1,0:T(8,128)} %param.5, f32[16,9,128,1024]{3,2,1,0:T(8,128)} %bitcast.1, pred[16,9]{1,0:T(8,128)(4,1)S(1)} %copy.31), kind=kOutput, calls=%fused_computation.17 | convolution fusion | flops 29012000768 | bytes 101712016 | tf_op jit(solution)/shard_map/ikab,ikbn->ian/dot_general | solution.py:73
  392.9 11.5 %pad_maximum_fusion = f32[2048,2304]{1,0:T(8,128)} fusion(f32[2048,640]{1,0:T(8,128)} %collective-permute-done.3, f32[2048,1024]{1,0:T(8,128)S(1)} %bitcast.46, f32[2048,640]{1,0:T(8,128)} %collective-permute-done.2), kind=kLoop, calls=%fused_computation.12 | loop fusion | flops 9437184 | bytes 37748736 | tf_op jit(solution)/shard_map/concatenate | solution.py:94
  404.4 18.8 %copy.35 = f32[2048,2304]{0,1:T(8,128)} copy(f32[2048,2304]{1,0:T(8,128)} %pad_maximum_fusion) | data formatting | bytes 37748736 | tf_op jit(solution)/shard_map/concatenate | solution.py:94
  423.2 18.6 %copy.36 = f32[2048,18,128]{2,0,1:T(8,128)} copy(f32[2048,18,128]{0,2,1:T(8,128)} %bitcast.47) | data formatting | bytes 37748736 | tf_op jit(solution)/shard_map/reshape | solution.py:94
  441.8 33.9 %gather_fusion.2 = f32[72,2048,128]{2,1,0:T(8,128)} fusion(f32[2048,18,128]{2,0,1:T(8,128)} %copy.36, s32[1024]{0:T(1024)S(1)} %pad_clamp_fusion), kind=kCustom, calls=%fused_computation.2 | custom fusion | bytes 150995232 | tf_op jit(solution)/shard_map/jit(_take)/gather | solution.py:97
  475.7 83.2 %bitcast_add_fusion.1 = f32[8,128,2048]{2,1,0:T(8,128)} fusion(f32[8,128,2048]{2,1,0:T(8,128)} %fusion.9, f32[8,9,128,128]{3,2,1,0:T(8,128)} %get-tuple-element.8, f32[8,9,2048,128]{3,2,1,0:T(8,128)} %bitcast.9, pred[8,9]{1,0:T(8,128)(4,1)S(1)} %copy-done.1), kind=kOutput, calls=%fused_computation.18 | convolution fusion | flops 29012000768 | bytes 96993352 | tf_op jit(solution)/shard_map/nikb,ikab->nia/dot_general | solution.py:98
  559.0 9.3 %copy.38 = f32[2048,1024]{1,0:T(8,128)} copy(f32[2048,1024]{0,1:T(8,128)} %bitcast.48) | data formatting | bytes 16777216 | tf_op jit(solution)/shard_map/reshape | solution.py:107
  568.3 13.7 %fusion.13 = f32[2048,1024]{1,0:T(8,128)} fusion(f32[2048,1024]{1,0:T(8,128)} %param.4, f32[2048,1024]{1,0:T(8,128)} %copy.38, f32[16,128,1024]{2,1,0:T(8,128)} %bitcast_add_fusion), kind=kLoop, calls=%fused_computation.21 | loop fusion | flops 6291456 | bytes 33554432 | tf_op jit(solution)/shard_map/add | solution.py:108
  (39 shorter events, 3.5 us)
Async XLA Ops:
  6.5 214.9 %all-reduce.5.cloned.1.call-start = ((), (), s32[]{:S(2)}) async-start(), calls=%async_computation | async-start | bytes 2097152 | tf_op jit(solution)/shard_map/psum | solution.py:15
  25.3 300.5 %all-reduce.7.cloned.1.call-start = ((), (), s32[]{:S(2)}) async-start(), calls=%async_computation.1 | async-start | bytes 10485760 | tf_op jit(solution)/shard_map/psum | solution.py:15
  30.1 203.7 %collective-permute-start = (f32[640,1024]{1,0:T(8,128)}, f32[640,1024]{1,0:T(8,128)}, u32[]{:S(2)}, u32[]{:S(2)}) collective-permute-start(f32[640,1024]{1,0:T(8,128)} %get-tuple-element.13), channel_id=1, source_target_pairs={{24,0},{0,8},{8,16},{16,24},{25,1},{1,9},{9,17},{17,25},{26,2},{2,... | collective-permute-start | bytes 7864328 | tf_op jit(solution)/shard_map/ppermute | solution.py:21
  30.6 203.2 %collective-permute-start.1 = (f32[640,1024]{1,0:T(8,128)S(1)}, f32[640,1024]{1,0:T(8,128)}, u32[]{:S(2)}, u32[]{:S(2)}) collective-permute-start(f32[640,1024]{1,0:T(8,128)S(1)} %get-tuple-element.14), channel_id=1, source_target_pairs={{8,0},{16,8},{24,16},{0,24},{9,1},{17,9},{25,17},{1,25},{10,2},{18... | collective-permute-start | bytes 7864328 | tf_op jit(solution)/shard_map/ppermute | solution.py:21
  37.9 14.0 %copy-start.3 = (f32[64]{0:T(128)S(1)}, f32[64]{0:T(128)}, u32[]{:S(2)}) copy-start(f32[64]{0:T(128)} %param.7) | copy-start | bytes 772
  37.9 14.0 %copy-start.2 = (s32[64,9]{0,1:T(8,128)S(1)}, s32[64,9]{0,1:T(8,128)}, u32[]{:S(2)}) copy-start(s32[64,9]{0,1:T(8,128)} %param.6) | copy-start | bytes 6916
  46.7 346.1 %collective-permute-start.2 = (f32[2048,640]{1,0:T(8,128)}, f32[2048,640]{1,0:T(8,128)}, u32[]{:S(2)}, u32[]{:S(2)}) collective-permute-start(f32[2048,640]{1,0:T(8,128)} %get-tuple-element.15), channel_id=1, source_target_pairs={{7,0},{0,1},{1,2},{2,3},{3,4},{4,5},{5,6},{6,7},{15,8},{8,9},{9,10... | collective-permute-start | bytes 15728648 | tf_op jit(solution)/shard_map/ppermute | solution.py:21
  48.9 343.9 %collective-permute-start.3 = (f32[2048,640]{1,0:T(8,128)}, f32[2048,640]{1,0:T(8,128)}, u32[]{:S(2)}, u32[]{:S(2)}) collective-permute-start(f32[2048,640]{1,0:T(8,128)} %get-tuple-element.16), channel_id=1, source_target_pairs={{1,0},{2,1},{3,2},{4,3},{5,4},{6,5},{7,6},{0,7},{9,8},{10,9},{11,1... | collective-permute-start | bytes 15728648 | tf_op jit(solution)/shard_map/ppermute | solution.py:21
  325.9 12.3 %copy-start = (f32[16,128,1024]{2,1,0:T(8,128)S(1)}, f32[16,128,1024]{2,1,0:T(8,128)}, u32[]{:S(2)}) copy-start(f32[16,128,1024]{2,1,0:T(8,128)} %fusion.18) | copy-start | bytes 25165828
  325.9 67.0 %slice-start = ((s8[8388608]{0:T(1024)(128)(4,1)}), s8[4194304]{0:T(1024)(128)(4,1)S(1)}, s32[]{:S(2)}) async-start(s8[8388608]{0:T(1024)(128)(4,1)} %bitcast.45), calls=%async_computation.2 | async-start | bytes 8388608
  338.1 54.8 %slice-start.1 = ((s8[8388608]{0:T(1024)(128)(4,1)}), s8[4194304]{0:T(1024)(128)(4,1)S(1)}, s32[]{:S(2)}) async-start(s8[8388608]{0:T(1024)(128)(4,1)} %bitcast.45), calls=%async_computation.3 | async-start | bytes 8388608
  441.8 33.9 %copy-start.1 = (pred[8,9]{1,0:T(8,128)(4,1)S(1)}, pred[8,9]{1,0:T(8,128)(4,1)}, u32[]{:S(2)}) copy-start(pred[8,9]{1,0:T(8,128)(4,1)} %get-tuple-element.11) | copy-start | bytes 220
Sparse Core Ops, SparseCore 0:
  25.4 195.9 all-reduce.4
  223.9 101.8 all-reduce.6
where the time goes:
time: 590 us; the launch traced here: 589 us
  waiting for transfers between devices  218 us (37%)
  matrix products  163 us (28%)
  local copies, waits for them, and re-layouts  134 us (23%)
  other arithmetic  52.1 us (9%)
  between operations  13.5 us (2%)
  starting transfers between devices  7.6 us (1%)
    psum x2, waiting for transfers between devices, from_root(): return lax.psum(block, axis)  218 us
    dot_general x1, matrix products, on_device(): jnp.einsum('nikb,ikab->nia', picked_cols, col_couplings, precision=lax.Pr...  83.2 us
    dot_general x1, matrix products, on_device(): jnp.einsum('ikab,ikbn->ian', couplings, picked_rows, precision=lax.Precis...  54.7 us
    gather x1, local copies, waits for them, and re-layouts, on_device(): picked_cols = jnp.take(extended_cols, col_positions, axis=1)  33.9 us
    gather x1, local copies, waits for them, and re-layouts, on_device(): picked_rows = jnp.take(extended_rows, row_positions, axis=0)  31.8 us
    concatenate x1, local copies, waits for them, and re-layouts, on_device(): jnp.concatenate(left_parts + [middle] + right_parts, axis=1)  18.8 us
    reshape x1, local copies, waits for them, and re-layouts, on_device(): jnp.concatenate(left_parts + [middle] + right_parts, axis=1)  18.6 us
    add x1, other arithmetic, on_device(): return covariance + step_size * (left_part + right_part)  13.7 us
  transfers between devices with their start and end apart: 6, of which 2 were waited for; matrix products, arithmetic and copies ran while one was open for 24% of the time, Pallas kernels for 0%

commit v1 on v0

--- a/solution.py
+++ b/solution.py
@@ -1,6 +1,10 @@
+import functools
+
 import jax
 import jax.numpy as jnp
 from jax import lax
+from jax.experimental import pallas as pl
+from jax.experimental.pallas import tpu as pltpu
 from jax.sharding import PartitionSpec as P
 
 BLOCK = 128
@@ -27,7 +31,7 @@
     return jnp.arange(count, dtype=jnp.int32)[:, None] + relative + REACH
 
 
-def on_device(covariance, couplings, block_columns, onsite):
+def general_step(covariance, couplings, block_columns, onsite):
     tile_rows, tile_cols = covariance.shape
     row_blocks = tile_rows // BLOCK
     col_blocks = tile_cols // BLOCK
@@ -47,7 +51,7 @@
     col_positions = relative_positions(col_columns, first_col, col_blocks, total_blocks)
     row_gains = lax.dynamic_slice_in_dim(onsite, first_row, row_blocks, 0)
     col_gains = lax.dynamic_slice_in_dim(onsite, first_col, col_blocks, 0)
-    middle = 0.5 * (covariance + covariance)
+    middle = covariance
     shaped = middle.reshape(row_blocks, BLOCK, col_blocks, BLOCK)
     picked = lax.dynamic_slice_in_dim(shaped, own_offset, col_blocks, 0)
     indices = jnp.arange(col_blocks, dtype=jnp.int32)
@@ -108,6 +112,286 @@
     return covariance + step_size * (left_part + right_part)
 
 
+GROUP = 2
+WINDOW = (GROUP + 2 * REACH) * BLOCK
+HALO = REACH * BLOCK
+VMEM = 56 * 1024 * 1024
+
+
+def halves(value):
+    high = value.astype(jnp.bfloat16)
+    return high, (value - high.astype(jnp.float32)).astype(jnp.bfloat16)
+
+
+def product(a_high, a_low, b_high, b_low, contract_b=0):
+    dims = (((1,), (contract_b,)), ((), ()))
+    dot = functools.partial(lax.dot_general, dimension_numbers=dims, preferred_element_type=jnp.float32)
+    return dot(a_high, b_high) + (dot(a_high, b_low) + dot(a_low, b_high))
+
+
+def band_kernel(places, gains, blocks, diagonal, high, low, whole, *, with_diagonal):
+    i = pl.program_id(0)
+    whole[...] = jnp.zeros_like(whole)
+    for k in range(blocks.shape[1]):
+        place = pl.multiple_of(places[i, k] * BLOCK, BLOCK)
+        whole[:, pl.ds(place, BLOCK)] = blocks[0, k]
+    if with_diagonal:
+        own = pl.multiple_of((REACH + i % GROUP) * BLOCK, BLOCK)
+        whole[:, pl.ds(own, BLOCK)] += gains[i] * diagonal[0]
+    high[...], low[...] = halves(whole[...])
+
+
+def band(blocks, columns, first_block, total_blocks, diagonal, gains):
+    count, stored = columns.shape
+    own_ids = first_block + jnp.arange(count, dtype=jnp.int32)
+    relative = (columns - own_ids[:, None] + total_blocks // 2) % total_blocks - total_blocks // 2
+    places = relative + REACH + (jnp.arange(count, dtype=jnp.int32) % GROUP)[:, None]
+    with_diagonal = diagonal is not None
+    if not with_diagonal:
+        diagonal = jnp.zeros((1, BLOCK, BLOCK), jnp.float32)
+    shape = jax.ShapeDtypeStruct((count * BLOCK, WINDOW), jnp.bfloat16)
+    return pl.pallas_call(
+        functools.partial(band_kernel, with_diagonal=with_diagonal),
+        out_shape=(shape, shape),
+        grid_spec=pltpu.PrefetchScalarGridSpec(
+            num_scalar_prefetch=2,
+            grid=(count,),
+            in_specs=[
+                pl.BlockSpec((1, stored, BLOCK, BLOCK), lambda i, *_: (i, 0, 0, 0)),
+                pl.BlockSpec((1, BLOCK, BLOCK), lambda i, *_: (i if with_diagonal else 0, 0, 0)),
+            ],
+            out_specs=[pl.BlockSpec((BLOCK, WINDOW), lambda i, *_: (i, 0))] * 2,
+            scratch_shapes=[pltpu.VMEM((BLOCK, WINDOW), jnp.float32)],
+        ),
+        compiler_params=pltpu.CompilerParams(vmem_limit_bytes=VMEM),
+        cost_estimate=pl.CostEstimate(
+            flops=0, bytes_accessed=count * BLOCK * (stored * BLOCK + WINDOW) * 4, transcendentals=0
+        ),
+        name="band",
+    )(places, gains, blocks, diagonal)
+
+
+def left_kernel(top, own, bottom, high, low, out, ext_high, ext_low):
+    rows = own.shape[0]
+    for start, part in ((0, top), (HALO, own), (HALO + rows, bottom)):
+        size = part.shape[0]
+        ext_high[start : start + size], ext_low[start : start + size] = halves(part[...])
+    step = GROUP * BLOCK
+    for g in range(rows // step):
+        here, window = slice(g * step, (g + 1) * step), slice(g * step, g * step + WINDOW)
+        value = product(high[here], low[here], ext_high[window], ext_low[window])
+        out[here] = own[here] + step_size * value
+
+
+def left_part(top, covariance, bottom, high, low, slab=256):
+    rows, cols = covariance.shape
+    whole = pl.BlockSpec((rows, WINDOW), lambda j: (0, 0), pipeline_mode=pl.Buffered(1))
+    return pl.pallas_call(
+        left_kernel,
+        out_shape=jax.ShapeDtypeStruct((rows, cols), jnp.float32),
+        grid=(cols // slab,),
+        in_specs=[
+            pl.BlockSpec((HALO, slab), lambda j: (0, j)),
+            pl.BlockSpec((rows, slab), lambda j: (0, j)),
+            pl.BlockSpec((HALO, slab), lambda j: (0, j)),
+            whole,
+            whole,
+        ],
+        out_specs=pl.BlockSpec((rows, slab), lambda j: (0, j)),
+        scratch_shapes=[pltpu.VMEM((rows + 2 * HALO, slab), jnp.bfloat16)] * 2,
+        compiler_params=pltpu.CompilerParams(vmem_limit_bytes=VMEM),
+        cost_estimate=pl.CostEstimate(
+            flops=6 * rows * cols * WINDOW, bytes_accessed=12 * rows * cols, transcendentals=0
+        ),
+        name="left_part",
+    )(top, covariance, bottom, high, low)
+
+
+def right_kernel(odd, pair, strip, own, row_diagonal, high, low, total, out, ext_high, ext_low):
+    rows, cols = own.shape
+
+    def put(start, value):
+        end = start + value.shape[1]
+        ext_high[:, start:end], ext_low[:, start:end] = halves(value)
+
+    put(HALO, own[...])
+
+    @pl.when(odd[0] == 0)
+    def _():
+        put(0, strip[...])
+        put(HALO + cols, pair[:, :HALO])
+
+    @pl.when(odd[0] == 1)
+    def _():
+        put(0, pair[:, cols - HALO :])
+        put(HALO + cols, strip[...])
+
+    step = GROUP * BLOCK
+    for g in range(cols // step):
+        here, window = slice(g * step, (g + 1) * step), slice(g * step, g * step + WINDOW)
+        value = product(ext_high[:, window], ext_low[:, window], high[here], low[here], 1)
+        out[:, here] = total[:, here] + step_size * value
+    for b in range(rows // BLOCK):
+        here, mine = slice(b * BLOCK, (b + 1) * BLOCK), slice(HALO, HALO + cols)
+        onsite_high, onsite_low = halves(row_diagonal[b])
+        value = product(onsite_high, onsite_low, ext_high[here, mine], ext_low[here, mine])
+        out[here] += step_size * value
+
+
+def right_part(first, odd, pair, strip, covariance, row_diagonal, high, low, total, rows):
+    cols = covariance.shape[1]
+    count = pair.shape[0] // rows
+    scalars = jnp.stack([odd, first // rows]).astype(jnp.int32)
+    whole = pl.BlockSpec(high.shape, lambda j, s: (0, 0), pipeline_mode=pl.Buffered(1))
+    there = pl.BlockSpec((rows, cols), lambda j, s: (s[1] + j, 0))
+    return pl.pallas_call(
+        right_kernel,
+        out_shape=jax.ShapeDtypeStruct(total.shape, jnp.float32),
+        grid_spec=pltpu.PrefetchScalarGridSpec(
+            num_scalar_prefetch=1,
+            grid=(count,),
+            in_specs=[
+                pl.BlockSpec((rows, cols), lambda j, s: (j, 0)),
+                pl.BlockSpec((rows, HALO), lambda j, s: (j, 0)),
+                there,
+                pl.BlockSpec((rows // BLOCK, BLOCK, BLOCK), lambda j, s: (s[1] + j, 0, 0)),
+                whole,
+                whole,
+                there,
+            ],
+            out_specs=there,
+            scratch_shapes=[pltpu.VMEM((rows, cols + 2 * HALO), jnp.bfloat16)] * 2,
+        ),
+        input_output_aliases={7: 0},
+        compiler_params=pltpu.CompilerParams(vmem_limit_bytes=VMEM),
+        cost_estimate=pl.CostEstimate(
+            flops=6 * rows * count * cols * WINDOW, bytes_accessed=18 * rows * count * cols, transcendentals=0
+        ),
+        name="right_part",
+    )(scalars, pair, strip, covariance, row_diagonal, high, low, total)
+
+
+def send(value, pairs, cols):
+    return lax.ppermute(value, ("row", "col"), [(a * cols + b, c * cols + d) for (a, b), (c, d) in pairs])
+
+
+def spread_over_rows(value, mesh_rows, mesh_cols, ratio):
+    place = lax.axis_index("row") ^ (lax.axis_index("col") // ratio)
+    hop = mesh_rows // 2
+    while hop:
+        pairs = []
+        for r in range(mesh_rows):
+            for c in range(mesh_cols):
+                if (r ^ (c // ratio)) & (2 * hop - 1) == 0:
+                    pairs.append(((r, c), (r ^ hop, c)))
+        value = jnp.where(place & (2 * hop - 1) == hop, send(value, pairs, mesh_cols), value)
+        hop //= 2
+    return value
+
+
+def spread_over_cols(value, mesh_rows, mesh_cols, ratio):
+    place = (lax.axis_index("col") // ratio) ^ lax.axis_index("row")
+    hop = mesh_cols // ratio // 2
+    while hop:
+        pairs = []
+        for r in range(mesh_rows):
+            for c in range(mesh_cols):
+                if ((c // ratio) ^ r) & (2 * hop - 1) == 0:
+                    pairs.append(((r, c), (r, ((c // ratio) ^ hop) * ratio + c % ratio)))
+        value = jnp.where(place & (2 * hop - 1) == hop, send(value, pairs, mesh_cols), value)
+        hop //= 2
+    return value
+
+
+def cut(total):
+    sizes = []
+    left = total
+    while left:
+        size = max(BLOCK, (left // 4) // (2 * BLOCK) * 2 * BLOCK)
+        sizes.append(min(size, left))
+        left -= sizes[-1]
+    return sizes
+
+
+def paired_step(covariance, couplings, block_columns, onsite):
+    tile_rows, tile_cols = covariance.shape
+    row_blocks, col_blocks = tile_rows // BLOCK, tile_cols // BLOCK
+    total_blocks = block_columns.shape[0]
+    mesh_rows, mesh_cols = lax.axis_size("row"), lax.axis_size("col")
+    ratio = tile_rows // tile_cols
+    row, col = lax.axis_index("row"), lax.axis_index("col")
+    odd = col % 2
+    first_row, first_col = row * row_blocks, col * col_blocks
+    offset = jnp.clip(first_col - first_row, 0, row_blocks - col_blocks)
+    devices = [(r, c) for r in range(mesh_rows) for c in range(mesh_cols)]
+
+    top = shifted(covariance[tile_rows - HALO :], "row", 1)
+    bottom = shifted(covariance[:HALO], "row", -1)
+
+    diagonal = jnp.stack(
+        [
+            lax.dynamic_slice(covariance, ((offset + j) * BLOCK, j * BLOCK), (BLOCK, BLOCK))
+            for j in range(col_blocks)
+        ]
+    )
+    other = send(diagonal, [((r, c), (r, c ^ 1)) for r, c in devices if c // 2 == r], mesh_cols)
+    both = jnp.where(odd == 0, jnp.stack([diagonal, other]), jnp.stack([other, diagonal]))
+    row_diagonal = spread_over_cols(both.reshape(row_blocks, BLOCK, BLOCK), mesh_rows, mesh_cols, ratio)
+    row_gains = lax.dynamic_slice_in_dim(onsite, first_row, row_blocks, 0)
+    row_diagonal = row_diagonal * row_gains[:, None, None]
+
+    own_couplings = lax.dynamic_slice_in_dim(couplings, offset, col_blocks, 0)
+    col_couplings = spread_over_rows(own_couplings, mesh_rows, mesh_cols, ratio)
+    col_diagonal = spread_over_rows(diagonal, mesh_rows, mesh_cols, ratio)
+
+    pairs, strips, firsts = [], [], []
+    start = 0
+    for size in cut(tile_rows):
+        chunk = covariance[start : start + size]
+        pair = send(chunk, [((r, c), (r, c ^ 1)) for r, c in devices], mesh_cols)
+        strip = lax.dynamic_slice_in_dim(pair, (1 - odd) * (tile_cols - HALO), HALO, 1)
+        strip = send(
+            strip, [((r, c), (r, (c + (2 if c % 2 == 0 else -2)) % mesh_cols)) for r, c in devices], mesh_cols
+        )
+        pairs.append(pair)
+        strips.append(strip)
+        firsts.append(start)
+        start += size
+
+    row_columns = lax.dynamic_slice_in_dim(block_columns, first_row, row_blocks, 0)
+    row_high, row_low = band(couplings, row_columns, first_row, total_blocks, None, row_gains)
+    total = left_part(top, covariance, bottom, row_high, row_low)
+
+    col_columns = lax.dynamic_slice_in_dim(block_columns, first_col, col_blocks, 0)
+    col_gains = lax.dynamic_slice_in_dim(onsite, first_col, col_blocks, 0)
+    col_high, col_low = band(col_couplings, col_columns, first_col, total_blocks, col_diagonal, col_gains)
+    for first, pair, strip in zip(firsts, pairs, strips):
+        rows = 2 * BLOCK if pair.shape[0] % (2 * BLOCK) == 0 and first % (2 * BLOCK) == 0 else BLOCK
+        total = right_part(
+            jnp.int32(first), odd, pair, strip, covariance, row_diagonal, col_high, col_low, total, rows
+        )
+    return total
+
+
+def power_of_two(number):
+    return number & (number - 1) == 0
+
+
+def on_device(covariance, couplings, block_columns, onsite):
+    tile_rows, tile_cols = covariance.shape
+    mesh_rows, mesh_cols = lax.axis_size("row"), lax.axis_size("col")
+    fits = (
+        tile_cols >= HALO
+        and tile_cols % (GROUP * BLOCK) == 0
+        and tile_rows == 2 * tile_cols
+        and mesh_cols == 2 * mesh_rows
+        and power_of_two(mesh_rows)
+        and block_columns.shape[0] >= 2 * REACH + 2
+    )
+    step = paired_step if fits else general_step
+    return step(covariance, couplings, block_columns, onsite)
+
+
 def solution(mesh):
     return jax.shard_map(
         on_device,

time: 590 us -> 378 us (0.64)
  matrix products: 163 us -> 0 us
  Pallas kernels: 0 us -> 142 us
  waiting for transfers between devices: 218 us -> 119 us
  local copies, waits for them, and re-layouts: 134 us -> 47.5 us
  starting transfers between devices: 7.6 us -> 48.1 us
  other arithmetic: 52.1 us -> 16.7 us
  between operations: 13.5 us -> 0.27 us
    psum x2 -> x0, waiting for transfers between devices: 218 us -> none  [from_root(): return lax.psum(block, axis)]
    dot_general x4 -> x0, matrix products: 163 us -> none  [the longest x1 83.2 us: on_device(): jnp.einsum('nikb,ikab->nia', picked_cols, col_couplings, precision=lax.Pr...]
    pallas_call x0 -> x13, Pallas kernels: none -> 142 us  [the longest x10 90.1 us: right_part(): pl.pallas_call(right_kernel, out_shape=jax.ShapeDtypeStruct(total.shape,...]
    ppermute x0 -> x27, waiting for transfers between devices: none -> 119 us  [send(): lax.ppermute(value, ('row', 'col'), [(a * cols + b, c * cols + d) for (a,...]
    gather x3 -> x0, local copies, waits for them, and re-layouts: 68.5 us -> none  [the longest x1 33.9 us: on_device(): picked_cols = jnp.take(extended_cols, col_positions, axis=1)]
    ppermute x0 -> x27, starting transfers between devices: none -> 48.1 us  [send(): lax.ppermute(value, ('row', 'col'), [(a * cols + b, c * cols + d) for (a,...]
    reshape x2 -> x0, local copies, waits for them, and re-layouts: 27.9 us -> none  [the longest x1 18.6 us: on_device(): jnp.concatenate(left_parts + [middle] + right_parts, axis=1)]
    concatenate x3 -> x0, other arithmetic: 21.4 us -> none  [the longest x1 11.5 us: on_device(): jnp.concatenate(left_parts + [middle] + right_parts, axis=1)]
  transfers between devices with their start and end apart: 6 -> 29, of which waited for: 2 -> 8; matrix products, arithmetic and copies ran while one was open for 24% -> 14% of each run, Pallas kernels for 0% -> 36%
where the time goes in v1:
time: 378 us; the launch traced here: 374 us
  Pallas kernels  142 us (38%)
  waiting for transfers between devices  119 us (31%)
  starting transfers between devices  48.1 us (13%)
  local copies, waits for them, and re-layouts  47.5 us (13%)
  other arithmetic  16.7 us (4%)
    ppermute x27, waiting for transfers between devices, send(): lax.ppermute(value, ('row', 'col'), [(a * cols + b, c * cols + d) for (a,...  119 us
    pallas_call x10, Pallas kernels, right_part(): pl.pallas_call(right_kernel, out_shape=jax.ShapeDtypeStruct(total.shape,...  90.1 us
    ppermute x27, starting transfers between devices, send(): lax.ppermute(value, ('row', 'col'), [(a * cols + b, c * cols + d) for (a,...  48.1 us
    pallas_call x1, Pallas kernels, left_part(): pl.pallas_call(left_kernel, out_shape=jax.ShapeDtypeStruct((rows, cols),...  27.8 us
    pallas_call x2, Pallas kernels, band(): pl.pallas_call(functools.partial(band_kernel, with_diagonal=with_diagonal...  24.1 us
    unnamed x79, local copies, waits for them, and re-layouts  12.2 us
    dynamic_slice x10, local copies, waits for them, and re-layouts, paired_step(): lax.dynamic_slice_in_dim(pair, (1 - odd) * (tile_cols - HALO), HALO, 1)  11.4 us
    slice x3, local copies, waits for them, and re-layouts, paired_step(): chunk = covariance[start:start + size]  10.3 us
  transfers between devices with their start and end apart: 29, of which 8 were waited for; matrix products, arithmetic and copies ran while one was open for 14% of the time, Pallas kernels for 36%

profile of v1, /device:TPU:0, one launch (start us, length us, event | category | flops | bytes accessed | tf_op | source)
XLA Modules:
  0.0 373.9 jit_solution(15959330654781622939)
XLA Ops:
  0.0 5.1 %constant_dynamic-slice_fusion.10 = f32[8,9,128,128]{3,2,1,0:T(8,128)} fusion(f32[16,9,128,128]{3,2,1,0:T(8,128)} %blocks.1, s32[]{:T(128)S(6)} %min.4), kind=kLoop, calls=%fused_computation.37 | loop fusion | bytes 9437188 | tf_op jit(solution)/shard_map/dynamic_slice | solution.py:343
  5.1 6.9 %collective-permute-start.5 = (f32[8,9,128,128]{3,2,1,0:T(8,128)}, f32[8,9,128,128]{3,2,1,0:T(8,128)}, u32[]{:S(2)}, u32[]{:S(2)}) collective-permute-start(f32[8,9,128,128]{3,2,1,0:T(8,128)} %constant_dynamic-slice_fusion.10), channel_id=1, source_target_pairs={{0,16},{1,17},{10,26},{11,27},{20,4},{21,5},{30,14},{31,15}} | collective-permute-start | bytes 14155784 | tf_op jit(solution)/shard_map/ppermute | solution.py:275
  32.8 5.7 %fusion.6 = (f32[640,1024]{1,0:T(8,128)}, f32[640,1024]{1,0:T(8,128)}) fusion(f32[2048,1024]{1,0:T(8,128)} %own.21), kind=kLoop, calls=%fused_computation.54 | loop fusion | bytes 10485760 | tf_op jit(solution)/shard_map/slice | solution.py:329
  40.5 26.9 %collective-permute-done.7 = f32[8,128,128]{2,1,0:T(8,128)S(1)} collective-permute-done((f32[8,128,128]{2,1,0:T(8,128)S(1)}, f32[8,128,128]{2,1,0:T(8,128)S(1)}, u32[]{:S(2)}, u32[]{:S(2)}) %collective-permute-start.7) | collective-permute-done | bytes 524320 | tf_op jit(solution)/shard_map/ppermute | solution.py:275
  76.9 15.4 %band.3 = (bf16[2048,1536]{1,0:T(8,128)(2,1)}, bf16[2048,1536]{1,0:T(8,128)(2,1)}) custom-call(s32[16,9]{1,0:T(8,128)} %fusion.2.places, f32[16]{0:T(128)} %dynamic_slice.78.gains, f32[16,9,128,128]{3,2,1,0:T(8,128)} %blocks.1, f32[1,128,128]{2,1,0:T(8,128)} %broadcast_in_dim.2.diagonal), custom_call_target="tpu_custom_call" | custom-call | bytes 22020096 | tf_op jit(solution)/shard_map/band/pallas_call | solution.py:153
  99.6 3.8 %broadcast_select_fusion = f32[8,9,128,128]{3,2,1,0:T(8,128)S(1)} fusion(f32[8,9,128,128]{3,2,1,0:T(8,128)} %collective-permute-done.5, pred[]{:T(512)S(6)} %eq.24, f32[16,9,128,128]{3,2,1,0:T(8,128)} %blocks.1, s32[]{:T(128)S(6)} %min.4), kind=kLoop, calls=%fused_computation | loop fusion | flops 1179648 | bytes 14155781 | tf_op jit(solution)/shard_map/jit(_where)/select_n | solution.py:287
  103.5 32.2 %collective-permute-done.9.pair = f32[128,1024]{1,0:T(8,128)S(1)} collective-permute-done((f32[128,1024]{1,0:T(8,128)}, f32[128,1024]{1,0:T(8,128)S(1)}, u32[]{:S(2)}, u32[]{:S(2)}) %collective-permute-start.9) | collective-permute-done | bytes 524320 | tf_op jit(solution)/shard_map/ppermute | solution.py:275
  135.7 5.6 %collective-permute-done.pair = f32[128,1024]{1,0:T(8,128)S(1)} collective-permute-done((f32[128,1024]{1,0:T(8,128)S(1)}, f32[128,1024]{1,0:T(8,128)S(1)}, u32[]{:S(2)}, u32[]{:S(2)}) %collective-permute-start) | collective-permute-done | bytes 524320 | tf_op jit(solution)/shard_map/ppermute | solution.py:275
  143.1 4.2 %collective-permute-start.6 = (f32[8,9,128,128]{3,2,1,0:T(8,128)S(1)}, f32[8,9,128,128]{3,2,1,0:T(8,128)}, u32[]{:S(2)}, u32[]{:S(2)}) collective-permute-start(f32[8,9,128,128]{3,2,1,0:T(8,128)S(1)} %broadcast_select_fusion), channel_id=1, source_target_pairs={{0,8},{1,9},{4,12},{5,13},{10,2},{11,3},{14,6},{15,7},{16,24},{17,... | collective-permute-start | bytes 14155784 | tf_op jit(solution)/shard_map/ppermute | solution.py:275
  152.8 14.6 %collective-permute-done.19.pair = f32[256,1024]{1,0:T(8,128)S(1)} collective-permute-done((f32[256,1024]{1,0:T(8,128)S(1)}, f32[256,1024]{1,0:T(8,128)S(1)}, u32[]{:S(2)}, u32[]{:S(2)}) %collective-permute-start.19) | collective-permute-done | bytes 1048608 | tf_op jit(solution)/shard_map/ppermute | solution.py:275
  182.6 29.2 %collective-permute-done.25.pair = f32[512,1024]{1,0:T(8,128)S(1)} collective-permute-done((f32[512,1024]{1,0:T(8,128)S(1)}, f32[512,1024]{1,0:T(8,128)S(1)}, u32[]{:S(2)}, u32[]{:S(2)}) %collective-permute-start.25) | collective-permute-done | bytes 2097184 | tf_op jit(solution)/shard_map/ppermute | solution.py:275
  219.6 27.8 %left_part.1.total = f32[2048,1024]{1,0:T(8,128)} custom-call(f32[640,1024]{1,0:T(8,128)} %copy-done.32, f32[2048,1024]{1,0:T(8,128)} %own.21, f32[640,1024]{1,0:T(8,128)} %copy-done.33, bf16[2048,1536]{1,0:T(8,128)(2,1)} %get-tuple-element.11.high, bf16[2048,1536]{1,0:T(8,128)(2,1)} %get-tuple-element.12.low), custom_call_target="tpu_custom_call" | custom-call | flops 19327352832 | bytes 25165824 | tf_op jit(solution)/shard_map/left_part/pallas_call | solution.py:189
  256.6 8.7 %band.2 = (bf16[1024,1536]{1,0:T(8,128)(2,1)}, bf16[1024,1536]{1,0:T(8,128)(2,1)}) custom-call(s32[8,9]{1,0:T(8,128)} %fusion.5.places, f32[8]{0:T(128)} %dynamic_slice.80.gains, f32[8,9,128,128]{3,2,1,0:T(8,128)} %broadcast_select_fusion.1.blocks, f32[8,128,128]{2,1,0:T(8,128)} %broadcast_select_fusion.4.diagonal), custom_call_target="tpu_custom_call" | custom-call | bytes 11010048 | tf_op jit(solution)/shard_map/band/pallas_call | solution.py:153
  265.4 5.0 %collective-permute-done.26.strip = f32[512,640]{1,0:T(8,128)} collective-permute-done((f32[512,640]{1,0:T(8,128)}, f32[512,640]{1,0:T(8,128)}, u32[]{:S(2)}, u32[]{:S(2)}) %collective-permute-start.26) | collective-permute-done | bytes 1310752 | tf_op jit(solution)/shard_map/ppermute | solution.py:275
  272.8 12.9 %right_part.10.total = f32[2048,1024]{1,0:T(8,128)} custom-call(s32[2]{0:T(128)} %pad_add_fusion.9.odd, f32[512,1024]{1,0:T(8,128)} %copy-done.2, f32[512,640]{1,0:T(8,128)} %collective-permute-done.26.strip, f32[2048,1024]{1,0:T(8,128)} %own.21, f32[16,128,128]{2,1,0:T(8,128)} %select_multiply_fusion.row_diagonal, ...), custom_call_target="tpu_custom_call", output_to_operand_aliasing={{}: (7, {})} | custom-call | flops 4831838208 | bytes 9437184 | tf_op jit(solution)/shard_map/right_part/pallas_call | solution.py:247
  286.8 9.0 %right_part.11.total = f32[2048,1024]{1,0:T(8,128)} custom-call(s32[2]{0:T(128)} %pad_add_fusion.8.odd, f32[256,1024]{1,0:T(8,128)} %copy-done.4, f32[256,640]{1,0:T(8,128)} %copy-done.16, f32[2048,1024]{1,0:T(8,128)} %own.21, f32[16,128,128]{2,1,0:T(8,128)} %select_multiply_fusion.row_diagonal, ...), custom_call_target="tpu_custom_call", output_to_operand_aliasing={{}: (7, {})} | custom-call | flops 2415919104 | bytes 4718592 | tf_op jit(solution)/shard_map/right_part/pallas_call | solution.py:247
  300.1 9.0 %right_part.12.total = f32[2048,1024]{1,0:T(8,128)} custom-call(s32[2]{0:T(128)} %pad_add_fusion.7.odd, f32[256,1024]{1,0:T(8,128)} %copy-done.3, f32[256,640]{1,0:T(8,128)} %copy-done.15, f32[2048,1024]{1,0:T(8,128)} %own.21, f32[16,128,128]{2,1,0:T(8,128)} %select_multiply_fusion.row_diagonal, ...), custom_call_target="tpu_custom_call", output_to_operand_aliasing={{}: (7, {})} | custom-call | flops 2415919104 | bytes 4718592 | tf_op jit(solution)/shard_map/right_part/pallas_call | solution.py:247
  310.6 9.0 %right_part.13.total = f32[2048,1024]{1,0:T(8,128)} custom-call(s32[2]{0:T(128)} %pad_add_fusion.6.odd, f32[256,1024]{1,0:T(8,128)} %copy-done.5, f32[256,640]{1,0:T(8,128)} %copy-done.17, f32[2048,1024]{1,0:T(8,128)} %own.21, f32[16,128,128]{2,1,0:T(8,128)} %select_multiply_fusion.row_diagonal, ...), custom_call_target="tpu_custom_call", output_to_operand_aliasing={{}: (7, {})} | custom-call | flops 2415919104 | bytes 4718592 | tf_op jit(solution)/shard_map/right_part/pallas_call | solution.py:247
  320.7 8.5 %right_part.14.total = f32[2048,1024]{1,0:T(8,128)} custom-call(s32[2]{0:T(128)} %pad_add_fusion.5.odd, f32[128,1024]{1,0:T(8,128)} %copy-done.8, f32[128,640]{1,0:T(8,128)} %copy-done.22, f32[2048,1024]{1,0:T(8,128)} %own.21, f32[16,128,128]{2,1,0:T(8,128)} %select_multiply_fusion.row_diagonal, ...), custom_call_target="tpu_custom_call", output_to_operand_aliasing={{}: (7, {})} | custom-call | flops 1207959552 | bytes 2359296 | tf_op jit(solution)/shard_map/right_part/pallas_call | solution.py:247
  329.2 8.3 %right_part.15.total = f32[2048,1024]{1,0:T(8,128)} custom-call(s32[2]{0:T(128)} %pad_add_fusion.4.odd, f32[128,1024]{1,0:T(8,128)} %copy-done.7, f32[128,640]{1,0:T(8,128)} %collective-permute-done.16.strip, f32[2048,1024]{1,0:T(8,128)} %own.21, f32[16,128,128]{2,1,0:T(8,128)} %select_multiply_fusion.row_diagonal, ...), custom_call_target="tpu_custom_call", output_to_operand_aliasing={{}: (7, {})} | custom-call | flops 1207959552 | bytes 2359296 | tf_op jit(solution)/shard_map/right_part/pallas_call | solution.py:247
  338.3 8.3 %right_part.16.total = f32[2048,1024]{1,0:T(8,128)} custom-call(s32[2]{0:T(128)} %pad_add_fusion.3.odd, f32[128,1024]{1,0:T(8,128)} %copy-done.10, f32[128,640]{1,0:T(8,128)} %copy-done.23, f32[2048,1024]{1,0:T(8,128)} %own.21, f32[16,128,128]{2,1,0:T(8,128)} %select_multiply_fusion.row_diagonal, ...), custom_call_target="tpu_custom_call", output_to_operand_aliasing={{}: (7, {})} | custom-call | flops 1207959552 | bytes 2359296 | tf_op jit(solution)/shard_map/right_part/pallas_call | solution.py:247
  347.3 8.3 %right_part.17.total = f32[2048,1024]{1,0:T(8,128)} custom-call(s32[2]{0:T(128)} %pad_add_fusion.2.odd, f32[128,1024]{1,0:T(8,128)} %copy-done.9, f32[128,640]{1,0:T(8,128)} %copy-done.24, f32[2048,1024]{1,0:T(8,128)} %own.21, f32[16,128,128]{2,1,0:T(8,128)} %select_multiply_fusion.row_diagonal, ...), custom_call_target="tpu_custom_call", output_to_operand_aliasing={{}: (7, {})} | custom-call | flops 1207959552 | bytes 2359296 | tf_op jit(solution)/shard_map/right_part/pallas_call | solution.py:247
  356.4 8.3 %right_part.18.total = f32[2048,1024]{1,0:T(8,128)} custom-call(s32[2]{0:T(128)} %get-tuple-element.25.odd, f32[128,1024]{1,0:T(8,128)} %copy-done.12, f32[128,640]{1,0:T(8,128)} %copy-done.25, f32[2048,1024]{1,0:T(8,128)} %own.21, f32[16,128,128]{2,1,0:T(8,128)} %select_multiply_fusion.row_diagonal, ...), custom_call_target="tpu_custom_call", output_to_operand_aliasing={{}: (7, {})} | custom-call | flops 1207959552 | bytes 2359296 | tf_op jit(solution)/shard_map/right_part/pallas_call | solution.py:247
  365.4 8.4 %right_part.19 = f32[2048,1024]{1,0:T(8,128)} custom-call(s32[2]{0:T(128)} %get-tuple-element.24.odd, f32[128,1024]{1,0:T(8,128)} %copy-done.11, f32[128,640]{1,0:T(8,128)} %copy-done.26, f32[2048,1024]{1,0:T(8,128)} %own.21, f32[16,128,128]{2,1,0:T(8,128)} %select_multiply_fusion.row_diagonal, ...), custom_call_target="tpu_custom_call", output_to_operand_aliasing={{}: (7, {})} | custom-call | flops 1207959552 | bytes 2359296 | tf_op jit(solution)/shard_map/right_part/pallas_call | solution.py:247
  (167 shorter events, 92.3 us)
Async XLA Ops:
  5.1 92.6 %collective-permute-start.5 = (f32[8,9,128,128]{3,2,1,0:T(8,128)}, f32[8,9,128,128]{3,2,1,0:T(8,128)}, u32[]{:S(2)}, u32[]{:S(2)}) collective-permute-start(f32[8,9,128,128]{3,2,1,0:T(8,128)} %constant_dynamic-slice_fusion.10), channel_id=1, source_target_pairs={{0,16},{1,17},{10,26},{11,27},{20,4},{21,5},{30,14},{31,15}} | collective-permute-start | bytes 14155784 | tf_op jit(solution)/shard_map/ppermute | solution.py:275
  18.8 48.6 %collective-permute-start.7 = (f32[8,128,128]{2,1,0:T(8,128)S(1)}, f32[8,128,128]{2,1,0:T(8,128)S(1)}, u32[]{:S(2)}, u32[]{:S(2)}) collective-permute-start(f32[8,128,128]{2,1,0:T(8,128)S(1)} %bitcast_dynamic-update-slice_fusion), channel_id=1, source_target_pairs={{0,16},{1,17},{10,26},{11,27},{20,4},{21,5},{30,14},{31,15}} | collective-permute-start | bytes 1572872 | tf_op jit(solution)/shard_map/ppermute | solution.py:275
  20.1 49.6 %collective-permute-start.2 = (f32[8,128,128]{2,1,0:T(8,128)S(1)}, f32[8,128,128]{2,1,0:T(8,128)S(1)}, u32[]{:S(2)}, u32[]{:S(2)}) collective-permute-start(f32[8,128,128]{2,1,0:T(8,128)S(1)} %bitcast_dynamic-update-slice_fusion), channel_id=1, source_target_pairs={{0,1},{1,0},{10,11},{11,10},{20,21},{21,20},{30,31},{31,30}} | collective-permute-start | bytes 1572872 | tf_op jit(solution)/shard_map/ppermute | solution.py:275
  27.0 65.3 %collective-permute-start.17 = (f32[128,1024]{1,0:T(8,128)}, f32[128,1024]{1,0:T(8,128)S(1)}, u32[]{:S(2)}, u32[]{:S(2)}) collective-permute-start(f32[128,1024]{1,0:T(8,128)} %get-tuple-element.18), channel_id=1, source_target_pairs={{0,1},{1,0},{2,3},{3,2},{4,5},{5,4},{6,7},{7,6},{8,9},{9,8},{10,11... | collective-permute-start | bytes 1572872 | tf_op jit(solution)/shard_map/ppermute | solution.py:275
  27.5 67.5 %collective-permute-start.15 = (f32[128,1024]{1,0:T(8,128)}, f32[128,1024]{1,0:T(8,128)S(1)}, u32[]{:S(2)}, u32[]{:S(2)}) collective-permute-start(f32[128,1024]{1,0:T(8,128)} %get-tuple-element.19), channel_id=1, source_target_pairs={{0,1},{1,0},{2,3},{3,2},{4,5},{5,4},{6,7},{7,6},{8,9},{9,8},{10,11... | collective-permute-start | bytes 1572872 | tf_op jit(solution)/shard_map/ppermute | solution.py:275
  92.3 50.8 %collective-permute-start.23 = (f32[256,1024]{1,0:T(8,128)}, f32[256,1024]{1,0:T(8,128)S(1)}, u32[]{:S(2)}, u32[]{:S(2)}) collective-permute-start(f32[256,1024]{1,0:T(8,128)} %get-tuple-element.15), channel_id=1, source_target_pairs={{0,1},{1,0},{2,3},{3,2},{4,5},{5,4},{6,7},{7,6},{8,9},{9,8},{10,11... | collective-permute-start | bytes 3145736 | tf_op jit(solution)/shard_map/ppermute | solution.py:275
  95.0 53.5 %collective-permute-start.21 = (f32[256,1024]{1,0:T(8,128)}, f32[256,1024]{1,0:T(8,128)S(1)}, u32[]{:S(2)}, u32[]{:S(2)}) collective-permute-start(f32[256,1024]{1,0:T(8,128)} %get-tuple-element.16), channel_id=1, source_target_pairs={{0,1},{1,0},{2,3},{3,2},{4,5},{5,4},{6,7},{7,6},{8,9},{9,8},{10,11... | collective-permute-start | bytes 3145736 | tf_op jit(solution)/shard_map/ppermute | solution.py:275
  95.6 40.0 %collective-permute-start.9 = (f32[128,1024]{1,0:T(8,128)}, f32[128,1024]{1,0:T(8,128)S(1)}, u32[]{:S(2)}, u32[]{:S(2)}) collective-permute-start(f32[128,1024]{1,0:T(8,128)} %get-tuple-element.22), channel_id=1, source_target_pairs={{0,1},{1,0},{2,3},{3,2},{4,5},{5,4},{6,7},{7,6},{8,9},{9,8},{10,11... | collective-permute-start | bytes 1572872 | tf_op jit(solution)/shard_map/ppermute | solution.py:275
  97.2 44.1 %collective-permute-start = (f32[128,1024]{1,0:T(8,128)S(1)}, f32[128,1024]{1,0:T(8,128)S(1)}, u32[]{:S(2)}, u32[]{:S(2)}) collective-permute-start(f32[128,1024]{1,0:T(8,128)S(1)} %get-tuple-element.23), channel_id=1, source_target_pairs={{0,1},{1,0},{2,3},{3,2},{4,5},{5,4},{6,7},{7,6},{8,9},{9,8},{10,11... | collective-permute-start | bytes 1572872 | tf_op jit(solution)/shard_map/ppermute | solution.py:275
  97.7 43.6 %collective-permute-start.8 = (f32[8,128,128]{2,1,0:T(8,128)S(1)}, f32[8,128,128]{2,1,0:T(8,128)S(1)}, u32[]{:S(2)}, u32[]{:S(2)}) collective-permute-start(f32[8,128,128]{2,1,0:T(8,128)S(1)} %broadcast_select_fusion.3), channel_id=1, source_target_pairs={{0,8},{1,9},{4,12},{5,13},{10,2},{11,3},{14,6},{15,7},{16,24},{17,... | collective-permute-start | bytes 1572872 | tf_op jit(solution)/shard_map/ppermute | solution.py:275
  135.7 79.5 %collective-permute-start.27 = (f32[640,1024]{1,0:T(8,128)}, f32[640,1024]{1,0:T(8,128)S(1)}, u32[]{:S(2)}, u32[]{:S(2)}) collective-permute-start(f32[640,1024]{1,0:T(8,128)} %get-tuple-element.14), channel_id=1, source_target_pairs={{24,0},{0,8},{8,16},{16,24},{25,1},{1,9},{9,17},{17,25},{26,2},{2,... | collective-permute-start | bytes 7864328 | tf_op jit(solution)/shard_map/ppermute | solution.py:25
  141.3 76.8 %collective-permute-start.28 = (f32[640,1024]{1,0:T(8,128)}, f32[640,1024]{1,0:T(8,128)S(1)}, u32[]{:S(2)}, u32[]{:S(2)}) collective-permute-start(f32[640,1024]{1,0:T(8,128)} %get-tuple-element.13), channel_id=1, source_target_pairs={{8,0},{16,8},{24,16},{0,24},{9,1},{17,9},{25,17},{1,25},{10,2},{18... | collective-permute-start | bytes 7864328 | tf_op jit(solution)/shard_map/ppermute | solution.py:25
  143.1 107.1 %collective-permute-start.6 = (f32[8,9,128,128]{3,2,1,0:T(8,128)S(1)}, f32[8,9,128,128]{3,2,1,0:T(8,128)}, u32[]{:S(2)}, u32[]{:S(2)}) collective-permute-start(f32[8,9,128,128]{3,2,1,0:T(8,128)S(1)} %broadcast_select_fusion), channel_id=1, source_target_pairs={{0,8},{1,9},{4,12},{5,13},{10,2},{11,3},{14,6},{15,7},{16,24},{17,... | collective-permute-start | bytes 14155784 | tf_op jit(solution)/shard_map/ppermute | solution.py:275
  148.6 63.2 %collective-permute-start.25 = (f32[512,1024]{1,0:T(8,128)S(1)}, f32[512,1024]{1,0:T(8,128)S(1)}, u32[]{:S(2)}, u32[]{:S(2)}) collective-permute-start(f32[512,1024]{1,0:T(8,128)S(1)} %copy-done.6), channel_id=1, source_target_pairs={{0,1},{1,0},{2,3},{3,2},{4,5},{5,4},{6,7},{7,6},{8,9},{9,8},{10,11... | collective-permute-start | bytes 6291464 | tf_op jit(solution)/shard_map/ppermute | solution.py:275
  182.5 137.1 %collective-permute-start.18 = (f32[128,640]{1,0:T(8,128)}, f32[128,640]{1,0:T(8,128)S(1)}, u32[]{:S(2)}, u32[]{:S(2)}) collective-permute-start(f32[128,640]{1,0:T(8,128)} %constant_dynamic-slice_fusion.5), channel_id=1, source_target_pairs={{0,2},{1,7},{2,4},{3,1},{4,6},{5,3},{6,0},{7,5},{8,10},{9,15},{10,... | collective-permute-start | bytes 983048 | tf_op jit(solution)/shard_map/ppermute | solution.py:275
  211.8 117.4 %collective-permute-start.16 = (f32[128,640]{1,0:T(8,128)}, f32[128,640]{1,0:T(8,128)}, u32[]{:S(2)}, u32[]{:S(2)}) collective-permute-start(f32[128,640]{1,0:T(8,128)} %constant_dynamic-slice_fusion.6), channel_id=1, source_target_pairs={{0,2},{1,7},{2,4},{3,1},{4,6},{5,3},{6,0},{7,5},{8,10},{9,15},{10,... | collective-permute-start | bytes 983048 | tf_op jit(solution)/shard_map/ppermute | solution.py:275
  218.2 52.2 %collective-permute-start.26 = (f32[512,640]{1,0:T(8,128)}, f32[512,640]{1,0:T(8,128)}, u32[]{:S(2)}, u32[]{:S(2)}) collective-permute-start(f32[512,640]{1,0:T(8,128)} %constant_dynamic-slice_fusion.1), channel_id=1, source_target_pairs={{0,2},{1,7},{2,4},{3,1},{4,6},{5,3},{6,0},{7,5},{8,10},{9,15},{10,... | collective-permute-start | bytes 3932168 | tf_op jit(solution)/shard_map/ppermute | solution.py:275
  247.5 38.3 %collective-permute-start.24 = (f32[256,640]{1,0:T(8,128)}, f32[256,640]{1,0:T(8,128)S(1)}, u32[]{:S(2)}, u32[]{:S(2)}) collective-permute-start(f32[256,640]{1,0:T(8,128)} %constant_dynamic-slice_fusion.2), channel_id=1, source_target_pairs={{0,2},{1,7},{2,4},{3,1},{4,6},{5,3},{6,0},{7,5},{8,10},{9,15},{10,... | collective-permute-start | bytes 1966088 | tf_op jit(solution)/shard_map/ppermute | solution.py:275
  250.2 47.5 %collective-permute-start.22 = (f32[256,640]{1,0:T(8,128)}, f32[256,640]{1,0:T(8,128)S(1)}, u32[]{:S(2)}, u32[]{:S(2)}) collective-permute-start(f32[256,640]{1,0:T(8,128)} %constant_dynamic-slice_fusion.3), channel_id=1, source_target_pairs={{0,2},{1,7},{2,4},{3,1},{4,6},{5,3},{6,0},{7,5},{8,10},{9,15},{10,... | collective-permute-start | bytes 1966088 | tf_op jit(solution)/shard_map/ppermute | solution.py:275
  270.4 38.7 %collective-permute-start.20 = (f32[256,640]{1,0:T(8,128)S(1)}, f32[256,640]{1,0:T(8,128)S(1)}, u32[]{:S(2)}, u32[]{:S(2)}) collective-permute-start(f32[256,640]{1,0:T(8,128)S(1)} %copy-done.14), channel_id=1, source_target_pairs={{0,2},{1,7},{2,4},{3,1},{4,6},{5,3},{6,0},{7,5},{8,10},{9,15},{10,... | collective-permute-start | bytes 1966088 | tf_op jit(solution)/shard_map/ppermute | solution.py:275
  285.8 51.7 %collective-permute-start.14 = (f32[128,640]{1,0:T(8,128)S(1)}, f32[128,640]{1,0:T(8,128)S(1)}, u32[]{:S(2)}, u32[]{:S(2)}) collective-permute-start(f32[128,640]{1,0:T(8,128)S(1)} %copy-done.30), channel_id=1, source_target_pairs={{0,2},{1,7},{2,4},{3,1},{4,6},{5,3},{6,0},{7,5},{8,10},{9,15},{10,... | collective-permute-start | bytes 983048 | tf_op jit(solution)/shard_map/ppermute | solution.py:275
  297.7 48.9 %collective-permute-start.12 = (f32[128,640]{1,0:T(8,128)S(1)}, f32[128,640]{1,0:T(8,128)S(1)}, u32[]{:S(2)}, u32[]{:S(2)}) collective-permute-start(f32[128,640]{1,0:T(8,128)S(1)} %copy-done.29), channel_id=1, source_target_pairs={{0,2},{1,7},{2,4},{3,1},{4,6},{5,3},{6,0},{7,5},{8,10},{9,15},{10,... | collective-permute-start | bytes 983048 | tf_op jit(solution)/shard_map/ppermute | solution.py:275
  309.1 46.5 %collective-permute-start.10 = (f32[128,640]{1,0:T(8,128)S(1)}, f32[128,640]{1,0:T(8,128)S(1)}, u32[]{:S(2)}, u32[]{:S(2)}) collective-permute-start(f32[128,640]{1,0:T(8,128)S(1)} %copy-done.28), channel_id=1, source_target_pairs={{0,2},{1,7},{2,4},{3,1},{4,6},{5,3},{6,0},{7,5},{8,10},{9,15},{10,... | collective-permute-start | bytes 983048 | tf_op jit(solution)/shard_map/ppermute | solution.py:275
  319.6 45.1 %collective-permute-start.1 = (f32[128,640]{1,0:T(8,128)S(1)}, f32[128,640]{1,0:T(8,128)S(1)}, u32[]{:S(2)}, u32[]{:S(2)}) collective-permute-start(f32[128,640]{1,0:T(8,128)S(1)} %copy-done.27), channel_id=1, source_target_pairs={{0,2},{1,7},{2,4},{3,1},{4,6},{5,3},{6,0},{7,5},{8,10},{9,15},{10,... | collective-permute-start | bytes 983048 | tf_op jit(solution)/shard_map/ppermute | solution.py:275
  (40 other events, 807.3 us)

commit v2 on v1

--- a/solution.py
+++ b/solution.py
@@ -116,6 +116,9 @@
 WINDOW = (GROUP + 2 * REACH) * BLOCK
 HALO = REACH * BLOCK
 VMEM = 56 * 1024 * 1024
+SHORT = pl.CostEstimate(flops=1, bytes_accessed=1, transcendentals=0)
+TOKEN = jax.ShapeDtypeStruct((8, 128), jnp.float32)
+TOKEN_SPEC = pl.BlockSpec((8, 128), lambda *_: (0, 0))
 
 
 def halves(value):
@@ -129,19 +132,26 @@
     return dot(a_high, b_high) + (dot(a_high, b_low) + dot(a_low, b_high))
 
 
-def band_kernel(places, gains, blocks, diagonal, high, low, whole, *, with_diagonal):
+def band_kernel(places, gains, choice, *refs, sources, with_diagonal):
+    blocks, diagonal, (high, low, token, whole) = refs[:sources], refs[sources], refs[sources + 1 :]
+    token[...] = jnp.zeros_like(token)
     i = pl.program_id(0)
     whole[...] = jnp.zeros_like(whole)
-    for k in range(blocks.shape[1]):
-        place = pl.multiple_of(places[i, k] * BLOCK, BLOCK)
-        whole[:, pl.ds(place, BLOCK)] = blocks[0, k]
+    for source in range(sources):
+
+        @pl.when(choice[0] == source)
+        def _():
+            for k in range(blocks[source].shape[0]):
+                place = pl.multiple_of(places[i, k] * BLOCK, BLOCK)
+                whole[:, pl.ds(place, BLOCK)] = blocks[source][k]
+
     if with_diagonal:
         own = pl.multiple_of((REACH + i % GROUP) * BLOCK, BLOCK)
         whole[:, pl.ds(own, BLOCK)] += gains[i] * diagonal[0]
     high[...], low[...] = halves(whole[...])
 
 
-def band(blocks, columns, first_block, total_blocks, diagonal, gains):
+def band(sources, choice, offset, columns, first_block, total_blocks, diagonal, gains):
     count, stored = columns.shape
     own_ids = first_block + jnp.arange(count, dtype=jnp.int32)
     relative = (columns - own_ids[:, None] + total_blocks // 2) % total_blocks - total_blocks // 2
@@ -150,32 +160,41 @@
     if not with_diagonal:
         diagonal = jnp.zeros((1, BLOCK, BLOCK), jnp.float32)
     shape = jax.ShapeDtypeStruct((count * BLOCK, WINDOW), jnp.bfloat16)
+
+    def blocks_of(source):
+        def index(i, places, gains, choice):
+            start = choice[1] if source == 0 else 0
+            return (jnp.where(choice[0] == source, start + i, 0), 0, 0)
+
+        return pl.BlockSpec((stored, BLOCK, BLOCK), index)
+
     return pl.pallas_call(
-        functools.partial(band_kernel, with_diagonal=with_diagonal),
-        out_shape=(shape, shape),
+        functools.partial(band_kernel, sources=len(sources), with_diagonal=with_diagonal),
+        out_shape=(shape, shape, TOKEN),
         grid_spec=pltpu.PrefetchScalarGridSpec(
-            num_scalar_prefetch=2,
+            num_scalar_prefetch=3,
             grid=(count,),
             in_specs=[
-                pl.BlockSpec((1, stored, BLOCK, BLOCK), lambda i, *_: (i, 0, 0, 0)),
+                *(blocks_of(source) for source in range(len(sources))),
                 pl.BlockSpec((1, BLOCK, BLOCK), lambda i, *_: (i if with_diagonal else 0, 0, 0)),
             ],
-            out_specs=[pl.BlockSpec((BLOCK, WINDOW), lambda i, *_: (i, 0))] * 2,
+            out_specs=[pl.BlockSpec((BLOCK, WINDOW), lambda i, *_: (i, 0))] * 2 + [TOKEN_SPEC],
             scratch_shapes=[pltpu.VMEM((BLOCK, WINDOW), jnp.float32)],
         ),
         compiler_params=pltpu.CompilerParams(vmem_limit_bytes=VMEM),
-        cost_estimate=pl.CostEstimate(
-            flops=0, bytes_accessed=count * BLOCK * (stored * BLOCK + WINDOW) * 4, transcendentals=0
-        ),
+        cost_estimate=SHORT,
         name="band",
-    )(places, gains, blocks, diagonal)
-
-
-def left_kernel(top, own, bottom, high, low, out, ext_high, ext_low):
+    )(places, gains, jnp.stack([choice, offset]).astype(jnp.int32), *sources, diagonal)
+
+
+def left_kernel(up, inner, own, outer, high, low, out, token, ext_high, ext_low):
+    token[...] = jnp.zeros_like(token)
     rows = own.shape[0]
-    for start, part in ((0, top), (HALO, own), (HALO + rows, bottom)):
+    top = jnp.where(up[0] == 0, outer[...], inner[...])
+    bottom = jnp.where(up[0] == 0, inner[...], outer[...])
+    for start, part in ((0, top), (HALO, own[...]), (HALO + rows, bottom)):
         size = part.shape[0]
-        ext_high[start : start + size], ext_low[start : start + size] = halves(part[...])
+        ext_high[start : start + size], ext_low[start : start + size] = halves(part)
     step = GROUP * BLOCK
     for g in range(rows // step):
         here, window = slice(g * step, (g + 1) * step), slice(g * step, g * step + WINDOW)
@@ -183,31 +202,29 @@
         out[here] = own[here] + step_size * value
 
 
-def left_part(top, covariance, bottom, high, low, slab=256):
+def left_part(up, inner, covariance, outer, high, low, slab=256):
     rows, cols = covariance.shape
-    whole = pl.BlockSpec((rows, WINDOW), lambda j: (0, 0), pipeline_mode=pl.Buffered(1))
+    whole = pl.BlockSpec((rows, WINDOW), lambda j, s: (0, 0), pipeline_mode=pl.Buffered(1))
+    beyond = pl.BlockSpec((HALO, slab), lambda j, s: (0, j))
+    here = pl.BlockSpec((rows, slab), lambda j, s: (0, j))
     return pl.pallas_call(
         left_kernel,
-        out_shape=jax.ShapeDtypeStruct((rows, cols), jnp.float32),
-        grid=(cols // slab,),
-        in_specs=[
-            pl.BlockSpec((HALO, slab), lambda j: (0, j)),
-            pl.BlockSpec((rows, slab), lambda j: (0, j)),
-            pl.BlockSpec((HALO, slab), lambda j: (0, j)),
-            whole,
-            whole,
-        ],
-        out_specs=pl.BlockSpec((rows, slab), lambda j: (0, j)),
-        scratch_shapes=[pltpu.VMEM((rows + 2 * HALO, slab), jnp.bfloat16)] * 2,
+        out_shape=(jax.ShapeDtypeStruct((rows, cols), jnp.float32), TOKEN),
+        grid_spec=pltpu.PrefetchScalarGridSpec(
+            num_scalar_prefetch=1,
+            grid=(cols // slab,),
+            in_specs=[beyond, here, beyond, whole, whole],
+            out_specs=[here, TOKEN_SPEC],
+            scratch_shapes=[pltpu.VMEM((rows + 2 * HALO, slab), jnp.bfloat16)] * 2,
+        ),
         compiler_params=pltpu.CompilerParams(vmem_limit_bytes=VMEM),
-        cost_estimate=pl.CostEstimate(
-            flops=6 * rows * cols * WINDOW, bytes_accessed=12 * rows * cols, transcendentals=0
-        ),
+        cost_estimate=SHORT,
         name="left_part",
-    )(top, covariance, bottom, high, low)
-
-
-def right_kernel(odd, pair, strip, own, row_diagonal, high, low, total, out, ext_high, ext_low):
+    )(up.reshape(1).astype(jnp.int32), inner, covariance, outer, high, low)
+
+
+def right_kernel(odd, pair, strip, own, row_diagonal, high, low, total, out, token, ext_high, ext_low):
+    token[...] = jnp.zeros_like(token)
     rows, cols = own.shape
 
     def put(start, value):
@@ -241,12 +258,12 @@
 def right_part(first, odd, pair, strip, covariance, row_diagonal, high, low, total, rows):
     cols = covariance.shape[1]
     count = pair.shape[0] // rows
-    scalars = jnp.stack([odd, first // rows]).astype(jnp.int32)
+    scalars = jnp.stack([odd, first]).astype(jnp.int32)
     whole = pl.BlockSpec(high.shape, lambda j, s: (0, 0), pipeline_mode=pl.Buffered(1))
-    there = pl.BlockSpec((rows, cols), lambda j, s: (s[1] + j, 0))
+    there = pl.BlockSpec((pl.Element(rows), pl.Element(cols)), lambda j, s: (pl.multiple_of(s[1] + j * rows, BLOCK), 0))
     return pl.pallas_call(
         right_kernel,
-        out_shape=jax.ShapeDtypeStruct(total.shape, jnp.float32),
+        out_shape=(jax.ShapeDtypeStruct(total.shape, jnp.float32), TOKEN),
         grid_spec=pltpu.PrefetchScalarGridSpec(
             num_scalar_prefetch=1,
             grid=(count,),
@@ -254,19 +271,17 @@
                 pl.BlockSpec((rows, cols), lambda j, s: (j, 0)),
                 pl.BlockSpec((rows, HALO), lambda j, s: (j, 0)),
                 there,
-                pl.BlockSpec((rows // BLOCK, BLOCK, BLOCK), lambda j, s: (s[1] + j, 0, 0)),
+                pl.BlockSpec((pl.Element(rows // BLOCK), pl.Element(BLOCK), pl.Element(BLOCK)), lambda j, s: (s[1] // BLOCK + j * (rows // BLOCK), 0, 0)),
                 whole,
                 whole,
                 there,
             ],
-            out_specs=there,
+            out_specs=[there, TOKEN_SPEC],
             scratch_shapes=[pltpu.VMEM((rows, cols + 2 * HALO), jnp.bfloat16)] * 2,
         ),
         input_output_aliases={7: 0},
         compiler_params=pltpu.CompilerParams(vmem_limit_bytes=VMEM),
-        cost_estimate=pl.CostEstimate(
-            flops=6 * rows * count * cols * WINDOW, bytes_accessed=18 * rows * count * cols, transcendentals=0
-        ),
+        cost_estimate=SHORT,
         name="right_part",
     )(scalars, pair, strip, covariance, row_diagonal, high, low, total)
 
@@ -275,102 +290,205 @@
     return lax.ppermute(value, ("row", "col"), [(a * cols + b, c * cols + d) for (a, b), (c, d) in pairs])
 
 
-def spread_over_rows(value, mesh_rows, mesh_cols, ratio):
-    place = lax.axis_index("row") ^ (lax.axis_index("col") // ratio)
-    hop = mesh_rows // 2
-    while hop:
-        pairs = []
-        for r in range(mesh_rows):
-            for c in range(mesh_cols):
-                if (r ^ (c // ratio)) & (2 * hop - 1) == 0:
-                    pairs.append(((r, c), (r ^ hop, c)))
-        value = jnp.where(place & (2 * hop - 1) == hop, send(value, pairs, mesh_cols), value)
-        hop //= 2
-    return value
-
-
-def spread_over_cols(value, mesh_rows, mesh_cols, ratio):
-    place = (lax.axis_index("col") // ratio) ^ lax.axis_index("row")
-    hop = mesh_cols // ratio // 2
-    while hop:
-        pairs = []
-        for r in range(mesh_rows):
-            for c in range(mesh_cols):
-                if ((c // ratio) ^ r) & (2 * hop - 1) == 0:
-                    pairs.append(((r, c), (r, ((c // ratio) ^ hop) * ratio + c % ratio)))
-        value = jnp.where(place & (2 * hop - 1) == hop, send(value, pairs, mesh_cols), value)
-        hop //= 2
-    return value
+def rows_route(hop, devices, ratio):
+    return [((r, c), (r ^ hop, c)) for r, c in devices if (r ^ (c // ratio)) & (2 * hop - 1) == 0]
+
+
+def cols_route(hop, devices, ratio):
+    return [
+        ((r, c), (r, ((c // ratio) ^ hop) * ratio + c % ratio))
+        for r, c in devices
+        if ((c // ratio) ^ r) & (2 * hop - 1) == 0
+    ]
 
 
 def cut(total):
-    sizes = []
-    left = total
-    while left:
-        size = max(BLOCK, (left // 4) // (2 * BLOCK) * 2 * BLOCK)
-        sizes.append(min(size, left))
+    first = total * 5 // 16 // BLOCK * BLOCK
+    sizes = [first, first]
+    left = total - 2 * first
+    while left > BLOCK:
+        sizes.append(-(-left // (2 * BLOCK)) * BLOCK)
         left -= sizes[-1]
-    return sizes
+    return sizes + [left] * (left > 0)
+
+
+def packed_kernel(first, upper, lower, out):
+    across = lax.broadcasted_iota(jnp.int32, (BLOCK, BLOCK), 1)
+    down = lax.broadcasted_iota(jnp.int32, (BLOCK, BLOCK), 0)
+    out[0] = jnp.where(across > down, upper[...], jnp.where(across < down, lower[...], 0.0))
+
+
+def packed_diagonal(covariance, first, count):
+    half = count // 2
+    return pl.pallas_call(
+        packed_kernel,
+        out_shape=jax.ShapeDtypeStruct((half, BLOCK, BLOCK), jnp.float32),
+        grid_spec=pltpu.PrefetchScalarGridSpec(
+            num_scalar_prefetch=1,
+            grid=(half,),
+            in_specs=[
+                pl.BlockSpec((BLOCK, BLOCK), lambda j, s: (s[0] + j, j)),
+                pl.BlockSpec((BLOCK, BLOCK), lambda j, s: (s[0] + half + j, half + j)),
+            ],
+            out_specs=pl.BlockSpec((1, BLOCK, BLOCK), lambda j, s: (j, 0, 0)),
+        ),
+        cost_estimate=SHORT,
+        name="packed_diagonal",
+    )(first.reshape(1).astype(jnp.int32), covariance, covariance)
+
+
+def unpacked(blocks):
+    upper, lower = jnp.triu(blocks), jnp.tril(blocks)
+    return jnp.concatenate([upper - upper.transpose(0, 2, 1), lower - lower.transpose(0, 2, 1)], axis=0)
+
+
+class Order:
+    def __init__(self):
+        self.clock = jnp.zeros(TOKEN.shape, TOKEN.dtype)
+
+    def after(self, value):
+        return lax.optimization_barrier((value, self.clock))[0]
+
+    def passed(self, value):
+        value, self.clock = lax.optimization_barrier((value, self.clock))
+        return value
+
+    def ran(self, results):
+        self.clock = results[-1]
+        return results[:-1]
 
 
 def paired_step(covariance, couplings, block_columns, onsite):
     tile_rows, tile_cols = covariance.shape
     row_blocks, col_blocks = tile_rows // BLOCK, tile_cols // BLOCK
-    total_blocks = block_columns.shape[0]
+    total_blocks, stored = block_columns.shape
     mesh_rows, mesh_cols = lax.axis_size("row"), lax.axis_size("col")
     ratio = tile_rows // tile_cols
     row, col = lax.axis_index("row"), lax.axis_index("col")
-    odd = col % 2
+    odd, up = col % 2, row % 2
     first_row, first_col = row * row_blocks, col * col_blocks
     offset = jnp.clip(first_col - first_row, 0, row_blocks - col_blocks)
     devices = [(r, c) for r in range(mesh_rows) for c in range(mesh_cols)]
-
-    top = shifted(covariance[tile_rows - HALO :], "row", 1)
-    bottom = shifted(covariance[:HALO], "row", -1)
-
-    diagonal = jnp.stack(
-        [
-            lax.dynamic_slice(covariance, ((offset + j) * BLOCK, j * BLOCK), (BLOCK, BLOCK))
-            for j in range(col_blocks)
-        ]
-    )
-    other = send(diagonal, [((r, c), (r, c ^ 1)) for r, c in devices if c // 2 == r], mesh_cols)
+    partners = [((r, c), (r, c ^ 1)) for r, c in devices]
+    next_pairs = [((r, c), (r, (c + (2 if c % 2 == 0 else -2)) % mesh_cols)) for r, c in devices]
+    inner_route = [((r, c), (r ^ 1, c)) for r, c in devices]
+    outer_route = [((r, c), ((r + (-1 if r % 2 == 0 else 1)) % mesh_rows, c)) for r, c in devices]
+    beside = 0
+    sizes = cut(tile_rows - beside)
+    firsts = [sum(sizes[:j]) for j in range(len(sizes))]
+    order = Order()
+    chunks, pairs, strips = {}, {}, {}
+
+    def move(value, route):
+        return send(order.after(value), route, mesh_cols)
+
+    def prepare(*numbers):
+        for j in numbers:
+            if j < len(sizes):
+                chunk = lax.dynamic_slice_in_dim(covariance, beside * odd + firsts[j], sizes[j], 0)
+                chunks[j] = order.passed(chunk)
+
+    def exchange(*numbers):
+        for j in numbers:
+            if j < len(sizes):
+                pairs[j] = move(chunks[j], partners)
+
+    def exchanged(j):
+        pairs[j] = order.passed(pairs[j])
+        strip = lax.dynamic_slice_in_dim(pairs[j], (1 - odd) * (tile_cols - HALO), HALO, 1)
+        strips[j] = move(strip, next_pairs)
+
+    def add_right(total, j):
+        first = beside * (1 - odd) + firsts[j]
+        (total,) = order.ran(
+            right_part(
+                order.after(jnp.int32(first)), odd, pairs[j], strips[j], covariance, row_diagonal,
+                col_high, col_low, total, sizes[j],
+            )
+        )
+        return total
+
+    far = tile_rows - HALO
+    diagonal = packed_diagonal(covariance, offset, col_blocks)
+    other = move(diagonal, [((r, c), (r, c ^ 1)) for r, c in devices if c // 2 == r])
+    prepare(0)
+    exchange(0)
+    outer = move(lax.dynamic_slice_in_dim(covariance, up * far, HALO, 0), outer_route)
+    inner = move(lax.dynamic_slice_in_dim(covariance, (1 - up) * far, HALO, 0), inner_route)
+    row_gains = lax.dynamic_slice_in_dim(onsite, first_row, row_blocks, 0)
+    row_columns = lax.dynamic_slice_in_dim(block_columns, first_row, row_blocks, 0)
+    blocks = couplings.reshape(-1, BLOCK, BLOCK)
+    zero = jnp.int32(0)
+    row_high, row_low = order.ran(
+        band([blocks], zero, zero, row_columns, first_row, total_blocks, None, order.after(row_gains))
+    )
+    count = col_blocks * stored
+    own_blocks = lax.dynamic_slice_in_dim(blocks, offset * stored, count, 0)
+    held = {0: order.passed(jnp.concatenate([own_blocks, diagonal], axis=0))}
+    prepare(1)
+    inner, outer, other = order.passed(inner), order.passed(outer), order.passed(other)
+
+    def hand_on(place):
+        low = place & -place
+        route = [((r, c), (r ^ low, c)) for r, c in devices if r ^ (c // ratio) == place ^ low]
+        held[place] = move(held[place ^ low], route)
+
+    exchanged(0)
+    exchange(1)
+    places = sorted(range(1, mesh_rows), key=lambda place: (bin(place).count("1"), -place))
+    nearest = [place for place in places if place & (place - 1) == 0]
+    for place in nearest:
+        hand_on(place)
     both = jnp.where(odd == 0, jnp.stack([diagonal, other]), jnp.stack([other, diagonal]))
-    row_diagonal = spread_over_cols(both.reshape(row_blocks, BLOCK, BLOCK), mesh_rows, mesh_cols, ratio)
-    row_gains = lax.dynamic_slice_in_dim(onsite, first_row, row_blocks, 0)
-    row_diagonal = row_diagonal * row_gains[:, None, None]
-
-    own_couplings = lax.dynamic_slice_in_dim(couplings, offset, col_blocks, 0)
-    col_couplings = spread_over_rows(own_couplings, mesh_rows, mesh_cols, ratio)
-    col_diagonal = spread_over_rows(diagonal, mesh_rows, mesh_cols, ratio)
-
-    pairs, strips, firsts = [], [], []
-    start = 0
-    for size in cut(tile_rows):
-        chunk = covariance[start : start + size]
-        pair = send(chunk, [((r, c), (r, c ^ 1)) for r, c in devices], mesh_cols)
-        strip = lax.dynamic_slice_in_dim(pair, (1 - odd) * (tile_cols - HALO), HALO, 1)
-        strip = send(
-            strip, [((r, c), (r, (c + (2 if c % 2 == 0 else -2)) % mesh_cols)) for r, c in devices], mesh_cols
-        )
-        pairs.append(pair)
-        strips.append(strip)
-        firsts.append(start)
-        start += size
-
-    row_columns = lax.dynamic_slice_in_dim(block_columns, first_row, row_blocks, 0)
-    row_high, row_low = band(couplings, row_columns, first_row, total_blocks, None, row_gains)
-    total = left_part(top, covariance, bottom, row_high, row_low)
-
+    both = both.reshape(-1, BLOCK, BLOCK)
+    across, hop = (col // ratio) ^ row, mesh_cols // ratio // 2
+    moved = move(both, cols_route(hop, devices, ratio))
+    (total,) = order.ran(left_part(order.after(up), inner, covariance, outer, row_high, row_low))
+    moved = order.passed(moved)
+    both = jnp.where(across & (2 * hop - 1) == hop, moved, both)
+    while hop > 1:
+        hop //= 2
+        moved = move(both, cols_route(hop, devices, ratio))
+        if hop > 1:
+            moved = order.passed(moved)
+            both = jnp.where(across & (2 * hop - 1) == hop, moved, both)
+    prepare(2, 3)
+    strips[0] = order.passed(strips[0])
+    for place in nearest:
+        held[place] = order.passed(held[place])
+    moved = order.passed(moved)
+    both = jnp.where(across & 1 == 1, moved, both)
+    half = both.shape[0] // 2
+    row_diagonal = jnp.concatenate([unpacked(both[:half]), unpacked(both[half:])], axis=0)
+    row_diagonal = order.passed(row_diagonal * row_gains[:, None, None])
+
+    exchanged(1)
+    exchange(2, 3)
+    for place in places[len(nearest) :]:
+        hand_on(place)
+        held[place] = order.passed(held[place])
+    prepare(4, 5)
+    place = row ^ (col // ratio)
+    col_diagonal = held[0][count:]
+    for source in places:
+        col_diagonal = jnp.where(place == source, held[source][count:], col_diagonal)
+    col_diagonal = unpacked(col_diagonal)
     col_columns = lax.dynamic_slice_in_dim(block_columns, first_col, col_blocks, 0)
     col_gains = lax.dynamic_slice_in_dim(onsite, first_col, col_blocks, 0)
-    col_high, col_low = band(col_couplings, col_columns, first_col, total_blocks, col_diagonal, col_gains)
-    for first, pair, strip in zip(firsts, pairs, strips):
-        rows = 2 * BLOCK if pair.shape[0] % (2 * BLOCK) == 0 and first % (2 * BLOCK) == 0 else BLOCK
-        total = right_part(
-            jnp.int32(first), odd, pair, strip, covariance, row_diagonal, col_high, col_low, total, rows
+    col_high, col_low = order.ran(
+        band(
+            [blocks] + [held[source] for source in sorted(places)],
+            place, offset, col_columns, first_col, total_blocks, order.after(col_diagonal), col_gains,
         )
-    return total
+    )
+    total = add_right(total, 0)
+    for j in range(2, len(sizes)):
+        exchanged(j)
+        exchange(j + 2)
+        strips[j - 1] = order.passed(strips[j - 1])
+        total = add_right(total, j - 1)
+    strips[len(sizes) - 1] = order.passed(strips[len(sizes) - 1])
+    return add_right(total, len(sizes) - 1)
 
 
 def power_of_two(number):
@@ -385,6 +503,7 @@
         and tile_cols % (GROUP * BLOCK) == 0
         and tile_rows == 2 * tile_cols
         and mesh_cols == 2 * mesh_rows
+        and mesh_rows > 2
         and power_of_two(mesh_rows)
         and block_columns.shape[0] >= 2 * REACH + 2
     )

time: 378 us -> 251 us (0.66)
  waiting for transfers between devices: 119 us -> 60.4 us
  Pallas kernels: 142 us -> 117 us
  starting transfers between devices: 48.1 us -> 27.1 us
  local copies, waits for them, and re-layouts: 47.5 us -> 31.5 us
  other arithmetic: 16.7 us -> 12.6 us
    ppermute x27 -> x18, waiting for transfers between devices: 119 us -> 60.4 us  [send(): lax.ppermute(value, ('row', 'col'), [(a * cols + b, c * cols + d) for (a,...]
    pallas_call x13 -> x9, Pallas kernels: 142 us -> 117 us  [the longest x5 61.1 us: right_part(): pl.pallas_call(right_kernel, out_shape=(jax.ShapeDtypeStruct(total.shape,...]
    ppermute x27 -> x18, starting transfers between devices: 48.1 us -> 27.1 us  [send(): lax.ppermute(value, ('row', 'col'), [(a * cols + b, c * cols + d) for (a,...]
    slice x4 -> x1, local copies, waits for them, and re-layouts: 16 us -> 0.13 us  [paired_step(): both[half:]]
    unnamed x79 -> x29, local copies, waits for them, and re-layouts: 12.2 us -> 2.84 us
    select_n x5 -> x6, other arithmetic: 8.55 us -> 2.24 us  [the longest x4 2.11 us: unpacked(): upper, lower = (jnp.triu(blocks), jnp.tril(blocks))]
    dynamic_slice x11 -> x10, local copies, waits for them, and re-layouts: 16.5 us -> 22.4 us  [the longest x4 15.2 us: prepare(): lax.dynamic_slice_in_dim(covariance, beside * odd + firsts[j], sizes[j], 0)]
  transfers between devices with their start and end apart: 29 -> 18, of which waited for: 8 -> 7; matrix products, arithmetic and copies ran while one was open for 14% -> 13% of each run, Pallas kernels for 36% -> 44%
where the time goes in v2:
time: 251 us; the launch traced here: 248 us
  Pallas kernels  117 us (47%)
  waiting for transfers between devices  60.4 us (24%)
  local copies, waits for them, and re-layouts  31.5 us (13%)
  starting transfers between devices  27.1 us (11%)
  other arithmetic  12.6 us (5%)
    pallas_call x5, Pallas kernels, right_part(): pl.pallas_call(right_kernel, out_shape=(jax.ShapeDtypeStruct(total.shape,...  61.1 us
    ppermute x18, waiting for transfers between devices, send(): lax.ppermute(value, ('row', 'col'), [(a * cols + b, c * cols + d) for (a,...  60.4 us
    pallas_call x1, Pallas kernels, left_part(): pl.pallas_call(left_kernel, out_shape=(jax.ShapeDtypeStruct((rows, cols),...  28 us
    ppermute x18, starting transfers between devices, send(): lax.ppermute(value, ('row', 'col'), [(a * cols + b, c * cols + d) for (a,...  27.1 us
    pallas_call x2, Pallas kernels, band(): pl.pallas_call(functools.partial(band_kernel, sources=len(sources), with_...  24.5 us
    dynamic_slice x4, local copies, waits for them, and re-layouts, prepare(): lax.dynamic_slice_in_dim(covariance, beside * odd + firsts[j], sizes[j], 0)  15.2 us
  transfers between devices with their start and end apart: 18, of which 7 were waited for; matrix products, arithmetic and copies ran while one was open for 13% of the time, Pallas kernels for 44%

profile of v2, /device:TPU:0, one launch (start us, length us, event | category | flops | bytes accessed | tf_op | source)
XLA Modules:
  0.0 248.5 jit_solution(3143791376272569984)
XLA Ops:
  0.0 9.0 %fusion.6 = (f32[640,1024]{1,0:T(8,128)}, f32[640,1024]{1,0:T(8,128)}, f32[640,1024]{1,0:T(8,128)}, f32[640,1024]{1,0:T(8,128)}) fusion(f32[2048,1024]{1,0:T(8,128)} %own.11, s32[]{:T(128)S(6)} %select_n.142, s32[]{:T(128)S(6)} %select_n.141), kind=kLoop, calls=%fused_computation.54 | loop fusion | bytes 20971528 | tf_op jit(solution)/shard_map/dynamic_slice | solution.py:388
  13.6 3.0 %packed_diagonal.1 = f32[4,128,128]{2,1,0:T(8,128)} custom-call(s32[1]{0:T(128)} %bitcast.2.first, f32[2048,1024]{1,0:T(8,128)} %own.11, f32[2048,1024]{1,0:T(8,128)} %own.11), custom_call_target="tpu_custom_call" | custom-call | flops 1 | bytes 1 | tf_op jit(solution)/shard_map/packed_diagonal/pallas_call | solution.py:323
  19.2 2.9 %constant_dynamic-slice_fusion.7 = f32[72,128,128]{2,1,0:T(8,128)S(1)} fusion(f32[144,128,128]{2,1,0:T(8,128)} %bitcast.26, s32[]{:T(128)S(6)} %select_n.143), kind=kLoop, calls=%fused_computation.40 | loop fusion | bytes 9437188 | tf_op jit(solution)/shard_map/dynamic_slice | solution.py:426
  24.7 15.1 %band.2 = (bf16[2048,1536]{1,0:T(8,128)(2,1)}, bf16[2048,1536]{1,0:T(8,128)(2,1)}, f32[8,128]{1,0:T(8,128)}) custom-call(s32[16,9]{1,0:T(8,128)} %fusion.2.places, f32[16]{0:T(128)} %dynamic_slice.59.gains, s32[2]{0:T(128)} %broadcast_12_choice.2.choice, f32[144,128,128]{2,1,0:T(8,128)} %bitcast.27, f32[1,128,128]{2,1,0:T(8,128)} %broadcast_in_dim.42.refs_1_), custom_call_target="tpu_custom_call" | custom-call | flops 1 | bytes 1 | tf_op jit(solution)/shard_map/band/pallas_call | solution.py:171
  39.7 2.9 %pad_maximum_fusion = f32[76,128,128]{2,1,0:T(8,128)} fusion(f32[4,128,128]{2,1,0:T(8,128)S(1)} %copy-done.5, f32[72,128,128]{2,1,0:T(8,128)S(1)} %constant_dynamic-slice_fusion.7), kind=kLoop, calls=%fused_computation | loop fusion | flops 1245184 | bytes 9961472 | tf_op jit(solution)/shard_map/concatenate | solution.py:427
  42.6 27.0 %collective-permute-done.1.outer = f32[640,1024]{1,0:T(8,128)} collective-permute-done((f32[640,1024]{1,0:T(8,128)}, f32[640,1024]{1,0:T(8,128)}, u32[]{:S(2)}, u32[]{:S(2)}) %collective-permute-start.1) | collective-permute-done | bytes 2621472 | tf_op jit(solution)/shard_map/ppermute | solution.py:290
  69.6 4.2 %collective-permute-done = f32[4,128,128]{2,1,0:T(8,128)S(1)} collective-permute-done((f32[4,128,128]{2,1,0:T(8,128)}, f32[4,128,128]{2,1,0:T(8,128)S(1)}, u32[]{:S(2)}, u32[]{:S(2)}) %collective-permute-start) | collective-permute-done | bytes 262176 | tf_op jit(solution)/shard_map/ppermute | solution.py:290
  73.9 3.5 %collective-permute-start.8 = (f32[76,128,128]{2,1,0:T(8,128)}, f32[76,128,128]{2,1,0:T(8,128)}, u32[]{:S(2)}, u32[]{:S(2)}) collective-permute-start(f32[76,128,128]{2,1,0:T(8,128)} %pad_maximum_fusion), channel_id=1, source_target_pairs={{0,16},{1,17},{10,26},{11,27},{20,4},{21,5},{30,14},{31,15}} | collective-permute-start | bytes 14942216 | tf_op jit(solution)/shard_map/ppermute | solution.py:290
  77.4 3.5 %collective-permute-start.7 = (f32[76,128,128]{2,1,0:T(8,128)}, f32[76,128,128]{2,1,0:T(8,128)}, u32[]{:S(2)}, u32[]{:S(2)}) collective-permute-start(f32[76,128,128]{2,1,0:T(8,128)} %pad_maximum_fusion), channel_id=1, source_target_pairs={{0,8},{1,9},{10,2},{11,3},{20,28},{21,29},{30,22},{31,23}} | collective-permute-start | bytes 14942216 | tf_op jit(solution)/shard_map/ppermute | solution.py:290
  83.4 3.0 %collective-permute-start.4 = (f32[8,128,128]{2,1,0:T(8,128)S(1)}, f32[8,128,128]{2,1,0:T(8,128)}, u32[]{:S(2)}, u32[]{:S(2)}) collective-permute-start(f32[8,128,128]{2,1,0:T(8,128)S(1)} %bitcast.30), channel_id=1, source_target_pairs={{0,4},{1,5},{10,14},{11,15},{20,16},{21,17},{30,26},{31,27}} | collective-permute-start | bytes 1572872 | tf_op jit(solution)/shard_map/ppermute | solution.py:290
  87.0 28.0 %left_part.1 = (f32[2048,1024]{1,0:T(8,128)}, f32[8,128]{1,0:T(8,128)}) custom-call(s32[1]{0:T(128)} %bitcast.7.up, f32[640,1024]{1,0:T(8,128)} %collective-permute-done.2.inner, f32[2048,1024]{1,0:T(8,128)} %own.11, f32[640,1024]{1,0:T(8,128)} %collective-permute-done.1.outer, bf16[2048,1536]{1,0:T(8,128)(2,1)} %get-tuple-element.99.high, ...), custom_call_target="tpu_custom_call" | custom-call | flops 1 | bytes 1 | tf_op jit(solution)/shard_map/left_part/pallas_call | solution.py:210
  115.0 9.4 %collective-permute-done.4 = f32[8,128,128]{2,1,0:T(8,128)} collective-permute-done((f32[8,128,128]{2,1,0:T(8,128)S(1)}, f32[8,128,128]{2,1,0:T(8,128)}, u32[]{:S(2)}, u32[]{:S(2)}) %collective-permute-start.4) | collective-permute-done | bytes 524320 | tf_op jit(solution)/shard_map/ppermute | solution.py:290
  125.8 2.8 %dynamic_slice.52 = f32[384,1024]{1,0:T(8,128)} slice(f32[2048,1024]{1,0:T(8,128)} %own.11), slice={[1280:1664], [0:1024]} | slice | bytes 3145728 | tf_op jit(solution)/shard_map/dynamic_slice | solution.py:388
  134.6 10.4 %collective-permute-done.5.pair = f32[640,1024]{1,0:T(8,128)} collective-permute-done((f32[640,1024]{1,0:T(8,128)}, f32[640,1024]{1,0:T(8,128)}, u32[]{:S(2)}, u32[]{:S(2)}) %collective-permute-start.5) | collective-permute-done | bytes 2621472 | tf_op jit(solution)/shard_map/ppermute | solution.py:290
  145.0 2.9 %collective-permute-start.11 = (f32[76,128,128]{2,1,0:T(8,128)}, f32[76,128,128]{2,1,0:T(8,128)}, u32[]{:S(2)}, u32[]{:S(2)}) collective-permute-start(f32[76,128,128]{2,1,0:T(8,128)} %collective-permute-done.8.refs_2_), channel_id=1, source_target_pairs={{4,12},{5,13},{14,6},{15,7},{16,24},{17,25},{26,18},{27,19}} | collective-permute-start | bytes 14942216 | tf_op jit(solution)/shard_map/ppermute | solution.py:290
  152.0 2.7 %constant_dynamic-slice_fusion.2 = f32[640,640]{1,0:T(8,128)} fusion(f32[640,1024]{1,0:T(8,128)} %collective-permute-done.5.pair, s32[]{:T(128)S(6)} %select_n.153), kind=kLoop, calls=%fused_computation.35 | loop fusion | bytes 3276804 | tf_op jit(solution)/shard_map/dynamic_slice | solution.py:398
  161.8 9.4 %band.3 = (bf16[1024,1536]{1,0:T(8,128)(2,1)}, bf16[1024,1536]{1,0:T(8,128)(2,1)}, f32[8,128]{1,0:T(8,128)}) custom-call(s32[8,9]{1,0:T(8,128)} %fusion.5.places, f32[8]{0:T(128)} %dynamic_slice.63.gains, s32[2]{0:T(128)} %get-tuple-element.167.choice, f32[144,128,128]{2,1,0:T(8,128)} %bitcast.28, f32[76,128,128]{2,1,0:T(8,128)} %collective-permute-done.7.refs_1_, ...), custom_call_target="tpu_custom_call" | custom-call | flops 1 | bytes 1 | tf_op jit(solution)/shard_map/band/pallas_call | solution.py:171
  171.2 16.2 %right_part.5 = (f32[2048,1024]{1,0:T(8,128)}, f32[8,128]{1,0:T(8,128)}) custom-call(s32[2]{0:T(128)} %get-tuple-element.166.odd, f32[640,1024]{1,0:T(8,128)} %copy-done.2, f32[640,640]{1,0:T(8,128)} %collective-permute-done.9.strip, f32[2048,1024]{1,0:T(8,128)} %own.11, ...), custom_call_target="tpu_custom_call", output_to_operand_aliasing={{0}: (7, {})} | custom-call | flops 1 | bytes 1 | tf_op jit(solution)/shard_map/right_part/pallas_call | solution.py:264
  191.0 3.5 %collective-permute-done.15.strip = f32[640,640]{1,0:T(8,128)} collective-permute-done((f32[640,640]{1,0:T(8,128)}, f32[640,640]{1,0:T(8,128)}, u32[]{:S(2)}, u32[]{:S(2)}) %collective-permute-start.15) | collective-permute-done | bytes 1638432 | tf_op jit(solution)/shard_map/ppermute | solution.py:290
  194.5 16.0 %right_part.6 = (f32[2048,1024]{1,0:T(8,128)}, f32[8,128]{1,0:T(8,128)}) custom-call(s32[2]{0:T(128)} %get-tuple-element.169.odd, f32[640,1024]{1,0:T(8,128)} %collective-permute-done.5.pair, f32[640,640]{1,0:T(8,128)} %collective-permute-done.15.strip, f32[2048,1024]{1,0:T(8,128)} %own.11, ...), custom_call_target="tpu_custom_call", output_to_operand_aliasing={{0}: (7, {})} | custom-call | flops 1 | bytes 1 | tf_op jit(solution)/shard_map/right_part/pallas_call | solution.py:264
  210.8 4.6 %collective-permute-done.13.strip = f32[384,640]{1,0:T(8,128)S(1)} collective-permute-done((f32[384,640]{1,0:T(8,128)S(1)}, f32[384,640]{1,0:T(8,128)S(1)}, u32[]{:S(2)}, u32[]{:S(2)}) %collective-permute-start.13) | collective-permute-done | bytes 983072 | tf_op jit(solution)/shard_map/ppermute | solution.py:290
  216.4 11.5 %right_part.7 = (f32[2048,1024]{1,0:T(8,128)}, f32[8,128]{1,0:T(8,128)}) custom-call(s32[2]{0:T(128)} %get-tuple-element.168.odd, f32[384,1024]{1,0:T(8,128)} %copy-done.3, f32[384,640]{1,0:T(8,128)} %copy-done.7, f32[2048,1024]{1,0:T(8,128)} %own.11, f32[16,128,128]{2,1,0:T(8,128)} %maximum_multiply_fusion.row_diagonal, ...), custom_call_target="tpu_custom_call", output_to_operand_aliasing={{0}: (7, {})} | custom-call | flops 1 | bytes 1 | tf_op jit(solution)/shard_map/right_part/pallas_call | solution.py:264
  230.3 9.0 %right_part.8 = (f32[2048,1024]{1,0:T(8,128)}, f32[8,128]{1,0:T(8,128)}) custom-call(s32[2]{0:T(128)} %pad_add_fusion.5.odd, f32[256,1024]{1,0:T(8,128)} %copy-done.4, f32[256,640]{1,0:T(8,128)} %copy-done.8, f32[2048,1024]{1,0:T(8,128)} %own.11, f32[16,128,128]{2,1,0:T(8,128)} %maximum_multiply_fusion.row_diagonal, ...), custom_call_target="tpu_custom_call", output_to_operand_aliasing={{0}: (7, {})} | custom-call | flops 1 | bytes 1 | tf_op jit(solution)/shard_map/right_part/pallas_call | solution.py:264
  240.0 8.4 %right_part.9 = (f32[2048,1024]{1,0:T(8,128)}, f32[8,128]{1,0:T(8,128)}) custom-call(s32[2]{0:T(128)} %pad_add_fusion.odd, f32[128,1024]{1,0:T(8,128)} %copy-done.6, f32[128,640]{1,0:T(8,128)} %copy-done.9, f32[2048,1024]{1,0:T(8,128)} %own.11, f32[16,128,128]{2,1,0:T(8,128)} %maximum_multiply_fusion.row_diagonal, ...), custom_call_target="tpu_custom_call", output_to_operand_aliasing={{0}: (7, {})} | custom-call | flops 1 | bytes 1 | tf_op jit(solution)/shard_map/right_part/pallas_call | solution.py:264
  (101 shorter events, 39.3 us)
Async XLA Ops:
  0.0 19.0 %copy-start = (s32[64,9]{0,1:T(8,128)S(1)}, s32[64,9]{0,1:T(8,128)}, u32[]{:S(2)}) copy-start(s32[64,9]{0,1:T(8,128)} %param.6) | copy-start | bytes 6916
  9.0 33.6 %collective-permute-start.2 = (f32[640,1024]{1,0:T(8,128)}, f32[640,1024]{1,0:T(8,128)}, u32[]{:S(2)}, u32[]{:S(2)}) collective-permute-start(f32[640,1024]{1,0:T(8,128)} %get-tuple-element.84), channel_id=1, source_target_pairs={{0,8},{1,9},{2,10},{3,11},{4,12},{5,13},{6,14},{7,15},{8,0},{9,1},... | collective-permute-start | bytes 7864328 | tf_op jit(solution)/shard_map/ppermute | solution.py:290
  9.5 60.1 %collective-permute-start.1 = (f32[640,1024]{1,0:T(8,128)}, f32[640,1024]{1,0:T(8,128)}, u32[]{:S(2)}, u32[]{:S(2)}) collective-permute-start(f32[640,1024]{1,0:T(8,128)} %get-tuple-element.83), channel_id=1, source_target_pairs={{0,24},{1,25},{2,26},{3,27},{4,28},{5,29},{6,30},{7,31},{8,16},{9,... | collective-permute-start | bytes 7864328 | tf_op jit(solution)/shard_map/ppermute | solution.py:290
  12.1 61.8 %collective-permute-start.3 = (f32[640,1024]{1,0:T(8,128)}, f32[640,1024]{1,0:T(8,128)S(1)}, u32[]{:S(2)}, u32[]{:S(2)}) collective-permute-start(f32[640,1024]{1,0:T(8,128)} %get-tuple-element.92), channel_id=1, source_target_pairs={{0,1},{1,0},{2,3},{3,2},{4,5},{5,4},{6,7},{7,6},{8,9},{9,8},{10,11... | collective-permute-start | bytes 7864328 | tf_op jit(solution)/shard_map/ppermute | solution.py:290
  16.6 57.2 %collective-permute-start = (f32[4,128,128]{2,1,0:T(8,128)}, f32[4,128,128]{2,1,0:T(8,128)S(1)}, u32[]{:S(2)}, u32[]{:S(2)}) collective-permute-start(f32[4,128,128]{2,1,0:T(8,128)} %packed_diagonal.1), channel_id=1, source_target_pairs={{0,1},{1,0},{10,11},{11,10},{20,21},{21,20},{30,31},{31,30}} | collective-permute-start | bytes 786440 | tf_op jit(solution)/shard_map/ppermute | solution.py:290
  24.7 15.1 %copy-start.5 = (f32[4,128,128]{2,1,0:T(8,128)S(1)}, f32[4,128,128]{2,1,0:T(8,128)}, u32[]{:S(2)}) copy-start(f32[4,128,128]{2,1,0:T(8,128)} %packed_diagonal.1) | copy-start | bytes 786436
  73.9 41.1 %copy-start.2 = (f32[640,1024]{1,0:T(8,128)}, f32[640,1024]{1,0:T(8,128)S(1)}, u32[]{:S(2)}) copy-start(f32[640,1024]{1,0:T(8,128)S(1)} %collective-permute-done.3.pair) | copy-start | bytes 7864324
  73.9 57.2 %collective-permute-start.8 = (f32[76,128,128]{2,1,0:T(8,128)}, f32[76,128,128]{2,1,0:T(8,128)}, u32[]{:S(2)}, u32[]{:S(2)}) collective-permute-start(f32[76,128,128]{2,1,0:T(8,128)} %pad_maximum_fusion), channel_id=1, source_target_pairs={{0,16},{1,17},{10,26},{11,27},{20,4},{21,5},{30,14},{31,15}} | collective-permute-start | bytes 14942216 | tf_op jit(solution)/shard_map/ppermute | solution.py:290
  77.4 53.7 %collective-permute-start.7 = (f32[76,128,128]{2,1,0:T(8,128)}, f32[76,128,128]{2,1,0:T(8,128)}, u32[]{:S(2)}, u32[]{:S(2)}) collective-permute-start(f32[76,128,128]{2,1,0:T(8,128)} %pad_maximum_fusion), channel_id=1, source_target_pairs={{0,8},{1,9},{10,2},{11,3},{20,28},{21,29},{30,22},{31,23}} | collective-permute-start | bytes 14942216 | tf_op jit(solution)/shard_map/ppermute | solution.py:290
  82.3 48.8 %collective-permute-start.9 = (f32[640,640]{1,0:T(8,128)}, f32[640,640]{1,0:T(8,128)}, u32[]{:S(2)}, u32[]{:S(2)}) collective-permute-start(f32[640,640]{1,0:T(8,128)} %constant_dynamic-slice_fusion.5), channel_id=1, source_target_pairs={{0,2},{1,7},{2,4},{3,1},{4,6},{5,3},{6,0},{7,5},{8,10},{9,15},{10,... | collective-permute-start | bytes 4915208 | tf_op jit(solution)/shard_map/ppermute | solution.py:290
  83.4 41.0 %collective-permute-start.4 = (f32[8,128,128]{2,1,0:T(8,128)S(1)}, f32[8,128,128]{2,1,0:T(8,128)}, u32[]{:S(2)}, u32[]{:S(2)}) collective-permute-start(f32[8,128,128]{2,1,0:T(8,128)S(1)} %bitcast.30), channel_id=1, source_target_pairs={{0,4},{1,5},{10,14},{11,15},{20,16},{21,17},{30,26},{31,27}} | collective-permute-start | bytes 1572872 | tf_op jit(solution)/shard_map/ppermute | solution.py:290
  86.3 58.7 %collective-permute-start.5 = (f32[640,1024]{1,0:T(8,128)}, f32[640,1024]{1,0:T(8,128)}, u32[]{:S(2)}, u32[]{:S(2)}) collective-permute-start(f32[640,1024]{1,0:T(8,128)} %get-tuple-element.105), channel_id=1, source_target_pairs={{0,1},{1,0},{2,3},{3,2},{4,5},{5,4},{6,7},{7,6},{8,9},{9,8},{10,11... | collective-permute-start | bytes 7864328 | tf_op jit(solution)/shard_map/ppermute | solution.py:290
  124.4 8.0 %collective-permute-start.6 = (f32[8,128,128]{2,1,0:T(8,128)S(1)}, f32[8,128,128]{2,1,0:T(8,128)S(1)}, u32[]{:S(2)}, u32[]{:S(2)}) collective-permute-start(f32[8,128,128]{2,1,0:T(8,128)S(1)} %broadcast_select_fusion), channel_id=1, source_target_pairs={{0,2},{1,3},{4,6},{5,7},{10,8},{11,9},{14,12},{15,13},{16,18},{17,... | collective-permute-start | bytes 1572872 | tf_op jit(solution)/shard_map/ppermute | solution.py:290
  145.0 10.6 %collective-permute-start.11 = (f32[76,128,128]{2,1,0:T(8,128)}, f32[76,128,128]{2,1,0:T(8,128)}, u32[]{:S(2)}, u32[]{:S(2)}) collective-permute-start(f32[76,128,128]{2,1,0:T(8,128)} %collective-permute-done.8.refs_2_), channel_id=1, source_target_pairs={{4,12},{5,13},{14,6},{15,7},{16,24},{17,25},{26,18},{27,19}} | collective-permute-start | bytes 14942216 | tf_op jit(solution)/shard_map/ppermute | solution.py:290
  148.7 38.7 %collective-permute-start.10 = (f32[384,1024]{1,0:T(8,128)}, f32[384,1024]{1,0:T(8,128)S(1)}, u32[]{:S(2)}, u32[]{:S(2)}) collective-permute-start(f32[384,1024]{1,0:T(8,128)} %dynamic_slice.52), channel_id=1, source_target_pairs={{0,1},{1,0},{2,3},{3,2},{4,5},{5,4},{6,7},{7,6},{8,9},{9,8},{10,11... | collective-permute-start | bytes 4718600 | tf_op jit(solution)/shard_map/ppermute | solution.py:290
  150.3 60.2 %collective-permute-start.14 = (f32[256,1024]{1,0:T(8,128)}, f32[256,1024]{1,0:T(8,128)S(1)}, u32[]{:S(2)}, u32[]{:S(2)}) collective-permute-start(f32[256,1024]{1,0:T(8,128)} %dynamic_slice.61), channel_id=1, source_target_pairs={{0,1},{1,0},{2,3},{3,2},{4,5},{5,4},{6,7},{7,6},{8,9},{9,8},{10,11... | collective-permute-start | bytes 3145736 | tf_op jit(solution)/shard_map/ppermute | solution.py:290
  154.7 39.7 %collective-permute-start.15 = (f32[640,640]{1,0:T(8,128)}, f32[640,640]{1,0:T(8,128)}, u32[]{:S(2)}, u32[]{:S(2)}) collective-permute-start(f32[640,640]{1,0:T(8,128)} %constant_dynamic-slice_fusion.2), channel_id=1, source_target_pairs={{0,2},{1,7},{2,4},{3,1},{4,6},{5,3},{6,0},{7,5},{8,10},{9,15},{10,... | collective-permute-start | bytes 4915208 | tf_op jit(solution)/shard_map/ppermute | solution.py:290
  187.4 23.1 %copy-start.3 = (f32[384,1024]{1,0:T(8,128)}, f32[384,1024]{1,0:T(8,128)S(1)}, u32[]{:S(2)}) copy-start(f32[384,1024]{1,0:T(8,128)S(1)} %collective-permute-done.10.pair) | copy-start | bytes 4718596
  187.5 28.0 %collective-permute-start.13 = (f32[384,640]{1,0:T(8,128)S(1)}, f32[384,640]{1,0:T(8,128)S(1)}, u32[]{:S(2)}, u32[]{:S(2)}) collective-permute-start(f32[384,640]{1,0:T(8,128)S(1)} %constant_dynamic-slice_fusion.3), channel_id=1, source_target_pairs={{0,2},{1,7},{2,4},{3,1},{4,6},{5,3},{6,0},{7,5},{8,10},{9,15},{10,... | collective-permute-start | bytes 2949128 | tf_op jit(solution)/shard_map/ppermute | solution.py:290
  189.3 38.6 %collective-permute-start.12 = (f32[128,1024]{1,0:T(8,128)S(1)}, f32[128,1024]{1,0:T(8,128)S(1)}, u32[]{:S(2)}, u32[]{:S(2)}) collective-permute-start(f32[128,1024]{1,0:T(8,128)S(1)} %dynamic_slice.51), channel_id=1, source_target_pairs={{0,1},{1,0},{2,3},{3,2},{4,5},{5,4},{6,7},{7,6},{8,9},{9,8},{10,11... | collective-permute-start | bytes 1572872 | tf_op jit(solution)/shard_map/ppermute | solution.py:290
  210.5 17.4 %copy-start.4 = (f32[256,1024]{1,0:T(8,128)}, f32[256,1024]{1,0:T(8,128)S(1)}, u32[]{:S(2)}) copy-start(f32[256,1024]{1,0:T(8,128)S(1)} %collective-permute-done.14.pair) | copy-start | bytes 3145732
  210.6 18.9 %collective-permute-start.17 = (f32[256,640]{1,0:T(8,128)S(1)}, f32[256,640]{1,0:T(8,128)S(1)}, u32[]{:S(2)}, u32[]{:S(2)}) collective-permute-start(f32[256,640]{1,0:T(8,128)S(1)} %constant_dynamic-slice_fusion), channel_id=1, source_target_pairs={{0,2},{1,7},{2,4},{3,1},{4,6},{5,3},{6,0},{7,5},{8,10},{9,15},{10,... | collective-permute-start | bytes 1966088 | tf_op jit(solution)/shard_map/ppermute | solution.py:290
  227.9 11.4 %copy-start.6 = (f32[128,1024]{1,0:T(8,128)}, f32[128,1024]{1,0:T(8,128)S(1)}, u32[]{:S(2)}) copy-start(f32[128,1024]{1,0:T(8,128)S(1)} %collective-permute-done.12.pair) | copy-start | bytes 1572868
  228.0 11.4 %collective-permute-start.16 = (f32[128,640]{1,0:T(8,128)S(1)}, f32[128,640]{1,0:T(8,128)S(1)}, u32[]{:S(2)}, u32[]{:S(2)}) collective-permute-start(f32[128,640]{1,0:T(8,128)S(1)} %constant_dynamic-slice_fusion.1), channel_id=1, source_target_pairs={{0,2},{1,7},{2,4},{3,1},{4,6},{5,3},{6,0},{7,5},{8,10},{9,15},{10,... | collective-permute-start | bytes 983048 | tf_op jit(solution)/shard_map/ppermute | solution.py:290
  (7 other events, 25.3 us)

commit v3 on v2

--- a/solution.py
+++ b/solution.py
@@ -117,8 +117,7 @@
 HALO = REACH * BLOCK
 VMEM = 56 * 1024 * 1024
 SHORT = pl.CostEstimate(flops=1, bytes_accessed=1, transcendentals=0)
-TOKEN = jax.ShapeDtypeStruct((8, 128), jnp.float32)
-TOKEN_SPEC = pl.BlockSpec((8, 128), lambda *_: (0, 0))
+LONG = pl.CostEstimate(flops=4 * 10**11, bytes_accessed=16 * 10**8, transcendentals=0)
 
 
 def halves(value):
@@ -132,63 +131,107 @@
     return dot(a_high, b_high) + (dot(a_high, b_low) + dot(a_low, b_high))
 
 
-def band_kernel(places, gains, choice, *refs, sources, with_diagonal):
-    blocks, diagonal, (high, low, token, whole) = refs[:sources], refs[sources], refs[sources + 1 :]
-    token[...] = jnp.zeros_like(token)
+def band_kernel(places, gains, scalars, *refs, sources, half):
+    blocks, diagonals, (high, low, whole) = refs[:sources], refs[sources:-3], refs[-3:]
     i = pl.program_id(0)
     whole[...] = jnp.zeros_like(whole)
+    down = lax.broadcasted_iota(jnp.int32, (BLOCK, BLOCK), 0)
+    across = lax.broadcasted_iota(jnp.int32, (BLOCK, BLOCK), 1)
+    beyond = jnp.where(i % (2 * half) < half, across - down, down - across)
+    own = pl.multiple_of((REACH + i % GROUP) * BLOCK, BLOCK)
     for source in range(sources):
 
-        @pl.when(choice[0] == source)
+        @pl.when(scalars[0] == source)
         def _():
             for k in range(blocks[source].shape[0]):
                 place = pl.multiple_of(places[i, k] * BLOCK, BLOCK)
                 whole[:, pl.ds(place, BLOCK)] = blocks[source][k]
-
-    if with_diagonal:
-        own = pl.multiple_of((REACH + i % GROUP) * BLOCK, BLOCK)
-        whole[:, pl.ds(own, BLOCK)] += gains[i] * diagonal[0]
+            if diagonals:
+                part = jnp.where(beyond > 0, diagonals[source][0], 0.0)
+                whole[:, pl.ds(own, BLOCK)] += gains[i] * (part - part.T)
+
     high[...], low[...] = halves(whole[...])
 
 
-def band(sources, choice, offset, columns, first_block, total_blocks, diagonal, gains):
+def band(sources, choice, offset, diagonals, diagonal_offset, half, columns, first_block, total_blocks, gains):
     count, stored = columns.shape
     own_ids = first_block + jnp.arange(count, dtype=jnp.int32)
     relative = (columns - own_ids[:, None] + total_blocks // 2) % total_blocks - total_blocks // 2
     places = relative + REACH + (jnp.arange(count, dtype=jnp.int32) % GROUP)[:, None]
-    with_diagonal = diagonal is not None
-    if not with_diagonal:
-        diagonal = jnp.zeros((1, BLOCK, BLOCK), jnp.float32)
     shape = jax.ShapeDtypeStruct((count * BLOCK, WINDOW), jnp.bfloat16)
 
     def blocks_of(source):
-        def index(i, places, gains, choice):
-            start = choice[1] if source == 0 else 0
-            return (jnp.where(choice[0] == source, start + i, 0), 0, 0)
+        def index(i, places, gains, scalars):
+            return (jnp.where(scalars[0] == source, scalars[1] + i, 0), 0, 0)
 
         return pl.BlockSpec((stored, BLOCK, BLOCK), index)
 
-    return pl.pallas_call(
-        functools.partial(band_kernel, sources=len(sources), with_diagonal=with_diagonal),
-        out_shape=(shape, shape, TOKEN),
+    def diagonal_of(source):
+        def index(i, places, gains, scalars):
+            return (jnp.where(scalars[0] == source, scalars[2] + i // (2 * half) * half + i % half, 0), 0, 0)
+
+        return pl.BlockSpec((1, BLOCK, BLOCK), index)
+
+    return pl.pallas_call(
+        functools.partial(band_kernel, sources=len(sources), half=half),
+        out_shape=(shape, shape),
         grid_spec=pltpu.PrefetchScalarGridSpec(
             num_scalar_prefetch=3,
             grid=(count,),
-            in_specs=[
-                *(blocks_of(source) for source in range(len(sources))),
-                pl.BlockSpec((1, BLOCK, BLOCK), lambda i, *_: (i if with_diagonal else 0, 0, 0)),
-            ],
-            out_specs=[pl.BlockSpec((BLOCK, WINDOW), lambda i, *_: (i, 0))] * 2 + [TOKEN_SPEC],
+            in_specs=[blocks_of(j) for j in range(len(sources))] + [diagonal_of(j) for j in range(len(diagonals))],
+            out_specs=[pl.BlockSpec((BLOCK, WINDOW), lambda i, *_: (i, 0))] * 2,
             scratch_shapes=[pltpu.VMEM((BLOCK, WINDOW), jnp.float32)],
         ),
         compiler_params=pltpu.CompilerParams(vmem_limit_bytes=VMEM),
         cost_estimate=SHORT,
         name="band",
-    )(places, gains, jnp.stack([choice, offset]).astype(jnp.int32), *sources, diagonal)
-
-
-def left_kernel(up, inner, own, outer, high, low, out, token, ext_high, ext_low):
-    token[...] = jnp.zeros_like(token)
+    )(places, gains, jnp.stack([choice, offset, diagonal_offset]).astype(jnp.int32), *sources, *diagonals)
+
+
+def onsite_kernel(gains, *refs, half):
+    diagonals, (high, low, new_high, new_low) = refs[:GROUP], refs[GROUP:]
+    g = pl.program_id(0)
+    down = lax.broadcasted_iota(jnp.int32, (BLOCK, BLOCK), 0)
+    across = lax.broadcasted_iota(jnp.int32, (BLOCK, BLOCK), 1)
+    new_high[...], new_low[...] = high[...], low[...]
+    for b, diagonal in enumerate(diagonals):
+        i = g * GROUP + b
+        here = slice(b * BLOCK, (b + 1) * BLOCK)
+        beyond = jnp.where(i % (2 * half) < half, across - down, down - across)
+        part = jnp.where(beyond > 0, diagonal[0], 0.0)
+        value = high[here, here].astype(jnp.float32) + low[here, here].astype(jnp.float32)
+        new_high[here, here], new_low[here, here] = halves(value + gains[i] * (part - part.T))
+
+
+def add_onsite(high, low, diagonals, half, gains):
+    step = GROUP * BLOCK
+    own = pl.BlockSpec((pl.Element(step), pl.Element(step)), lambda g, gains: (g * step, HALO))
+    shape = jax.ShapeDtypeStruct(high.shape, high.dtype)
+
+    def diagonal_of(b):
+        def index(g, gains):
+            i = g * GROUP + b
+            return (i // (2 * half) * half + i % half, 0, 0)
+
+        return pl.BlockSpec((1, BLOCK, BLOCK), index)
+
+    return pl.pallas_call(
+        functools.partial(onsite_kernel, half=half),
+        out_shape=(shape, shape),
+        grid_spec=pltpu.PrefetchScalarGridSpec(
+            num_scalar_prefetch=1,
+            grid=(high.shape[0] // step,),
+            in_specs=[diagonal_of(b) for b in range(GROUP)] + [own, own],
+            out_specs=[own, own],
+        ),
+        input_output_aliases={1 + GROUP: 0, 2 + GROUP: 1},
+        compiler_params=pltpu.CompilerParams(vmem_limit_bytes=VMEM),
+        cost_estimate=SHORT,
+        name="add_onsite",
+    )(gains, *([diagonals] * GROUP), high, low)
+
+
+def left_kernel(up, inner, own, outer, high, low, out, ext_high, ext_low):
     rows = own.shape[0]
     top = jnp.where(up[0] == 0, outer[...], inner[...])
     bottom = jnp.where(up[0] == 0, inner[...], outer[...])
@@ -202,19 +245,19 @@
         out[here] = own[here] + step_size * value
 
 
-def left_part(up, inner, covariance, outer, high, low, slab=256):
+def left_part(up, inner, covariance, outer, high, low, slab=2 * BLOCK):
     rows, cols = covariance.shape
     whole = pl.BlockSpec((rows, WINDOW), lambda j, s: (0, 0), pipeline_mode=pl.Buffered(1))
     beyond = pl.BlockSpec((HALO, slab), lambda j, s: (0, j))
     here = pl.BlockSpec((rows, slab), lambda j, s: (0, j))
     return pl.pallas_call(
         left_kernel,
-        out_shape=(jax.ShapeDtypeStruct((rows, cols), jnp.float32), TOKEN),
+        out_shape=jax.ShapeDtypeStruct((rows, cols), jnp.float32),
         grid_spec=pltpu.PrefetchScalarGridSpec(
             num_scalar_prefetch=1,
             grid=(cols // slab,),
             in_specs=[beyond, here, beyond, whole, whole],
-            out_specs=[here, TOKEN_SPEC],
+            out_specs=here,
             scratch_shapes=[pltpu.VMEM((rows + 2 * HALO, slab), jnp.bfloat16)] * 2,
         ),
         compiler_params=pltpu.CompilerParams(vmem_limit_bytes=VMEM),
@@ -223,8 +266,7 @@
     )(up.reshape(1).astype(jnp.int32), inner, covariance, outer, high, low)
 
 
-def right_kernel(odd, pair, strip, own, row_diagonal, high, low, total, out, token, ext_high, ext_low):
-    token[...] = jnp.zeros_like(token)
+def right_kernel(odd, pair, strip, own, high, low, total, out, ext_high, ext_low):
     rows, cols = own.shape
 
     def put(start, value):
@@ -248,14 +290,9 @@
         here, window = slice(g * step, (g + 1) * step), slice(g * step, g * step + WINDOW)
         value = product(ext_high[:, window], ext_low[:, window], high[here], low[here], 1)
         out[:, here] = total[:, here] + step_size * value
-    for b in range(rows // BLOCK):
-        here, mine = slice(b * BLOCK, (b + 1) * BLOCK), slice(HALO, HALO + cols)
-        onsite_high, onsite_low = halves(row_diagonal[b])
-        value = product(onsite_high, onsite_low, ext_high[here, mine], ext_low[here, mine])
-        out[here] += step_size * value
-
-
-def right_part(first, odd, pair, strip, covariance, row_diagonal, high, low, total, rows):
+
+
+def right_part(first, odd, pair, strip, covariance, high, low, total, rows):
     cols = covariance.shape[1]
     count = pair.shape[0] // rows
     scalars = jnp.stack([odd, first]).astype(jnp.int32)
@@ -263,7 +300,7 @@
     there = pl.BlockSpec((pl.Element(rows), pl.Element(cols)), lambda j, s: (pl.multiple_of(s[1] + j * rows, BLOCK), 0))
     return pl.pallas_call(
         right_kernel,
-        out_shape=(jax.ShapeDtypeStruct(total.shape, jnp.float32), TOKEN),
+        out_shape=jax.ShapeDtypeStruct(total.shape, jnp.float32),
         grid_spec=pltpu.PrefetchScalarGridSpec(
             num_scalar_prefetch=1,
             grid=(count,),
@@ -271,27 +308,22 @@
                 pl.BlockSpec((rows, cols), lambda j, s: (j, 0)),
                 pl.BlockSpec((rows, HALO), lambda j, s: (j, 0)),
                 there,
-                pl.BlockSpec((pl.Element(rows // BLOCK), pl.Element(BLOCK), pl.Element(BLOCK)), lambda j, s: (s[1] // BLOCK + j * (rows // BLOCK), 0, 0)),
                 whole,
                 whole,
                 there,
             ],
-            out_specs=[there, TOKEN_SPEC],
+            out_specs=there,
             scratch_shapes=[pltpu.VMEM((rows, cols + 2 * HALO), jnp.bfloat16)] * 2,
         ),
-        input_output_aliases={7: 0},
+        input_output_aliases={6: 0},
         compiler_params=pltpu.CompilerParams(vmem_limit_bytes=VMEM),
         cost_estimate=SHORT,
         name="right_part",
-    )(scalars, pair, strip, covariance, row_diagonal, high, low, total)
+    )(scalars, pair, strip, covariance, high, low, total)
 
 
 def send(value, pairs, cols):
     return lax.ppermute(value, ("row", "col"), [(a * cols + b, c * cols + d) for (a, b), (c, d) in pairs])
-
-
-def rows_route(hop, devices, ratio):
-    return [((r, c), (r ^ hop, c)) for r, c in devices if (r ^ (c // ratio)) & (2 * hop - 1) == 0]
 
 
 def cols_route(hop, devices, ratio):
@@ -310,6 +342,27 @@
         sizes.append(-(-left // (2 * BLOCK)) * BLOCK)
         left -= sizes[-1]
     return sizes + [left] * (left > 0)
+
+
+def rows_kernel(first, rows, out):
+    out[...] = rows[...]
+
+
+def rows_of(covariance, first, size):
+    cols = covariance.shape[1]
+    step = size // 2 if size % (16 * BLOCK // 8) == 0 else size
+    return pl.pallas_call(
+        rows_kernel,
+        out_shape=jax.ShapeDtypeStruct((size, cols), covariance.dtype),
+        grid_spec=pltpu.PrefetchScalarGridSpec(
+            num_scalar_prefetch=1,
+            grid=(size // step,),
+            in_specs=[pl.BlockSpec((pl.Element(step), pl.Element(cols)), lambda j, s: (pl.multiple_of(s[0] + j * step, 8), 0))],
+            out_specs=pl.BlockSpec((step, cols), lambda j, s: (j, 0)),
+        ),
+        cost_estimate=SHORT,
+        name="rows_of",
+    )(jnp.asarray(first, jnp.int32).reshape(1), covariance)
 
 
 def packed_kernel(first, upper, lower, out):
@@ -337,25 +390,22 @@
     )(first.reshape(1).astype(jnp.int32), covariance, covariance)
 
 
-def unpacked(blocks):
-    upper, lower = jnp.triu(blocks), jnp.tril(blocks)
-    return jnp.concatenate([upper - upper.transpose(0, 2, 1), lower - lower.transpose(0, 2, 1)], axis=0)
-
-
-class Order:
-    def __init__(self):
-        self.clock = jnp.zeros(TOKEN.shape, TOKEN.dtype)
-
-    def after(self, value):
-        return lax.optimization_barrier((value, self.clock))[0]
-
-    def passed(self, value):
-        value, self.clock = lax.optimization_barrier((value, self.clock))
-        return value
-
-    def ran(self, results):
-        self.clock = results[-1]
-        return results[:-1]
+def gate_kernel(*refs):
+    pass
+
+
+def gate(*arrays, cost=SHORT):
+    shapes = tuple(jax.ShapeDtypeStruct(array.shape, array.dtype) for array in arrays)
+    anywhere = [pl.BlockSpec(memory_space=pl.ANY)] * len(arrays)
+    return pl.pallas_call(
+        gate_kernel,
+        out_shape=shapes,
+        in_specs=anywhere,
+        out_specs=tuple(anywhere),
+        input_output_aliases={j: j for j in range(len(arrays))},
+        cost_estimate=cost,
+        name="gate",
+    )(*arrays)
 
 
 def paired_step(covariance, couplings, block_columns, onsite):
@@ -376,118 +426,92 @@
     beside = 0
     sizes = cut(tile_rows - beside)
     firsts = [sum(sizes[:j]) for j in range(len(sizes))]
-    order = Order()
-    chunks, pairs, strips = {}, {}, {}
+    chunks = {j: rows_of(covariance, firsts[j], sizes[j]) for j in range(len(sizes))}
+    pairs, strips = {}, {}
 
     def move(value, route):
-        return send(order.after(value), route, mesh_cols)
-
-    def prepare(*numbers):
-        for j in numbers:
-            if j < len(sizes):
-                chunk = lax.dynamic_slice_in_dim(covariance, beside * odd + firsts[j], sizes[j], 0)
-                chunks[j] = order.passed(chunk)
+        return send(value, route, mesh_cols)
 
     def exchange(*numbers):
         for j in numbers:
             if j < len(sizes):
                 pairs[j] = move(chunks[j], partners)
 
-    def exchanged(j):
-        pairs[j] = order.passed(pairs[j])
+    def hand_strip_on(j):
         strip = lax.dynamic_slice_in_dim(pairs[j], (1 - odd) * (tile_cols - HALO), HALO, 1)
         strips[j] = move(strip, next_pairs)
 
     def add_right(total, j):
-        first = beside * (1 - odd) + firsts[j]
-        (total,) = order.ran(
-            right_part(
-                order.after(jnp.int32(first)), odd, pairs[j], strips[j], covariance, row_diagonal,
-                col_high, col_low, total, sizes[j],
-            )
-        )
-        return total
-
-    far = tile_rows - HALO
+        first = jnp.int32(firsts[j])
+        return right_part(first, odd, pairs[j], strips[j], covariance, col_high, col_low, total, sizes[j])
+
     diagonal = packed_diagonal(covariance, offset, col_blocks)
     other = move(diagonal, [((r, c), (r, c ^ 1)) for r, c in devices if c // 2 == r])
-    prepare(0)
+    far = tile_rows - HALO
+    outer = move(rows_of(covariance, up * far, HALO), outer_route)
+    other, chunks[0] = gate(other, chunks[0])
     exchange(0)
-    outer = move(lax.dynamic_slice_in_dim(covariance, up * far, HALO, 0), outer_route)
-    inner = move(lax.dynamic_slice_in_dim(covariance, (1 - up) * far, HALO, 0), inner_route)
+    inner = move(rows_of(covariance, (1 - up) * far, HALO), inner_route)
+    both = jnp.where(odd == 0, jnp.stack([diagonal, other]), jnp.stack([other, diagonal]))
+    both = both.reshape(-1, BLOCK, BLOCK)
+    across, hop = (col // ratio) ^ row, mesh_cols // ratio // 2
+    while hop:
+        (moved,) = gate(move(both, cols_route(hop, devices, ratio)))
+        both = jnp.where(across & (2 * hop - 1) == hop, moved, both)
+        hop //= 2
+    zero = jnp.int32(0)
+    half = col_blocks // 2
+    blocks = couplings.reshape(-1, BLOCK, BLOCK)
+    columns = lax.dynamic_slice_in_dim(block_columns, first_row, row_blocks, 0)
     row_gains = lax.dynamic_slice_in_dim(onsite, first_row, row_blocks, 0)
-    row_columns = lax.dynamic_slice_in_dim(block_columns, first_row, row_blocks, 0)
-    blocks = couplings.reshape(-1, BLOCK, BLOCK)
-    zero = jnp.int32(0)
-    row_high, row_low = order.ran(
-        band([blocks], zero, zero, row_columns, first_row, total_blocks, None, order.after(row_gains))
-    )
+    row_high, row_low = band([blocks], zero, zero, [], zero, half, columns, first_row, total_blocks, row_gains)
+    row_high, row_low = add_onsite(row_high, row_low, both, half, row_gains)
     count = col_blocks * stored
     own_blocks = lax.dynamic_slice_in_dim(blocks, offset * stored, count, 0)
-    held = {0: order.passed(jnp.concatenate([own_blocks, diagonal], axis=0))}
-    prepare(1)
-    inner, outer, other = order.passed(inner), order.passed(outer), order.passed(other)
+    held = {0: jnp.concatenate([own_blocks, diagonal], axis=0)}
 
     def hand_on(place):
         low = place & -place
         route = [((r, c), (r ^ low, c)) for r, c in devices if r ^ (c // ratio) == place ^ low]
         held[place] = move(held[place ^ low], route)
 
-    exchanged(0)
-    exchange(1)
     places = sorted(range(1, mesh_rows), key=lambda place: (bin(place).count("1"), -place))
     nearest = [place for place in places if place & (place - 1) == 0]
+
+    pairs[0], outer = gate(pairs[0], outer, cost=LONG)
+    pairs[0], chunks[1], outer, inner, row_high, held[0] = gate(
+        pairs[0], chunks[1], outer, inner, row_high, held[0]
+    )
+    exchange(1)
     for place in nearest:
         hand_on(place)
-    both = jnp.where(odd == 0, jnp.stack([diagonal, other]), jnp.stack([other, diagonal]))
-    both = both.reshape(-1, BLOCK, BLOCK)
-    across, hop = (col // ratio) ^ row, mesh_cols // ratio // 2
-    moved = move(both, cols_route(hop, devices, ratio))
-    (total,) = order.ran(left_part(order.after(up), inner, covariance, outer, row_high, row_low))
-    moved = order.passed(moved)
-    both = jnp.where(across & (2 * hop - 1) == hop, moved, both)
-    while hop > 1:
-        hop //= 2
-        moved = move(both, cols_route(hop, devices, ratio))
-        if hop > 1:
-            moved = order.passed(moved)
-            both = jnp.where(across & (2 * hop - 1) == hop, moved, both)
-    prepare(2, 3)
-    strips[0] = order.passed(strips[0])
-    for place in nearest:
-        held[place] = order.passed(held[place])
-    moved = order.passed(moved)
-    both = jnp.where(across & 1 == 1, moved, both)
-    half = both.shape[0] // 2
-    row_diagonal = jnp.concatenate([unpacked(both[:half]), unpacked(both[half:])], axis=0)
-    row_diagonal = order.passed(row_diagonal * row_gains[:, None, None])
-
-    exchanged(1)
-    exchange(2, 3)
+    hand_strip_on(0)
+    total = left_part(up, inner, covariance, outer, row_high, row_low)
+
+    (pairs[1],) = gate(pairs[1], cost=LONG)
+    pairs[1], strips[0], total, chunks[2], chunks[3], *got = gate(
+        pairs[1], strips[0], total, chunks[2], chunks[3], *(held[place] for place in nearest)
+    )
+    held.update(zip(nearest, got))
     for place in places[len(nearest) :]:
         hand_on(place)
-        held[place] = order.passed(held[place])
-    prepare(4, 5)
-    place = row ^ (col // ratio)
-    col_diagonal = held[0][count:]
-    for source in places:
-        col_diagonal = jnp.where(place == source, held[source][count:], col_diagonal)
-    col_diagonal = unpacked(col_diagonal)
-    col_columns = lax.dynamic_slice_in_dim(block_columns, first_col, col_blocks, 0)
-    col_gains = lax.dynamic_slice_in_dim(onsite, first_col, col_blocks, 0)
-    col_high, col_low = order.ran(
-        band(
-            [blocks] + [held[source] for source in sorted(places)],
-            place, offset, col_columns, first_col, total_blocks, order.after(col_diagonal), col_gains,
-        )
+    exchange(2, 3)
+    hand_strip_on(1)
+    sources = [held[place] for place in range(mesh_rows)]
+    columns = lax.dynamic_slice_in_dim(block_columns, first_col, col_blocks, 0)
+    gains = lax.dynamic_slice_in_dim(onsite, first_col, col_blocks, 0)
+    col_high, col_low = band(
+        sources, row ^ (col // ratio), zero, sources, jnp.int32(count), half, columns, first_col, total_blocks, gains
     )
     total = add_right(total, 0)
     for j in range(2, len(sizes)):
-        exchanged(j)
+        if j + 2 < len(sizes):
+            pairs[j], total, chunks[j + 2] = gate(pairs[j], total, chunks[j + 2])
+        else:
+            pairs[j], total = gate(pairs[j], total)
+        hand_strip_on(j)
         exchange(j + 2)
-        strips[j - 1] = order.passed(strips[j - 1])
         total = add_right(total, j - 1)
-    strips[len(sizes) - 1] = order.passed(strips[len(sizes) - 1])
     return add_right(total, len(sizes) - 1)
 
 

time: 251 us -> 241 us (0.960)
  waiting for transfers between devices: 60.4 us -> 34 us
  Pallas kernels: 117 us -> 140 us
  local copies, waits for them, and re-layouts: 31.5 us -> 24.8 us
  starting transfers between devices: 27.1 us -> 29.7 us
    ppermute x18, waiting for transfers between devices: 60.4 us -> 34 us  [send(): lax.ppermute(value, ('row', 'col'), [(a * cols + b, c * cols + d) for (a,...]
    pallas_call x8 -> x26, Pallas kernels: 114 us -> 137 us  [the longest x5 57.1 us: right_part(): pl.pallas_call(right_kernel, out_shape=jax.ShapeDtypeStruct(total.shape,...]
    dynamic_slice x12 -> x8, local copies, waits for them, and re-layouts: 20.2 us -> 10.5 us  [the longest x5 9.77 us: hand_strip_on(): lax.dynamic_slice_in_dim(pairs[j], (1 - odd) * (tile_cols - HALO), HALO, 1)]
    unnamed x29 -> x30, local copies, waits for them, and re-layouts: 2.84 us -> 10.3 us
    select_n x1 -> x2, other arithmetic: 0.08 us -> 2.82 us  [paired_step(): both = jnp.where(across & 2 * hop - 1 == hop, moved, both)]
    ppermute x18, starting transfers between devices: 27.1 us -> 29.7 us  [send(): lax.ppermute(value, ('row', 'col'), [(a * cols + b, c * cols + d) for (a,...]
    select_n x7 -> x0, local copies, waits for them, and re-layouts: 2.57 us -> none  [the longest x6 2.44 us: unpacked(): upper, lower = (jnp.triu(blocks), jnp.tril(blocks))]
  transfers between devices with their start and end apart: 18 -> 18, of which waited for: 7 -> 8; matrix products, arithmetic and copies ran while one was open for 13% -> 11% of each run, Pallas kernels for 44% -> 54%
where the time goes in v3:
time: 241 us; the launch traced here: 239 us
  Pallas kernels  140 us (58%)
  waiting for transfers between devices  34 us (14%)
  starting transfers between devices  29.7 us (12%)
  local copies, waits for them, and re-layouts  24.8 us (10%)
  other arithmetic  11.1 us (5%)
    pallas_call x5, Pallas kernels, right_part(): pl.pallas_call(right_kernel, out_shape=jax.ShapeDtypeStruct(total.shape,...  57.1 us
    ppermute x18, waiting for transfers between devices, send(): lax.ppermute(value, ('row', 'col'), [(a * cols + b, c * cols + d) for (a,...  34 us
    ppermute x18, starting transfers between devices, send(): lax.ppermute(value, ('row', 'col'), [(a * cols + b, c * cols + d) for (a,...  29.7 us
    pallas_call x1, Pallas kernels, left_part(): pl.pallas_call(left_kernel, out_shape=jax.ShapeDtypeStruct((rows, cols),...  28 us
    pallas_call x2, Pallas kernels, band(): pl.pallas_call(functools.partial(band_kernel, sources=len(sources), half=...  24.3 us
    pallas_call x7, Pallas kernels, rows_of(): pl.pallas_call(rows_kernel, out_shape=jax.ShapeDtypeStruct((size, cols),...  20.2 us
    unnamed x30, local copies, waits for them, and re-layouts  10.3 us
    dynamic_slice x5, local copies, waits for them, and re-layouts, hand_strip_on(): lax.dynamic_slice_in_dim(pairs[j], (1 - odd) * (tile_cols - HALO), HALO, 1)  9.77 us
  transfers between devices with their start and end apart: 18, of which 8 were waited for; matrix products, arithmetic and copies ran while one was open for 11% of the time, Pallas kernels for 54%

profile of v3, /device:TPU:0, one launch (start us, length us, event | category | flops | bytes accessed | tf_op | source)
XLA Modules:
  0.0 239.4 jit_solution(11452554129914483961)
XLA Ops:
  0.0 3.0 %packed_diagonal.1 = f32[4,128,128]{2,1,0:T(8,128)} custom-call(s32[1]{0:T(128)} %bitcast.1.first, f32[2048,1024]{1,0:T(8,128)} %own.11, f32[2048,1024]{1,0:T(8,128)} %own.11), custom_call_target="tpu_custom_call" | custom-call | flops 1 | bytes 1 | tf_op jit(solution)/shard_map/packed_diagonal/pallas_call | solution.py:376
  3.0 4.9 %collective-permute-start = (f32[4,128,128]{2,1,0:T(8,128)}, f32[4,128,128]{2,1,0:T(8,128)S(1)}, u32[]{:S(2)}, u32[]{:S(2)}) collective-permute-start(f32[4,128,128]{2,1,0:T(8,128)} %packed_diagonal.1), channel_id=1, source_target_pairs={{0,1},{1,0},{10,11},{11,10},{20,21},{21,20},{30,31},{31,30}} | collective-permute-start | bytes 786440 | tf_op jit(solution)/shard_map/ppermute | solution.py:326
  7.9 3.4 %rows_of.8 = f32[640,1024]{1,0:T(8,128)} custom-call(s32[1]{0:T(128)} %bitcast.2.first, f32[2048,1024]{1,0:T(8,128)} %own.11), custom_call_target="tpu_custom_call" | custom-call | flops 1 | bytes 1 | tf_op jit(solution)/shard_map/rows_of/pallas_call | solution.py:354
  11.3 3.4 %rows_of.7.refs_1_ = f32[640,1024]{1,0:T(8,128)} custom-call(s32[1]{0:T(128)} %constant.103.clone.1.first, f32[2048,1024]{1,0:T(8,128)} %own.11), custom_call_target="tpu_custom_call" | custom-call | flops 1 | bytes 1 | tf_op jit(solution)/shard_map/rows_of/pallas_call | solution.py:354
  16.5 4.9 %collective-permute-start.4 = (f32[8,128,128]{2,1,0:T(8,128)S(1)}, f32[8,128,128]{2,1,0:T(8,128)}, u32[]{:S(2)}, u32[]{:S(2)}) collective-permute-start(f32[8,128,128]{2,1,0:T(8,128)S(1)} %bitcast.14), channel_id=1, source_target_pairs={{0,4},{1,5},{10,14},{11,15},{20,16},{21,17},{30,26},{31,27}} | collective-permute-start | bytes 1572872 | tf_op jit(solution)/shard_map/ppermute | solution.py:326
  21.5 3.4 %rows_of.10 = f32[640,1024]{1,0:T(8,128)} custom-call(s32[1]{0:T(128)} %bitcast.3.first, f32[2048,1024]{1,0:T(8,128)} %own.11), custom_call_target="tpu_custom_call" | custom-call | flops 1 | bytes 1 | tf_op jit(solution)/shard_map/rows_of/pallas_call | solution.py:354
  30.3 3.4 %rows_of.9.refs_1_ = f32[640,1024]{1,0:T(8,128)} custom-call(s32[1]{0:T(128)} %constant.105.clone.1.first, f32[2048,1024]{1,0:T(8,128)} %own.11), custom_call_target="tpu_custom_call" | custom-call | flops 1 | bytes 1 | tf_op jit(solution)/shard_map/rows_of/pallas_call | solution.py:354
  34.8 14.9 %band.2 = (bf16[2048,1536]{1,0:T(8,128)(2,1)}, bf16[2048,1536]{1,0:T(8,128)(2,1)}) custom-call(s32[16,9]{1,0:T(8,128)} %fusion.2.places, f32[16]{0:T(128)} %dynamic_slice.30.gains, s32[3]{0:T(128)} %broadcast_12_scalars.2.scalars, f32[144,128,128]{2,1,0:T(8,128)} %bitcast.11), custom_call_target="tpu_custom_call" | custom-call | flops 1 | bytes 1 | tf_op jit(solution)/shard_map/band/pallas_call | solution.py:175
  49.7 2.9 %constant_dynamic-slice_fusion.6 = f32[72,128,128]{2,1,0:T(8,128)S(1)} fusion(f32[144,128,128]{2,1,0:T(8,128)} %bitcast.12, s32[]{:T(128)S(6)} %select_n.105), kind=kLoop, calls=%fused_computation.22 | loop fusion | bytes 9437188 | tf_op jit(solution)/shard_map/dynamic_slice | solution.py:470
  58.1 7.1 %add_onsite.1 = (bf16[2048,1536]{1,0:T(8,128)(2,1)}, bf16[2048,1536]{1,0:T(8,128)(2,1)}) custom-call(f32[16]{0:T(128)} %dynamic_slice.30.gains, f32[8,128,128]{2,1,0:T(8,128)} %broadcast_select_fusion.1.refs_0_.refs_1_, f32[8,128,128]{2,1,0:T(8,128)} %broadcast_select_fusion.1.refs_0_.refs_1_, ...), custom_call_target="tpu_custom_call", output_to_operand_aliasing={{0}: (3, {}), {1}: (4, {})} | custom-call | flops 1 | bytes 1 | tf_op jit(solution)/shard_map/add_onsite/pallas_call | solution.py:218
  68.1 5.2 %collective-permute-done.1.refs_0_ = f32[640,1024]{1,0:T(8,128)S(1)} collective-permute-done((f32[640,1024]{1,0:T(8,128)}, f32[640,1024]{1,0:T(8,128)S(1)}, u32[]{:S(2)}, u32[]{:S(2)}) %collective-permute-start.1) | collective-permute-done | bytes 2621472 | tf_op jit(solution)/shard_map/ppermute | solution.py:326
  81.0 4.8 %collective-permute-start.8 = (f32[76,128,128]{2,1,0:T(8,128)}, f32[76,128,128]{2,1,0:T(8,128)}, u32[]{:S(2)}, u32[]{:S(2)}) collective-permute-start(f32[76,128,128]{2,1,0:T(8,128)} %get-tuple-element.48.refs_0_.refs_4_), channel_id=1, source_target_pairs={{0,16},{1,17},{10,26},{11,27},{20,4},{21,5},{30,14},{31,15}} | collective-permute-start | bytes 14942216 | tf_op jit(solution)/shard_map/ppermute | solution.py:326
  85.8 3.6 %collective-permute-start.9 = (f32[76,128,128]{2,1,0:T(8,128)}, f32[76,128,128]{2,1,0:T(8,128)}, u32[]{:S(2)}, u32[]{:S(2)}) collective-permute-start(f32[76,128,128]{2,1,0:T(8,128)} %get-tuple-element.48.refs_0_.refs_4_), channel_id=1, source_target_pairs={{0,8},{1,9},{10,2},{11,3},{20,28},{21,29},{30,22},{31,23}} | collective-permute-start | bytes 14942216 | tf_op jit(solution)/shard_map/ppermute | solution.py:326
  92.1 28.0 %left_part.1.refs_2_ = f32[2048,1024]{1,0:T(8,128)} custom-call(s32[1]{0:T(128)} %bitcast.8.up, f32[640,1024]{1,0:T(8,128)} %get-tuple-element.44.inner, f32[2048,1024]{1,0:T(8,128)} %own.11, f32[640,1024]{1,0:T(8,128)} %get-tuple-element.45.outer, bf16[2048,1536]{1,0:T(8,128)(2,1)} %get-tuple-element.46.high, bf16[2048,1536]{1,0:T(8,128)(2,1)} %get-tuple-element.47.low), custom_call_target="tpu_custom_call" | custom-call | flops 1 | bytes 1 | tf_op jit(solution)/shard_map/left_part/pallas_call | solution.py:253
  120.1 13.0 %collective-permute-done.6.refs_0_ = f32[640,1024]{1,0:T(8,128)S(1)} collective-permute-done((f32[640,1024]{1,0:T(8,128)}, f32[640,1024]{1,0:T(8,128)S(1)}, u32[]{:S(2)}, u32[]{:S(2)}) %collective-permute-start.6) | collective-permute-done | bytes 2621472 | tf_op jit(solution)/shard_map/ppermute | solution.py:326
  134.6 3.6 %collective-permute-done.8.refs_5_ = f32[76,128,128]{2,1,0:T(8,128)} collective-permute-done((f32[76,128,128]{2,1,0:T(8,128)}, f32[76,128,128]{2,1,0:T(8,128)}, u32[]{:S(2)}, u32[]{:S(2)}) %collective-permute-start.8) | collective-permute-done | bytes 4980768 | tf_op jit(solution)/shard_map/ppermute | solution.py:326
  138.3 2.9 %collective-permute-start.11 = (f32[76,128,128]{2,1,0:T(8,128)}, f32[76,128,128]{2,1,0:T(8,128)}, u32[]{:S(2)}, u32[]{:S(2)}) collective-permute-start(f32[76,128,128]{2,1,0:T(8,128)} %get-tuple-element.52.refs_2_.refs_6_), channel_id=1, source_target_pairs={{4,12},{5,13},{14,6},{15,7},{16,24},{17,25},{26,18},{27,19}} | collective-permute-start | bytes 14942216 | tf_op jit(solution)/shard_map/ppermute | solution.py:326
  150.6 9.4 %band.3 = (bf16[1024,1536]{1,0:T(8,128)(2,1)}, bf16[1024,1536]{1,0:T(8,128)(2,1)}) custom-call(s32[8,9]{1,0:T(8,128)} %fusion.5.places, f32[8]{0:T(128)} %dynamic_slice.35.gains, s32[3]{0:T(128)} %pad_add_fusion.2.scalars, f32[76,128,128]{2,1,0:T(8,128)} %get-tuple-element.48.refs_0_.refs_4_, f32[76,128,128]{2,1,0:T(8,128)} %get-tuple-element.51.refs_1_.refs_5_, ...), custom_call_target="tpu_custom_call" | custom-call | flops 1 | bytes 1 | tf_op jit(solution)/shard_map/band/pallas_call | solution.py:175
  160.0 15.0 %right_part.5.refs_1_ = f32[2048,1024]{1,0:T(8,128)} custom-call(s32[2]{0:T(128)} %pad_add_fusion.1.odd, f32[640,1024]{1,0:T(8,128)} %get-tuple-element.43.pair, f32[640,640]{1,0:T(8,128)} %get-tuple-element.50.strip, f32[2048,1024]{1,0:T(8,128)} %own.11, bf16[1024,1536]{1,0:T(8,128)(2,1)} %get-tuple-element.53.high, ...), custom_call_target="tpu_custom_call", output_to_operand_aliasing={{}: (6, {})} | custom-call | flops 1 | bytes 1 | tf_op jit(solution)/shard_map/right_part/pallas_call | solution.py:301
  175.0 3.7 %collective-permute-done.10.refs_0_ = f32[384,1024]{1,0:T(8,128)S(1)} collective-permute-done((f32[384,1024]{1,0:T(8,128)}, f32[384,1024]{1,0:T(8,128)S(1)}, u32[]{:S(2)}, u32[]{:S(2)}) %collective-permute-start.10) | collective-permute-done | bytes 1572896 | tf_op jit(solution)/shard_map/ppermute | solution.py:326
  184.3 14.9 %right_part.6.refs_1_ = f32[2048,1024]{1,0:T(8,128)} custom-call(s32[2]{0:T(128)} %pad_add_fusion.4.odd, f32[640,1024]{1,0:T(8,128)} %get-tuple-element.59.pair, f32[640,640]{1,0:T(8,128)} %collective-permute-done.15.strip, f32[2048,1024]{1,0:T(8,128)} %own.11, bf16[1024,1536]{1,0:T(8,128)(2,1)} %get-tuple-element.53.high, ...), custom_call_target="tpu_custom_call", output_to_operand_aliasing={{}: (6, {})} | custom-call | flops 1 | bytes 1 | tf_op jit(solution)/shard_map/right_part/pallas_call | solution.py:301
  207.5 10.6 %right_part.7.refs_1_ = f32[2048,1024]{1,0:T(8,128)} custom-call(s32[2]{0:T(128)} %pad_add_fusion.3.odd, f32[384,1024]{1,0:T(8,128)} %get-tuple-element.57.pair, f32[384,640]{1,0:T(8,128)} %copy-done.9, f32[2048,1024]{1,0:T(8,128)} %own.11, bf16[1024,1536]{1,0:T(8,128)(2,1)} %get-tuple-element.53.high, ...), custom_call_target="tpu_custom_call", output_to_operand_aliasing={{}: (6, {})} | custom-call | flops 1 | bytes 1 | tf_op jit(solution)/shard_map/right_part/pallas_call | solution.py:301
  222.1 8.5 %right_part.8.total = f32[2048,1024]{1,0:T(8,128)} custom-call(s32[2]{0:T(128)} %get-tuple-element.66.odd, f32[256,1024]{1,0:T(8,128)} %get-tuple-element.63.pair, f32[256,640]{1,0:T(8,128)} %copy-done.10, f32[2048,1024]{1,0:T(8,128)} %own.11, bf16[1024,1536]{1,0:T(8,128)(2,1)} %get-tuple-element.53.high, ...), custom_call_target="tpu_custom_call", output_to_operand_aliasing={{}: (6, {})} | custom-call | flops 1 | bytes 1 | tf_op jit(solution)/shard_map/right_part/pallas_call | solution.py:301
  231.4 8.1 %right_part.9 = f32[2048,1024]{1,0:T(8,128)} custom-call(s32[2]{0:T(128)} %get-tuple-element.65.odd, f32[128,1024]{1,0:T(8,128)} %get-tuple-element.62.pair, f32[128,640]{1,0:T(8,128)} %copy-done.11, f32[2048,1024]{1,0:T(8,128)} %own.11, bf16[1024,1536]{1,0:T(8,128)(2,1)} %get-tuple-element.53.high, ...), custom_call_target="tpu_custom_call", output_to_operand_aliasing={{}: (6, {})} | custom-call | flops 1 | bytes 1 | tf_op jit(solution)/shard_map/right_part/pallas_call | solution.py:301
  (93 shorter events, 56.7 us)
Async XLA Ops:
  0.0 24.9 %copy-start = (s32[64,9]{0,1:T(8,128)S(1)}, s32[64,9]{0,1:T(8,128)}, u32[]{:S(2)}) copy-start(s32[64,9]{0,1:T(8,128)} %param.6) | copy-start | bytes 6916
  3.0 11.7 %collective-permute-start = (f32[4,128,128]{2,1,0:T(8,128)}, f32[4,128,128]{2,1,0:T(8,128)S(1)}, u32[]{:S(2)}, u32[]{:S(2)}) collective-permute-start(f32[4,128,128]{2,1,0:T(8,128)} %packed_diagonal.1), channel_id=1, source_target_pairs={{0,1},{1,0},{10,11},{11,10},{20,21},{21,20},{30,31},{31,30}} | collective-permute-start | bytes 786440 | tf_op jit(solution)/shard_map/ppermute | solution.py:326
  11.3 4.2 %copy-start.6 = (f32[4,128,128]{2,1,0:T(8,128)S(1)}, f32[4,128,128]{2,1,0:T(8,128)}, u32[]{:S(2)}) copy-start(f32[4,128,128]{2,1,0:T(8,128)} %packed_diagonal.1) | copy-start | bytes 786436
  11.3 56.8 %collective-permute-start.2 = (f32[640,1024]{1,0:T(8,128)}, f32[640,1024]{1,0:T(8,128)}, u32[]{:S(2)}, u32[]{:S(2)}) collective-permute-start(f32[640,1024]{1,0:T(8,128)} %rows_of.8), channel_id=1, source_target_pairs={{0,24},{1,25},{2,26},{3,27},{4,28},{5,29},{6,30},{7,31},{8,16},{9,... | collective-permute-start | bytes 7864328 | tf_op jit(solution)/shard_map/ppermute | solution.py:326
  15.4 57.8 %collective-permute-start.1 = (f32[640,1024]{1,0:T(8,128)}, f32[640,1024]{1,0:T(8,128)S(1)}, u32[]{:S(2)}, u32[]{:S(2)}) collective-permute-start(f32[640,1024]{1,0:T(8,128)} %get-tuple-element.35), channel_id=1, source_target_pairs={{0,1},{1,0},{2,3},{3,2},{4,5},{5,4},{6,7},{7,6},{8,9},{9,8},{10,11... | collective-permute-start | bytes 7864328 | tf_op jit(solution)/shard_map/ppermute | solution.py:326
  16.5 10.9 %collective-permute-start.4 = (f32[8,128,128]{2,1,0:T(8,128)S(1)}, f32[8,128,128]{2,1,0:T(8,128)}, u32[]{:S(2)}, u32[]{:S(2)}) collective-permute-start(f32[8,128,128]{2,1,0:T(8,128)S(1)} %bitcast.14), channel_id=1, source_target_pairs={{0,4},{1,5},{10,14},{11,15},{20,16},{21,17},{30,26},{31,27}} | collective-permute-start | bytes 1572872 | tf_op jit(solution)/shard_map/ppermute | solution.py:326
  24.9 49.8 %collective-permute-start.3 = (f32[640,1024]{1,0:T(8,128)}, f32[640,1024]{1,0:T(8,128)}, u32[]{:S(2)}, u32[]{:S(2)}) collective-permute-start(f32[640,1024]{1,0:T(8,128)} %rows_of.10), channel_id=1, source_target_pairs={{0,8},{1,9},{2,10},{3,11},{4,12},{5,13},{6,14},{7,15},{8,0},{9,1},... | collective-permute-start | bytes 7864328 | tf_op jit(solution)/shard_map/ppermute | solution.py:326
  28.3 27.1 %collective-permute-start.5 = (f32[8,128,128]{2,1,0:T(8,128)}, f32[8,128,128]{2,1,0:T(8,128)S(1)}, u32[]{:S(2)}, u32[]{:S(2)}) collective-permute-start(f32[8,128,128]{2,1,0:T(8,128)} %broadcast_select_fusion), channel_id=1, source_target_pairs={{0,2},{1,3},{4,6},{5,7},{10,8},{11,9},{14,12},{15,13},{16,18},{17,... | collective-permute-start | bytes 1572872 | tf_op jit(solution)/shard_map/ppermute | solution.py:326
  30.3 3.4 %copy-start.12 = (f32[64]{0:T(128)S(1)}, f32[64]{0:T(128)}, u32[]{:S(2)}) copy-start(f32[64]{0:T(128)} %param.7) | copy-start | bytes 772
  73.2 1.5 copy-start.2
  74.8 58.3 %collective-permute-start.6 = (f32[640,1024]{1,0:T(8,128)}, f32[640,1024]{1,0:T(8,128)S(1)}, u32[]{:S(2)}, u32[]{:S(2)}) collective-permute-start(f32[640,1024]{1,0:T(8,128)} %get-tuple-element.42), channel_id=1, source_target_pairs={{0,1},{1,0},{2,3},{3,2},{4,5},{5,4},{6,7},{7,6},{8,9},{9,8},{10,11... | collective-permute-start | bytes 7864328 | tf_op jit(solution)/shard_map/ppermute | solution.py:326
  81.0 57.3 %collective-permute-start.8 = (f32[76,128,128]{2,1,0:T(8,128)}, f32[76,128,128]{2,1,0:T(8,128)}, u32[]{:S(2)}, u32[]{:S(2)}) collective-permute-start(f32[76,128,128]{2,1,0:T(8,128)} %get-tuple-element.48.refs_0_.refs_4_), channel_id=1, source_target_pairs={{0,16},{1,17},{10,26},{11,27},{20,4},{21,5},{30,14},{31,15}} | collective-permute-start | bytes 14942216 | tf_op jit(solution)/shard_map/ppermute | solution.py:326
  85.8 52.5 %collective-permute-start.9 = (f32[76,128,128]{2,1,0:T(8,128)}, f32[76,128,128]{2,1,0:T(8,128)}, u32[]{:S(2)}, u32[]{:S(2)}) collective-permute-start(f32[76,128,128]{2,1,0:T(8,128)} %get-tuple-element.48.refs_0_.refs_4_), channel_id=1, source_target_pairs={{0,8},{1,9},{10,2},{11,3},{20,28},{21,29},{30,22},{31,23}} | collective-permute-start | bytes 14942216 | tf_op jit(solution)/shard_map/ppermute | solution.py:326
  92.1 42.6 %collective-permute-start.7 = (f32[640,640]{1,0:T(8,128)}, f32[640,640]{1,0:T(8,128)}, u32[]{:S(2)}, u32[]{:S(2)}) collective-permute-start(f32[640,640]{1,0:T(8,128)} %constant_dynamic-slice_fusion.5), channel_id=1, source_target_pairs={{0,2},{1,7},{2,4},{3,1},{4,6},{5,3},{6,0},{7,5},{8,10},{9,15},{10,... | collective-permute-start | bytes 4915208 | tf_op jit(solution)/shard_map/ppermute | solution.py:326
  133.0 1.6 copy-start.1
  138.3 12.3 %collective-permute-start.11 = (f32[76,128,128]{2,1,0:T(8,128)}, f32[76,128,128]{2,1,0:T(8,128)}, u32[]{:S(2)}, u32[]{:S(2)}) collective-permute-start(f32[76,128,128]{2,1,0:T(8,128)} %get-tuple-element.52.refs_2_.refs_6_), channel_id=1, source_target_pairs={{4,12},{5,13},{14,6},{15,7},{16,24},{17,25},{26,18},{27,19}} | collective-permute-start | bytes 14942216 | tf_op jit(solution)/shard_map/ppermute | solution.py:326
  141.2 37.5 %collective-permute-start.10 = (f32[384,1024]{1,0:T(8,128)}, f32[384,1024]{1,0:T(8,128)S(1)}, u32[]{:S(2)}, u32[]{:S(2)}) collective-permute-start(f32[384,1024]{1,0:T(8,128)} %get-tuple-element.49), channel_id=1, source_target_pairs={{0,1},{1,0},{2,3},{3,2},{4,5},{5,4},{6,7},{7,6},{8,9},{9,8},{10,11... | collective-permute-start | bytes 4718600 | tf_op jit(solution)/shard_map/ppermute | solution.py:326
  144.4 39.9 %collective-permute-start.15 = (f32[640,640]{1,0:T(8,128)}, f32[640,640]{1,0:T(8,128)}, u32[]{:S(2)}, u32[]{:S(2)}) collective-permute-start(f32[640,640]{1,0:T(8,128)} %constant_dynamic-slice_fusion.2), channel_id=1, source_target_pairs={{0,2},{1,7},{2,4},{3,1},{4,6},{5,3},{6,0},{7,5},{8,10},{9,15},{10,... | collective-permute-start | bytes 4915208 | tf_op jit(solution)/shard_map/ppermute | solution.py:326
  145.2 55.6 %collective-permute-start.14 = (f32[256,1024]{1,0:T(8,128)}, f32[256,1024]{1,0:T(8,128)S(1)}, u32[]{:S(2)}, u32[]{:S(2)}) collective-permute-start(f32[256,1024]{1,0:T(8,128)} %get-tuple-element.58), channel_id=1, source_target_pairs={{0,1},{1,0},{2,3},{3,2},{4,5},{5,4},{6,7},{7,6},{8,9},{9,8},{10,11... | collective-permute-start | bytes 3145736 | tf_op jit(solution)/shard_map/ppermute | solution.py:326
  147.3 1.9 copy-start.13
  182.1 24.4 %collective-permute-start.13 = (f32[384,640]{1,0:T(8,128)}, f32[384,640]{1,0:T(8,128)S(1)}, u32[]{:S(2)}, u32[]{:S(2)}) collective-permute-start(f32[384,640]{1,0:T(8,128)} %constant_dynamic-slice_fusion.3), channel_id=1, source_target_pairs={{0,2},{1,7},{2,4},{3,1},{4,6},{5,3},{6,0},{7,5},{8,10},{9,15},{10,... | collective-permute-start | bytes 2949128 | tf_op jit(solution)/shard_map/ppermute | solution.py:326
  182.1 36.0 %collective-permute-start.12 = (f32[128,1024]{1,0:T(8,128)}, f32[128,1024]{1,0:T(8,128)S(1)}, u32[]{:S(2)}, u32[]{:S(2)}) collective-permute-start(f32[128,1024]{1,0:T(8,128)} %get-tuple-element.56), channel_id=1, source_target_pairs={{0,1},{1,0},{2,3},{3,2},{4,5},{5,4},{6,7},{7,6},{8,9},{9,8},{10,11... | collective-permute-start | bytes 1572872 | tf_op jit(solution)/shard_map/ppermute | solution.py:326
  202.9 18.4 %collective-permute-start.17 = (f32[256,640]{1,0:T(8,128)S(1)}, f32[256,640]{1,0:T(8,128)S(1)}, u32[]{:S(2)}, u32[]{:S(2)}) collective-permute-start(f32[256,640]{1,0:T(8,128)S(1)} %constant_dynamic-slice_fusion), channel_id=1, source_target_pairs={{0,2},{1,7},{2,4},{3,1},{4,6},{5,3},{6,0},{7,5},{8,10},{9,15},{10,... | collective-permute-start | bytes 1966088 | tf_op jit(solution)/shard_map/ppermute | solution.py:326
  219.9 10.7 %collective-permute-start.16 = (f32[128,640]{1,0:T(8,128)S(1)}, f32[128,640]{1,0:T(8,128)S(1)}, u32[]{:S(2)}, u32[]{:S(2)}) collective-permute-start(f32[128,640]{1,0:T(8,128)S(1)} %constant_dynamic-slice_fusion.1), channel_id=1, source_target_pairs={{0,2},{1,7},{2,4},{3,1},{4,6},{5,3},{6,0},{7,5},{8,10},{9,15},{10,... | collective-permute-start | bytes 983048 | tf_op jit(solution)/shard_map/ppermute | solution.py:326
  (8 other events, 7.0 us)

commit v4 on v3

--- a/solution.py
+++ b/solution.py
@@ -117,6 +117,7 @@
 HALO = REACH * BLOCK
 VMEM = 56 * 1024 * 1024
 SHORT = pl.CostEstimate(flops=1, bytes_accessed=1, transcendentals=0)
+SOME = pl.CostEstimate(flops=10**10, bytes_accessed=4 * 10**7, transcendentals=0)
 LONG = pl.CostEstimate(flops=4 * 10**11, bytes_accessed=16 * 10**8, transcendentals=0)
 
 
@@ -266,53 +267,55 @@
     )(up.reshape(1).astype(jnp.int32), inner, covariance, outer, high, low)
 
 
-def right_kernel(odd, pair, strip, own, high, low, total, out, ext_high, ext_low):
-    rows, cols = own.shape
+def right_kernel(scalars, pair, strip, own, high, low, total, out, ext_high, ext_low):
+    cols = own.shape[1]
 
     def put(start, value):
         end = start + value.shape[1]
         ext_high[:, start:end], ext_low[:, start:end] = halves(value)
 
-    put(HALO, own[...])
-
-    @pl.when(odd[0] == 0)
+    g = pl.program_id(0)
+
+    @pl.when(g == 0)
+    def _():
+        put(HALO, own[...])
+
+    @pl.when((g == 0) & (scalars[0] == 0))
     def _():
         put(0, strip[...])
         put(HALO + cols, pair[:, :HALO])
 
-    @pl.when(odd[0] == 1)
+    @pl.when((g == 0) & (scalars[0] == 1))
     def _():
         put(0, pair[:, cols - HALO :])
         put(HALO + cols, strip[...])
 
+    window = pl.ds(pl.multiple_of(g * (GROUP * BLOCK), GROUP * BLOCK), WINDOW)
+    value = product(ext_high[:, window], ext_low[:, window], high[...], low[...], 1)
+    out[...] = total[...] + step_size * value
+
+
+def right_part(first, odd, pair, strip, covariance, high, low, total):
+    rows, cols = pair.shape
     step = GROUP * BLOCK
-    for g in range(cols // step):
-        here, window = slice(g * step, (g + 1) * step), slice(g * step, g * step + WINDOW)
-        value = product(ext_high[:, window], ext_low[:, window], high[here], low[here], 1)
-        out[:, here] = total[:, here] + step_size * value
-
-
-def right_part(first, odd, pair, strip, covariance, high, low, total, rows):
-    cols = covariance.shape[1]
-    count = pair.shape[0] // rows
     scalars = jnp.stack([odd, first]).astype(jnp.int32)
-    whole = pl.BlockSpec(high.shape, lambda j, s: (0, 0), pipeline_mode=pl.Buffered(1))
-    there = pl.BlockSpec((pl.Element(rows), pl.Element(cols)), lambda j, s: (pl.multiple_of(s[1] + j * rows, BLOCK), 0))
+    band_rows = pl.BlockSpec((step, WINDOW), lambda g, s: (g, 0))
+    here = pl.BlockSpec((pl.Element(rows), pl.Element(step)), lambda g, s: (pl.multiple_of(s[1], BLOCK), g * step))
     return pl.pallas_call(
         right_kernel,
         out_shape=jax.ShapeDtypeStruct(total.shape, jnp.float32),
         grid_spec=pltpu.PrefetchScalarGridSpec(
             num_scalar_prefetch=1,
-            grid=(count,),
+            grid=(cols // step,),
             in_specs=[
-                pl.BlockSpec((rows, cols), lambda j, s: (j, 0)),
-                pl.BlockSpec((rows, HALO), lambda j, s: (j, 0)),
-                there,
-                whole,
-                whole,
-                there,
+                pl.BlockSpec((rows, cols), lambda g, s: (0, 0)),
+                pl.BlockSpec((rows, HALO), lambda g, s: (0, 0)),
+                pl.BlockSpec((pl.Element(rows), pl.Element(cols)), lambda g, s: (pl.multiple_of(s[1], BLOCK), 0)),
+                band_rows,
+                band_rows,
+                here,
             ],
-            out_specs=there,
+            out_specs=here,
             scratch_shapes=[pltpu.VMEM((rows, cols + 2 * HALO), jnp.bfloat16)] * 2,
         ),
         input_output_aliases={6: 0},
@@ -443,7 +446,7 @@
 
     def add_right(total, j):
         first = jnp.int32(firsts[j])
-        return right_part(first, odd, pairs[j], strips[j], covariance, col_high, col_low, total, sizes[j])
+        return right_part(first, odd, pairs[j], strips[j], covariance, col_high, col_low, total)
 
     diagonal = packed_diagonal(covariance, offset, col_blocks)
     other = move(diagonal, [((r, c), (r, c ^ 1)) for r, c in devices if c // 2 == r])
@@ -479,8 +482,8 @@
     nearest = [place for place in places if place & (place - 1) == 0]
 
     pairs[0], outer = gate(pairs[0], outer, cost=LONG)
-    pairs[0], chunks[1], outer, inner, row_high, held[0] = gate(
-        pairs[0], chunks[1], outer, inner, row_high, held[0]
+    pairs[0], outer, inner, row_high, held[0], chunks[1], chunks[2], chunks[3] = gate(
+        pairs[0], outer, inner, row_high, held[0], chunks[1], chunks[2], chunks[3]
     )
     exchange(1)
     for place in nearest:
@@ -488,9 +491,11 @@
     hand_strip_on(0)
     total = left_part(up, inner, covariance, outer, row_high, row_low)
 
+    for place in nearest[:-1]:
+        (held[place],) = gate(held[place], cost=SOME)
     (pairs[1],) = gate(pairs[1], cost=LONG)
-    pairs[1], strips[0], total, chunks[2], chunks[3], *got = gate(
-        pairs[1], strips[0], total, chunks[2], chunks[3], *(held[place] for place in nearest)
+    pairs[1], strips[0], total, *got = gate(
+        pairs[1], strips[0], total, *(held[place] for place in nearest)
     )
     held.update(zip(nearest, got))
     for place in places[len(nearest) :]:

time: 241 us -> 240 us (level)
  Pallas kernels: 140 us -> 136 us
    pallas_call x5, Pallas kernels: 57.1 us -> 53.4 us  [right_part(): pl.pallas_call(right_kernel, out_shape=jax.ShapeDtypeStruct(total.shape,...]
  transfers between devices with their start and end apart: 18 -> 18, of which waited for: 8 -> 9; matrix products, arithmetic and copies ran while one was open for 11% -> 11% of each run, Pallas kernels for 54% -> 53%
where the time goes in v4:
time: 240 us; the launch traced here: 238 us
  Pallas kernels  136 us (57%)
  waiting for transfers between devices  34.4 us (14%)
  starting transfers between devices  31.3 us (13%)
  local copies, waits for them, and re-layouts  24.8 us (10%)
  other arithmetic  11.1 us (5%)
    pallas_call x5, Pallas kernels, right_part(): pl.pallas_call(right_kernel, out_shape=jax.ShapeDtypeStruct(total.shape,...  53.4 us
    ppermute x18, waiting for transfers between devices, send(): lax.ppermute(value, ('row', 'col'), [(a * cols + b, c * cols + d) for (a,...  34.4 us
    ppermute x18, starting transfers between devices, send(): lax.ppermute(value, ('row', 'col'), [(a * cols + b, c * cols + d) for (a,...  31.3 us
    pallas_call x1, Pallas kernels, left_part(): pl.pallas_call(left_kernel, out_shape=jax.ShapeDtypeStruct((rows, cols),...  28 us
    pallas_call x2, Pallas kernels, band(): pl.pallas_call(functools.partial(band_kernel, sources=len(sources), half=...  24.4 us
    pallas_call x7, Pallas kernels, rows_of(): pl.pallas_call(rows_kernel, out_shape=jax.ShapeDtypeStruct((size, cols),...  20.2 us
    unnamed x30, local copies, waits for them, and re-layouts  10.3 us
    dynamic_slice x5, local copies, waits for them, and re-layouts, hand_strip_on(): lax.dynamic_slice_in_dim(pairs[j], (1 - odd) * (tile_cols - HALO), HALO, 1)  9.77 us
  transfers between devices with their start and end apart: 18, of which 9 were waited for; matrix products, arithmetic and copies ran while one was open for 11% of the time, Pallas kernels for 53%

profile of v4, /device:TPU:0, one launch (start us, length us, event | category | flops | bytes accessed | tf_op | source)
XLA Modules:
  0.0 238.0 jit_solution(1196261462127295664)
XLA Ops:
  0.0 3.0 %packed_diagonal.1 = f32[4,128,128]{2,1,0:T(8,128)} custom-call(s32[1]{0:T(128)} %bitcast.1.first, f32[2048,1024]{1,0:T(8,128)} %own.11, f32[2048,1024]{1,0:T(8,128)} %own.11), custom_call_target="tpu_custom_call" | custom-call | flops 1 | bytes 1 | tf_op jit(solution)/shard_map/packed_diagonal/pallas_call | solution.py:379
  3.0 4.9 %collective-permute-start = (f32[4,128,128]{2,1,0:T(8,128)}, f32[4,128,128]{2,1,0:T(8,128)S(1)}, u32[]{:S(2)}, u32[]{:S(2)}) collective-permute-start(f32[4,128,128]{2,1,0:T(8,128)} %packed_diagonal.1), channel_id=1, source_target_pairs={{0,1},{1,0},{10,11},{11,10},{20,21},{21,20},{30,31},{31,30}} | collective-permute-start | bytes 786440 | tf_op jit(solution)/shard_map/ppermute | solution.py:329
  7.9 3.4 %rows_of.8 = f32[640,1024]{1,0:T(8,128)} custom-call(s32[1]{0:T(128)} %bitcast.2.first, f32[2048,1024]{1,0:T(8,128)} %own.11), custom_call_target="tpu_custom_call" | custom-call | flops 1 | bytes 1 | tf_op jit(solution)/shard_map/rows_of/pallas_call | solution.py:357
  11.3 3.4 %rows_of.7.refs_1_ = f32[640,1024]{1,0:T(8,128)} custom-call(s32[1]{0:T(128)} %constant.103.clone.1.first, f32[2048,1024]{1,0:T(8,128)} %own.11), custom_call_target="tpu_custom_call" | custom-call | flops 1 | bytes 1 | tf_op jit(solution)/shard_map/rows_of/pallas_call | solution.py:357
  16.5 4.9 %collective-permute-start.4 = (f32[8,128,128]{2,1,0:T(8,128)S(1)}, f32[8,128,128]{2,1,0:T(8,128)}, u32[]{:S(2)}, u32[]{:S(2)}) collective-permute-start(f32[8,128,128]{2,1,0:T(8,128)S(1)} %bitcast.14), channel_id=1, source_target_pairs={{0,4},{1,5},{10,14},{11,15},{20,16},{21,17},{30,26},{31,27}} | collective-permute-start | bytes 1572872 | tf_op jit(solution)/shard_map/ppermute | solution.py:329
  21.5 3.4 %rows_of.9 = f32[640,1024]{1,0:T(8,128)} custom-call(s32[1]{0:T(128)} %bitcast.3.first, f32[2048,1024]{1,0:T(8,128)} %own.11), custom_call_target="tpu_custom_call" | custom-call | flops 1 | bytes 1 | tf_op jit(solution)/shard_map/rows_of/pallas_call | solution.py:357
  30.3 3.4 %rows_of.10.refs_5_ = f32[640,1024]{1,0:T(8,128)} custom-call(s32[1]{0:T(128)} %constant.113.clone.1.first, f32[2048,1024]{1,0:T(8,128)} %own.11), custom_call_target="tpu_custom_call" | custom-call | flops 1 | bytes 1 | tf_op jit(solution)/shard_map/rows_of/pallas_call | solution.py:357
  39.5 15.0 %band.2 = (bf16[2048,1536]{1,0:T(8,128)(2,1)}, bf16[2048,1536]{1,0:T(8,128)(2,1)}) custom-call(s32[16,9]{1,0:T(8,128)} %fusion.2.places, f32[16]{0:T(128)} %dynamic_slice.30.gains, s32[3]{0:T(128)} %broadcast_12_scalars.2.scalars, f32[144,128,128]{2,1,0:T(8,128)} %bitcast.11), custom_call_target="tpu_custom_call" | custom-call | flops 1 | bytes 1 | tf_op jit(solution)/shard_map/band/pallas_call | solution.py:176
  62.9 7.1 %add_onsite.1 = (bf16[2048,1536]{1,0:T(8,128)(2,1)}, bf16[2048,1536]{1,0:T(8,128)(2,1)}) custom-call(f32[16]{0:T(128)} %dynamic_slice.30.gains, f32[8,128,128]{2,1,0:T(8,128)} %broadcast_select_fusion.1.refs_0_.refs_1_, f32[8,128,128]{2,1,0:T(8,128)} %broadcast_select_fusion.1.refs_0_.refs_1_, ...), custom_call_target="tpu_custom_call", output_to_operand_aliasing={{0}: (3, {}), {1}: (4, {})} | custom-call | flops 1 | bytes 1 | tf_op jit(solution)/shard_map/add_onsite/pallas_call | solution.py:219
  70.0 3.2 %collective-permute-done.1.refs_0_ = f32[640,1024]{1,0:T(8,128)S(1)} collective-permute-done((f32[640,1024]{1,0:T(8,128)}, f32[640,1024]{1,0:T(8,128)S(1)}, u32[]{:S(2)}, u32[]{:S(2)}) %collective-permute-start.1) | collective-permute-done | bytes 2621472 | tf_op jit(solution)/shard_map/ppermute | solution.py:329
  76.3 9.5 %collective-permute-start.9 = (f32[76,128,128]{2,1,0:T(8,128)}, f32[76,128,128]{2,1,0:T(8,128)}, u32[]{:S(2)}, u32[]{:S(2)}) collective-permute-start(f32[76,128,128]{2,1,0:T(8,128)} %get-tuple-element.49.refs_0_.refs_4_), channel_id=1, source_target_pairs={{0,16},{1,17},{10,26},{11,27},{20,4},{21,5},{30,14},{31,15}} | collective-permute-start | bytes 14942216 | tf_op jit(solution)/shard_map/ppermute | solution.py:329
  85.8 3.5 %collective-permute-start.10 = (f32[76,128,128]{2,1,0:T(8,128)}, f32[76,128,128]{2,1,0:T(8,128)}, u32[]{:S(2)}, u32[]{:S(2)}) collective-permute-start(f32[76,128,128]{2,1,0:T(8,128)} %get-tuple-element.49.refs_0_.refs_4_), channel_id=1, source_target_pairs={{0,8},{1,9},{10,2},{11,3},{20,28},{21,29},{30,22},{31,23}} | collective-permute-start | bytes 14942216 | tf_op jit(solution)/shard_map/ppermute | solution.py:329
  92.1 28.0 %left_part.1.refs_2_ = f32[2048,1024]{1,0:T(8,128)} custom-call(s32[1]{0:T(128)} %bitcast.8.up, f32[640,1024]{1,0:T(8,128)} %get-tuple-element.45.inner, f32[2048,1024]{1,0:T(8,128)} %own.11, f32[640,1024]{1,0:T(8,128)} %get-tuple-element.46.outer, bf16[2048,1536]{1,0:T(8,128)(2,1)} %get-tuple-element.47.high, bf16[2048,1536]{1,0:T(8,128)(2,1)} %get-tuple-element.48.low), custom_call_target="tpu_custom_call" | custom-call | flops 1 | bytes 1 | tf_op jit(solution)/shard_map/left_part/pallas_call | solution.py:254
  120.1 13.0 %collective-permute-done.7.refs_0_ = f32[640,1024]{1,0:T(8,128)S(1)} collective-permute-done((f32[640,1024]{1,0:T(8,128)}, f32[640,1024]{1,0:T(8,128)S(1)}, u32[]{:S(2)}, u32[]{:S(2)}) %collective-permute-start.7) | collective-permute-done | bytes 2621472 | tf_op jit(solution)/shard_map/ppermute | solution.py:329
  134.6 3.6 %collective-permute-done.9.refs_0_ = f32[76,128,128]{2,1,0:T(8,128)} collective-permute-done((f32[76,128,128]{2,1,0:T(8,128)}, f32[76,128,128]{2,1,0:T(8,128)}, u32[]{:S(2)}, u32[]{:S(2)}) %collective-permute-start.9) | collective-permute-done | bytes 4980768 | tf_op jit(solution)/shard_map/ppermute | solution.py:329
  138.3 2.9 %collective-permute-start.11 = (f32[76,128,128]{2,1,0:T(8,128)}, f32[76,128,128]{2,1,0:T(8,128)}, u32[]{:S(2)}, u32[]{:S(2)}) collective-permute-start(f32[76,128,128]{2,1,0:T(8,128)} %get-tuple-element.52.refs_2_.refs_6_), channel_id=1, source_target_pairs={{4,12},{5,13},{14,6},{15,7},{16,24},{17,25},{26,18},{27,19}} | collective-permute-start | bytes 14942216 | tf_op jit(solution)/shard_map/ppermute | solution.py:329
  150.6 9.4 %band.3 = (bf16[1024,1536]{1,0:T(8,128)(2,1)}, bf16[1024,1536]{1,0:T(8,128)(2,1)}) custom-call(s32[8,9]{1,0:T(8,128)} %fusion.5.places, f32[8]{0:T(128)} %dynamic_slice.35.gains, s32[3]{0:T(128)} %pad_add_fusion.2.scalars, f32[76,128,128]{2,1,0:T(8,128)} %get-tuple-element.49.refs_0_.refs_4_, f32[76,128,128]{2,1,0:T(8,128)} %get-tuple-element.51.refs_1_.refs_5_, ...), custom_call_target="tpu_custom_call" | custom-call | flops 1 | bytes 1 | tf_op jit(solution)/shard_map/band/pallas_call | solution.py:176
  160.0 13.5 %right_part.5.refs_1_ = f32[2048,1024]{1,0:T(8,128)} custom-call(s32[2]{0:T(128)} %pad_add_fusion.1.scalars, f32[640,1024]{1,0:T(8,128)} %get-tuple-element.43.pair, f32[640,640]{1,0:T(8,128)} %get-tuple-element.50.strip, f32[2048,1024]{1,0:T(8,128)} %own.11, bf16[1024,1536]{1,0:T(8,128)(2,1)} %get-tuple-element.53.high, ...), custom_call_target="tpu_custom_call", output_to_operand_aliasing={{}: (6, {})} | custom-call | flops 1 | bytes 1 | tf_op jit(solution)/shard_map/right_part/pallas_call | solution.py:304
  173.4 5.3 %collective-permute-done.6.refs_0_ = f32[384,1024]{1,0:T(8,128)S(1)} collective-permute-done((f32[384,1024]{1,0:T(8,128)}, f32[384,1024]{1,0:T(8,128)S(1)}, u32[]{:S(2)}, u32[]{:S(2)}) %collective-permute-start.6) | collective-permute-done | bytes 1572896 | tf_op jit(solution)/shard_map/ppermute | solution.py:329
  183.9 13.5 %right_part.6.refs_1_ = f32[2048,1024]{1,0:T(8,128)} custom-call(s32[2]{0:T(128)} %pad_add_fusion.4.scalars, f32[640,1024]{1,0:T(8,128)} %get-tuple-element.59.pair, f32[640,640]{1,0:T(8,128)} %collective-permute-done.15.strip, f32[2048,1024]{1,0:T(8,128)} %own.11, bf16[1024,1536]{1,0:T(8,128)(2,1)} %get-tuple-element.53.high, ...), custom_call_target="tpu_custom_call", output_to_operand_aliasing={{}: (6, {})} | custom-call | flops 1 | bytes 1 | tf_op jit(solution)/shard_map/right_part/pallas_call | solution.py:304
  197.4 3.4 %collective-permute-done.14.refs_0_ = f32[256,1024]{1,0:T(8,128)S(1)} collective-permute-done((f32[256,1024]{1,0:T(8,128)}, f32[256,1024]{1,0:T(8,128)S(1)}, u32[]{:S(2)}, u32[]{:S(2)}) %collective-permute-start.14) | collective-permute-done | bytes 1048608 | tf_op jit(solution)/shard_map/ppermute | solution.py:329
  207.0 10.1 %right_part.7.refs_1_ = f32[2048,1024]{1,0:T(8,128)} custom-call(s32[2]{0:T(128)} %pad_add_fusion.3.scalars, f32[384,1024]{1,0:T(8,128)} %get-tuple-element.57.pair, f32[384,640]{1,0:T(8,128)} %copy-done.9, f32[2048,1024]{1,0:T(8,128)} %own.11, bf16[1024,1536]{1,0:T(8,128)(2,1)} %get-tuple-element.53.high, ...), custom_call_target="tpu_custom_call", output_to_operand_aliasing={{}: (6, {})} | custom-call | flops 1 | bytes 1 | tf_op jit(solution)/shard_map/right_part/pallas_call | solution.py:304
  220.8 8.5 %right_part.8.total = f32[2048,1024]{1,0:T(8,128)} custom-call(s32[2]{0:T(128)} %get-tuple-element.66.scalars, f32[256,1024]{1,0:T(8,128)} %get-tuple-element.63.pair, f32[256,640]{1,0:T(8,128)} %copy-done.10, f32[2048,1024]{1,0:T(8,128)} %own.11, bf16[1024,1536]{1,0:T(8,128)(2,1)} %get-tuple-element.53.high, ...), custom_call_target="tpu_custom_call", output_to_operand_aliasing={{}: (6, {})} | custom-call | flops 1 | bytes 1 | tf_op jit(solution)/shard_map/right_part/pallas_call | solution.py:304
  230.1 7.9 %right_part.9 = f32[2048,1024]{1,0:T(8,128)} custom-call(s32[2]{0:T(128)} %get-tuple-element.65.scalars, f32[128,1024]{1,0:T(8,128)} %get-tuple-element.62.pair, f32[128,640]{1,0:T(8,128)} %copy-done.11, f32[2048,1024]{1,0:T(8,128)} %own.11, bf16[1024,1536]{1,0:T(8,128)(2,1)} %get-tuple-element.53.high, ...), custom_call_target="tpu_custom_call", output_to_operand_aliasing={{}: (6, {})} | custom-call | flops 1 | bytes 1 | tf_op jit(solution)/shard_map/right_part/pallas_call | solution.py:304
  (94 shorter events, 54.0 us)
Async XLA Ops:
  0.0 24.9 %copy-start = (s32[64,9]{0,1:T(8,128)S(1)}, s32[64,9]{0,1:T(8,128)}, u32[]{:S(2)}) copy-start(s32[64,9]{0,1:T(8,128)} %param.6) | copy-start | bytes 6916
  3.0 11.7 %collective-permute-start = (f32[4,128,128]{2,1,0:T(8,128)}, f32[4,128,128]{2,1,0:T(8,128)S(1)}, u32[]{:S(2)}, u32[]{:S(2)}) collective-permute-start(f32[4,128,128]{2,1,0:T(8,128)} %packed_diagonal.1), channel_id=1, source_target_pairs={{0,1},{1,0},{10,11},{11,10},{20,21},{21,20},{30,31},{31,30}} | collective-permute-start | bytes 786440 | tf_op jit(solution)/shard_map/ppermute | solution.py:329
  11.3 4.2 %copy-start.6 = (f32[4,128,128]{2,1,0:T(8,128)S(1)}, f32[4,128,128]{2,1,0:T(8,128)}, u32[]{:S(2)}) copy-start(f32[4,128,128]{2,1,0:T(8,128)} %packed_diagonal.1) | copy-start | bytes 786436
  11.3 58.7 %collective-permute-start.2 = (f32[640,1024]{1,0:T(8,128)}, f32[640,1024]{1,0:T(8,128)}, u32[]{:S(2)}, u32[]{:S(2)}) collective-permute-start(f32[640,1024]{1,0:T(8,128)} %rows_of.8), channel_id=1, source_target_pairs={{0,24},{1,25},{2,26},{3,27},{4,28},{5,29},{6,30},{7,31},{8,16},{9,... | collective-permute-start | bytes 7864328 | tf_op jit(solution)/shard_map/ppermute | solution.py:329
  15.4 57.8 %collective-permute-start.1 = (f32[640,1024]{1,0:T(8,128)}, f32[640,1024]{1,0:T(8,128)S(1)}, u32[]{:S(2)}, u32[]{:S(2)}) collective-permute-start(f32[640,1024]{1,0:T(8,128)} %get-tuple-element.35), channel_id=1, source_target_pairs={{0,1},{1,0},{2,3},{3,2},{4,5},{5,4},{6,7},{7,6},{8,9},{9,8},{10,11... | collective-permute-start | bytes 7864328 | tf_op jit(solution)/shard_map/ppermute | solution.py:329
  16.5 10.9 %collective-permute-start.4 = (f32[8,128,128]{2,1,0:T(8,128)S(1)}, f32[8,128,128]{2,1,0:T(8,128)}, u32[]{:S(2)}, u32[]{:S(2)}) collective-permute-start(f32[8,128,128]{2,1,0:T(8,128)S(1)} %bitcast.14), channel_id=1, source_target_pairs={{0,4},{1,5},{10,14},{11,15},{20,16},{21,17},{30,26},{31,27}} | collective-permute-start | bytes 1572872 | tf_op jit(solution)/shard_map/ppermute | solution.py:329
  24.9 49.8 %collective-permute-start.3 = (f32[640,1024]{1,0:T(8,128)}, f32[640,1024]{1,0:T(8,128)}, u32[]{:S(2)}, u32[]{:S(2)}) collective-permute-start(f32[640,1024]{1,0:T(8,128)} %rows_of.9), channel_id=1, source_target_pairs={{0,8},{1,9},{2,10},{3,11},{4,12},{5,13},{6,14},{7,15},{8,0},{9,1},... | collective-permute-start | bytes 7864328 | tf_op jit(solution)/shard_map/ppermute | solution.py:329
  28.3 31.8 %collective-permute-start.5 = (f32[8,128,128]{2,1,0:T(8,128)}, f32[8,128,128]{2,1,0:T(8,128)S(1)}, u32[]{:S(2)}, u32[]{:S(2)}) collective-permute-start(f32[8,128,128]{2,1,0:T(8,128)} %broadcast_select_fusion), channel_id=1, source_target_pairs={{0,2},{1,3},{4,6},{5,7},{10,8},{11,9},{14,12},{15,13},{16,18},{17,... | collective-permute-start | bytes 1572872 | tf_op jit(solution)/shard_map/ppermute | solution.py:329
  36.3 2.1 copy-start.12
  73.2 1.5 copy-start.1
  74.8 58.3 %collective-permute-start.7 = (f32[640,1024]{1,0:T(8,128)}, f32[640,1024]{1,0:T(8,128)S(1)}, u32[]{:S(2)}, u32[]{:S(2)}) collective-permute-start(f32[640,1024]{1,0:T(8,128)} %get-tuple-element.44), channel_id=1, source_target_pairs={{0,1},{1,0},{2,3},{3,2},{4,5},{5,4},{6,7},{7,6},{8,9},{9,8},{10,11... | collective-permute-start | bytes 7864328 | tf_op jit(solution)/shard_map/ppermute | solution.py:329
  76.3 62.0 %collective-permute-start.9 = (f32[76,128,128]{2,1,0:T(8,128)}, f32[76,128,128]{2,1,0:T(8,128)}, u32[]{:S(2)}, u32[]{:S(2)}) collective-permute-start(f32[76,128,128]{2,1,0:T(8,128)} %get-tuple-element.49.refs_0_.refs_4_), channel_id=1, source_target_pairs={{0,16},{1,17},{10,26},{11,27},{20,4},{21,5},{30,14},{31,15}} | collective-permute-start | bytes 14942216 | tf_op jit(solution)/shard_map/ppermute | solution.py:329
  85.8 52.4 %collective-permute-start.10 = (f32[76,128,128]{2,1,0:T(8,128)}, f32[76,128,128]{2,1,0:T(8,128)}, u32[]{:S(2)}, u32[]{:S(2)}) collective-permute-start(f32[76,128,128]{2,1,0:T(8,128)} %get-tuple-element.49.refs_0_.refs_4_), channel_id=1, source_target_pairs={{0,8},{1,9},{10,2},{11,3},{20,28},{21,29},{30,22},{31,23}} | collective-permute-start | bytes 14942216 | tf_op jit(solution)/shard_map/ppermute | solution.py:329
  92.1 46.2 %collective-permute-start.8 = (f32[640,640]{1,0:T(8,128)}, f32[640,640]{1,0:T(8,128)}, u32[]{:S(2)}, u32[]{:S(2)}) collective-permute-start(f32[640,640]{1,0:T(8,128)} %constant_dynamic-slice_fusion.5), channel_id=1, source_target_pairs={{0,2},{1,7},{2,4},{3,1},{4,6},{5,3},{6,0},{7,5},{8,10},{9,15},{10,... | collective-permute-start | bytes 4915208 | tf_op jit(solution)/shard_map/ppermute | solution.py:329
  133.0 1.6 copy-start.2
  138.3 12.3 %collective-permute-start.11 = (f32[76,128,128]{2,1,0:T(8,128)}, f32[76,128,128]{2,1,0:T(8,128)}, u32[]{:S(2)}, u32[]{:S(2)}) collective-permute-start(f32[76,128,128]{2,1,0:T(8,128)} %get-tuple-element.52.refs_2_.refs_6_), channel_id=1, source_target_pairs={{4,12},{5,13},{14,6},{15,7},{16,24},{17,25},{26,18},{27,19}} | collective-permute-start | bytes 14942216 | tf_op jit(solution)/shard_map/ppermute | solution.py:329
  141.2 37.5 %collective-permute-start.6 = (f32[384,1024]{1,0:T(8,128)}, f32[384,1024]{1,0:T(8,128)S(1)}, u32[]{:S(2)}, u32[]{:S(2)}) collective-permute-start(f32[384,1024]{1,0:T(8,128)} %get-tuple-element.42), channel_id=1, source_target_pairs={{0,1},{1,0},{2,3},{3,2},{4,5},{5,4},{6,7},{7,6},{8,9},{9,8},{10,11... | collective-permute-start | bytes 4718600 | tf_op jit(solution)/shard_map/ppermute | solution.py:329
  144.4 39.5 %collective-permute-start.15 = (f32[640,640]{1,0:T(8,128)}, f32[640,640]{1,0:T(8,128)}, u32[]{:S(2)}, u32[]{:S(2)}) collective-permute-start(f32[640,640]{1,0:T(8,128)} %constant_dynamic-slice_fusion.2), channel_id=1, source_target_pairs={{0,2},{1,7},{2,4},{3,1},{4,6},{5,3},{6,0},{7,5},{8,10},{9,15},{10,... | collective-permute-start | bytes 4915208 | tf_op jit(solution)/shard_map/ppermute | solution.py:329
  145.7 55.0 %collective-permute-start.14 = (f32[256,1024]{1,0:T(8,128)}, f32[256,1024]{1,0:T(8,128)S(1)}, u32[]{:S(2)}, u32[]{:S(2)}) collective-permute-start(f32[256,1024]{1,0:T(8,128)} %get-tuple-element.58), channel_id=1, source_target_pairs={{0,1},{1,0},{2,3},{3,2},{4,5},{5,4},{6,7},{7,6},{8,9},{9,8},{10,11... | collective-permute-start | bytes 3145736 | tf_op jit(solution)/shard_map/ppermute | solution.py:329
  147.3 1.9 copy-start.13
  182.1 23.9 %collective-permute-start.13 = (f32[384,640]{1,0:T(8,128)}, f32[384,640]{1,0:T(8,128)S(1)}, u32[]{:S(2)}, u32[]{:S(2)}) collective-permute-start(f32[384,640]{1,0:T(8,128)} %constant_dynamic-slice_fusion.3), channel_id=1, source_target_pairs={{0,2},{1,7},{2,4},{3,1},{4,6},{5,3},{6,0},{7,5},{8,10},{9,15},{10,... | collective-permute-start | bytes 2949128 | tf_op jit(solution)/shard_map/ppermute | solution.py:329
  182.1 35.0 %collective-permute-start.12 = (f32[128,1024]{1,0:T(8,128)}, f32[128,1024]{1,0:T(8,128)S(1)}, u32[]{:S(2)}, u32[]{:S(2)}) collective-permute-start(f32[128,1024]{1,0:T(8,128)} %get-tuple-element.56), channel_id=1, source_target_pairs={{0,1},{1,0},{2,3},{3,2},{4,5},{5,4},{6,7},{7,6},{8,9},{9,8},{10,11... | collective-permute-start | bytes 1572872 | tf_op jit(solution)/shard_map/ppermute | solution.py:329
  202.9 17.1 %collective-permute-start.17 = (f32[256,640]{1,0:T(8,128)S(1)}, f32[256,640]{1,0:T(8,128)S(1)}, u32[]{:S(2)}, u32[]{:S(2)}) collective-permute-start(f32[256,640]{1,0:T(8,128)S(1)} %constant_dynamic-slice_fusion), channel_id=1, source_target_pairs={{0,2},{1,7},{2,4},{3,1},{4,6},{5,3},{6,0},{7,5},{8,10},{9,15},{10,... | collective-permute-start | bytes 1966088 | tf_op jit(solution)/shard_map/ppermute | solution.py:329
  219.0 10.4 %collective-permute-start.16 = (f32[128,640]{1,0:T(8,128)S(1)}, f32[128,640]{1,0:T(8,128)S(1)}, u32[]{:S(2)}, u32[]{:S(2)}) collective-permute-start(f32[128,640]{1,0:T(8,128)S(1)} %constant_dynamic-slice_fusion.1), channel_id=1, source_target_pairs={{0,2},{1,7},{2,4},{3,1},{4,6},{5,3},{6,0},{7,5},{8,10},{9,15},{10,... | collective-permute-start | bytes 983048 | tf_op jit(solution)/shard_map/ppermute | solution.py:329
  (8 other events, 7.0 us)

commit v5 on v4

--- a/solution.py
+++ b/solution.py
@@ -341,10 +341,10 @@
     first = total * 5 // 16 // BLOCK * BLOCK
     sizes = [first, first]
     left = total - 2 * first
-    while left > BLOCK:
-        sizes.append(-(-left // (2 * BLOCK)) * BLOCK)
+    while left:
+        sizes.append(min(left, 2 * BLOCK))
         left -= sizes[-1]
-    return sizes + [left] * (left > 0)
+    return sizes
 
 
 def rows_kernel(first, rows, out):

time: 240 us -> 243 us (1.012)
  starting transfers between devices: 31.3 us -> 35.6 us
    ppermute x18, starting transfers between devices: 31.3 us -> 35.6 us  [send(): lax.ppermute(value, ('row', 'col'), [(a * cols + b, c * cols + d) for (a,...]
  transfers between devices with their start and end apart: 18 -> 18, of which waited for: 9 -> 7; matrix products, arithmetic and copies ran while one was open for 11% -> 10% of each run, Pallas kernels for 53% -> 51%
where the time goes in v5:
time: 243 us; the launch traced here: 241 us
  Pallas kernels  135 us (56%)
  waiting for transfers between devices  36.2 us (15%)
  starting transfers between devices  35.6 us (15%)
  local copies, waits for them, and re-layouts  23.1 us (10%)
  other arithmetic  11.2 us (5%)
    pallas_call x5, Pallas kernels, right_part(): pl.pallas_call(right_kernel, out_shape=jax.ShapeDtypeStruct(total.shape,...  52.5 us
    ppermute x18, waiting for transfers between devices, send(): lax.ppermute(value, ('row', 'col'), [(a * cols + b, c * cols + d) for (a,...  36.2 us
    ppermute x18, starting transfers between devices, send(): lax.ppermute(value, ('row', 'col'), [(a * cols + b, c * cols + d) for (a,...  35.6 us
    pallas_call x1, Pallas kernels, left_part(): pl.pallas_call(left_kernel, out_shape=jax.ShapeDtypeStruct((rows, cols),...  28 us
    pallas_call x2, Pallas kernels, band(): pl.pallas_call(functools.partial(band_kernel, sources=len(sources), half=...  24.4 us
    pallas_call x7, Pallas kernels, rows_of(): pl.pallas_call(rows_kernel, out_shape=jax.ShapeDtypeStruct((size, cols),...  19.8 us
    unnamed x30, local copies, waits for them, and re-layouts  9.47 us
    dynamic_slice x5, local copies, waits for them, and re-layouts, hand_strip_on(): lax.dynamic_slice_in_dim(pairs[j], (1 - odd) * (tile_cols - HALO), HALO, 1)  8.81 us
  transfers between devices with their start and end apart: 18, of which 7 were waited for; matrix products, arithmetic and copies ran while one was open for 10% of the time, Pallas kernels for 51%

profile of v5, /device:TPU:0, one launch (start us, length us, event | category | flops | bytes accessed | tf_op | source)
XLA Modules:
  0.0 241.0 jit_solution(17982484417713237128)
XLA Ops:
  0.0 3.0 %packed_diagonal.1 = f32[4,128,128]{2,1,0:T(8,128)} custom-call(s32[1]{0:T(128)} %bitcast.1.first, f32[2048,1024]{1,0:T(8,128)} %own.11, f32[2048,1024]{1,0:T(8,128)} %own.11), custom_call_target="tpu_custom_call" | custom-call | flops 1 | bytes 1 | tf_op jit(solution)/shard_map/packed_diagonal/pallas_call | solution.py:379
  3.0 4.9 %collective-permute-start = (f32[4,128,128]{2,1,0:T(8,128)}, f32[4,128,128]{2,1,0:T(8,128)S(1)}, u32[]{:S(2)}, u32[]{:S(2)}) collective-permute-start(f32[4,128,128]{2,1,0:T(8,128)} %packed_diagonal.1), channel_id=1, source_target_pairs={{0,1},{1,0},{10,11},{11,10},{20,21},{21,20},{30,31},{31,30}} | collective-permute-start | bytes 786440 | tf_op jit(solution)/shard_map/ppermute | solution.py:329
  7.9 3.4 %rows_of.8 = f32[640,1024]{1,0:T(8,128)} custom-call(s32[1]{0:T(128)} %bitcast.2.first, f32[2048,1024]{1,0:T(8,128)} %own.11), custom_call_target="tpu_custom_call" | custom-call | flops 1 | bytes 1 | tf_op jit(solution)/shard_map/rows_of/pallas_call | solution.py:357
  11.3 3.4 %rows_of.7.refs_1_ = f32[640,1024]{1,0:T(8,128)} custom-call(s32[1]{0:T(128)} %constant.103.clone.1.first, f32[2048,1024]{1,0:T(8,128)} %own.11), custom_call_target="tpu_custom_call" | custom-call | flops 1 | bytes 1 | tf_op jit(solution)/shard_map/rows_of/pallas_call | solution.py:357
  16.5 4.9 %collective-permute-start.4 = (f32[8,128,128]{2,1,0:T(8,128)S(1)}, f32[8,128,128]{2,1,0:T(8,128)}, u32[]{:S(2)}, u32[]{:S(2)}) collective-permute-start(f32[8,128,128]{2,1,0:T(8,128)S(1)} %bitcast.14), channel_id=1, source_target_pairs={{0,4},{1,5},{10,14},{11,15},{20,16},{21,17},{30,26},{31,27}} | collective-permute-start | bytes 1572872 | tf_op jit(solution)/shard_map/ppermute | solution.py:329
  21.5 3.4 %rows_of.9 = f32[640,1024]{1,0:T(8,128)} custom-call(s32[1]{0:T(128)} %bitcast.3.first, f32[2048,1024]{1,0:T(8,128)} %own.11), custom_call_target="tpu_custom_call" | custom-call | flops 1 | bytes 1 | tf_op jit(solution)/shard_map/rows_of/pallas_call | solution.py:357
  30.3 3.4 %rows_of.10.refs_5_ = f32[640,1024]{1,0:T(8,128)} custom-call(s32[1]{0:T(128)} %constant.113.clone.1.first, f32[2048,1024]{1,0:T(8,128)} %own.11), custom_call_target="tpu_custom_call" | custom-call | flops 1 | bytes 1 | tf_op jit(solution)/shard_map/rows_of/pallas_call | solution.py:357
  38.9 15.0 %band.2 = (bf16[2048,1536]{1,0:T(8,128)(2,1)}, bf16[2048,1536]{1,0:T(8,128)(2,1)}) custom-call(s32[16,9]{1,0:T(8,128)} %fusion.2.places, f32[16]{0:T(128)} %dynamic_slice.30.gains, s32[3]{0:T(128)} %broadcast_12_scalars.2.scalars, f32[144,128,128]{2,1,0:T(8,128)} %bitcast.11), custom_call_target="tpu_custom_call" | custom-call | flops 1 | bytes 1 | tf_op jit(solution)/shard_map/band/pallas_call | solution.py:176
  62.3 7.1 %add_onsite.1 = (bf16[2048,1536]{1,0:T(8,128)(2,1)}, bf16[2048,1536]{1,0:T(8,128)(2,1)}) custom-call(f32[16]{0:T(128)} %dynamic_slice.30.gains, f32[8,128,128]{2,1,0:T(8,128)} %broadcast_select_fusion.1.refs_0_.refs_1_, f32[8,128,128]{2,1,0:T(8,128)} %broadcast_select_fusion.1.refs_0_.refs_1_, ...), custom_call_target="tpu_custom_call", output_to_operand_aliasing={{0}: (3, {}), {1}: (4, {})} | custom-call | flops 1 | bytes 1 | tf_op jit(solution)/shard_map/add_onsite/pallas_call | solution.py:219
  69.5 3.8 %collective-permute-done.1.refs_0_ = f32[640,1024]{1,0:T(8,128)S(1)} collective-permute-done((f32[640,1024]{1,0:T(8,128)}, f32[640,1024]{1,0:T(8,128)S(1)}, u32[]{:S(2)}, u32[]{:S(2)}) %collective-permute-start.1) | collective-permute-done | bytes 2621472 | tf_op jit(solution)/shard_map/ppermute | solution.py:329
  76.3 9.0 %collective-permute-start.9 = (f32[76,128,128]{2,1,0:T(8,128)}, f32[76,128,128]{2,1,0:T(8,128)}, u32[]{:S(2)}, u32[]{:S(2)}) collective-permute-start(f32[76,128,128]{2,1,0:T(8,128)} %get-tuple-element.49.refs_0_.refs_4_), channel_id=1, source_target_pairs={{0,16},{1,17},{10,26},{11,27},{20,4},{21,5},{30,14},{31,15}} | collective-permute-start | bytes 14942216 | tf_op jit(solution)/shard_map/ppermute | solution.py:329
  85.3 3.5 %collective-permute-start.10 = (f32[76,128,128]{2,1,0:T(8,128)}, f32[76,128,128]{2,1,0:T(8,128)}, u32[]{:S(2)}, u32[]{:S(2)}) collective-permute-start(f32[76,128,128]{2,1,0:T(8,128)} %get-tuple-element.49.refs_0_.refs_4_), channel_id=1, source_target_pairs={{0,8},{1,9},{10,2},{11,3},{20,28},{21,29},{30,22},{31,23}} | collective-permute-start | bytes 14942216 | tf_op jit(solution)/shard_map/ppermute | solution.py:329
  91.5 28.0 %left_part.1.refs_2_ = f32[2048,1024]{1,0:T(8,128)} custom-call(s32[1]{0:T(128)} %bitcast.8.up, f32[640,1024]{1,0:T(8,128)} %get-tuple-element.45.inner, f32[2048,1024]{1,0:T(8,128)} %own.11, f32[640,1024]{1,0:T(8,128)} %get-tuple-element.46.outer, bf16[2048,1536]{1,0:T(8,128)(2,1)} %get-tuple-element.47.high, bf16[2048,1536]{1,0:T(8,128)(2,1)} %get-tuple-element.48.low), custom_call_target="tpu_custom_call" | custom-call | flops 1 | bytes 1 | tf_op jit(solution)/shard_map/left_part/pallas_call | solution.py:254
  119.5 13.5 %collective-permute-done.7.refs_0_ = f32[640,1024]{1,0:T(8,128)S(1)} collective-permute-done((f32[640,1024]{1,0:T(8,128)}, f32[640,1024]{1,0:T(8,128)S(1)}, u32[]{:S(2)}, u32[]{:S(2)}) %collective-permute-start.7) | collective-permute-done | bytes 2621472 | tf_op jit(solution)/shard_map/ppermute | solution.py:329
  134.6 3.1 %collective-permute-done.9.refs_0_ = f32[76,128,128]{2,1,0:T(8,128)} collective-permute-done((f32[76,128,128]{2,1,0:T(8,128)}, f32[76,128,128]{2,1,0:T(8,128)}, u32[]{:S(2)}, u32[]{:S(2)}) %collective-permute-start.9) | collective-permute-done | bytes 4980768 | tf_op jit(solution)/shard_map/ppermute | solution.py:329
  137.7 3.1 %collective-permute-start.11 = (f32[76,128,128]{2,1,0:T(8,128)}, f32[76,128,128]{2,1,0:T(8,128)}, u32[]{:S(2)}, u32[]{:S(2)}) collective-permute-start(f32[76,128,128]{2,1,0:T(8,128)} %get-tuple-element.52.refs_2_.refs_6_), channel_id=1, source_target_pairs={{4,12},{5,13},{14,6},{15,7},{16,24},{17,25},{26,18},{27,19}} | collective-permute-start | bytes 14942216 | tf_op jit(solution)/shard_map/ppermute | solution.py:329
  150.3 9.4 %band.3 = (bf16[1024,1536]{1,0:T(8,128)(2,1)}, bf16[1024,1536]{1,0:T(8,128)(2,1)}) custom-call(s32[8,9]{1,0:T(8,128)} %fusion.5.places, f32[8]{0:T(128)} %dynamic_slice.35.gains, s32[3]{0:T(128)} %pad_add_fusion.2.scalars, f32[76,128,128]{2,1,0:T(8,128)} %get-tuple-element.49.refs_0_.refs_4_, f32[76,128,128]{2,1,0:T(8,128)} %get-tuple-element.51.refs_1_.refs_5_, ...), custom_call_target="tpu_custom_call" | custom-call | flops 1 | bytes 1 | tf_op jit(solution)/shard_map/band/pallas_call | solution.py:176
  159.7 13.4 %right_part.5.refs_1_ = f32[2048,1024]{1,0:T(8,128)} custom-call(s32[2]{0:T(128)} %pad_add_fusion.1.scalars, f32[640,1024]{1,0:T(8,128)} %get-tuple-element.43.pair, f32[640,640]{1,0:T(8,128)} %get-tuple-element.50.strip, f32[2048,1024]{1,0:T(8,128)} %own.11, bf16[1024,1536]{1,0:T(8,128)(2,1)} %get-tuple-element.53.high, ...), custom_call_target="tpu_custom_call", output_to_operand_aliasing={{}: (6, {})} | custom-call | flops 1 | bytes 1 | tf_op jit(solution)/shard_map/right_part/pallas_call | solution.py:304
  179.9 4.8 %collective-permute-done.15.strip = f32[640,640]{1,0:T(8,128)} collective-permute-done((f32[640,640]{1,0:T(8,128)}, f32[640,640]{1,0:T(8,128)}, u32[]{:S(2)}, u32[]{:S(2)}) %collective-permute-start.15) | collective-permute-done | bytes 1638432 | tf_op jit(solution)/shard_map/ppermute | solution.py:329
  184.8 13.5 %right_part.6.refs_1_ = f32[2048,1024]{1,0:T(8,128)} custom-call(s32[2]{0:T(128)} %pad_add_fusion.4.scalars, f32[640,1024]{1,0:T(8,128)} %get-tuple-element.59.pair, f32[640,640]{1,0:T(8,128)} %collective-permute-done.15.strip, f32[2048,1024]{1,0:T(8,128)} %own.11, bf16[1024,1536]{1,0:T(8,128)(2,1)} %get-tuple-element.53.high, ...), custom_call_target="tpu_custom_call", output_to_operand_aliasing={{}: (6, {})} | custom-call | flops 1 | bytes 1 | tf_op jit(solution)/shard_map/right_part/pallas_call | solution.py:304
  200.4 8.5 %right_part.7.refs_1_ = f32[2048,1024]{1,0:T(8,128)} custom-call(s32[2]{0:T(128)} %pad_add_fusion.3.scalars, f32[256,1024]{1,0:T(8,128)} %get-tuple-element.57.pair, f32[256,640]{1,0:T(8,128)} %collective-permute-done.13.strip, f32[2048,1024]{1,0:T(8,128)} %own.11, bf16[1024,1536]{1,0:T(8,128)(2,1)} %get-tuple-element.53.high, ...), custom_call_target="tpu_custom_call", output_to_operand_aliasing={{}: (6, {})} | custom-call | flops 1 | bytes 1 | tf_op jit(solution)/shard_map/right_part/pallas_call | solution.py:304
  213.6 6.3 %collective-permute-done.17.strip = f32[256,640]{1,0:T(8,128)S(1)} collective-permute-done((f32[256,640]{1,0:T(8,128)S(1)}, f32[256,640]{1,0:T(8,128)S(1)}, u32[]{:S(2)}, u32[]{:S(2)}) %collective-permute-start.17) | collective-permute-done | bytes 655392 | tf_op jit(solution)/shard_map/ppermute | solution.py:329
  220.7 8.5 %right_part.8.total = f32[2048,1024]{1,0:T(8,128)} custom-call(s32[2]{0:T(128)} %get-tuple-element.66.scalars, f32[256,1024]{1,0:T(8,128)} %get-tuple-element.63.pair, f32[256,640]{1,0:T(8,128)} %copy-done.10, f32[2048,1024]{1,0:T(8,128)} %own.11, bf16[1024,1536]{1,0:T(8,128)(2,1)} %get-tuple-element.53.high, ...), custom_call_target="tpu_custom_call", output_to_operand_aliasing={{}: (6, {})} | custom-call | flops 1 | bytes 1 | tf_op jit(solution)/shard_map/right_part/pallas_call | solution.py:304
  232.4 8.5 %right_part.9 = f32[2048,1024]{1,0:T(8,128)} custom-call(s32[2]{0:T(128)} %get-tuple-element.65.scalars, f32[256,1024]{1,0:T(8,128)} %get-tuple-element.62.pair, f32[256,640]{1,0:T(8,128)} %copy-done.11, f32[2048,1024]{1,0:T(8,128)} %own.11, bf16[1024,1536]{1,0:T(8,128)(2,1)} %get-tuple-element.53.high, ...), custom_call_target="tpu_custom_call", output_to_operand_aliasing={{}: (6, {})} | custom-call | flops 1 | bytes 1 | tf_op jit(solution)/shard_map/right_part/pallas_call | solution.py:304
  (94 shorter events, 55.4 us)
Async XLA Ops:
  0.0 24.9 %copy-start = (s32[64,9]{0,1:T(8,128)S(1)}, s32[64,9]{0,1:T(8,128)}, u32[]{:S(2)}) copy-start(s32[64,9]{0,1:T(8,128)} %param.6) | copy-start | bytes 6916
  3.0 11.7 %collective-permute-start = (f32[4,128,128]{2,1,0:T(8,128)}, f32[4,128,128]{2,1,0:T(8,128)S(1)}, u32[]{:S(2)}, u32[]{:S(2)}) collective-permute-start(f32[4,128,128]{2,1,0:T(8,128)} %packed_diagonal.1), channel_id=1, source_target_pairs={{0,1},{1,0},{10,11},{11,10},{20,21},{21,20},{30,31},{31,30}} | collective-permute-start | bytes 786440 | tf_op jit(solution)/shard_map/ppermute | solution.py:329
  11.3 4.2 %copy-start.7 = (f32[4,128,128]{2,1,0:T(8,128)S(1)}, f32[4,128,128]{2,1,0:T(8,128)}, u32[]{:S(2)}) copy-start(f32[4,128,128]{2,1,0:T(8,128)} %packed_diagonal.1) | copy-start | bytes 786436
  11.3 58.2 %collective-permute-start.2 = (f32[640,1024]{1,0:T(8,128)}, f32[640,1024]{1,0:T(8,128)}, u32[]{:S(2)}, u32[]{:S(2)}) collective-permute-start(f32[640,1024]{1,0:T(8,128)} %rows_of.8), channel_id=1, source_target_pairs={{0,24},{1,25},{2,26},{3,27},{4,28},{5,29},{6,30},{7,31},{8,16},{9,... | collective-permute-start | bytes 7864328 | tf_op jit(solution)/shard_map/ppermute | solution.py:329
  15.4 57.8 %collective-permute-start.1 = (f32[640,1024]{1,0:T(8,128)}, f32[640,1024]{1,0:T(8,128)S(1)}, u32[]{:S(2)}, u32[]{:S(2)}) collective-permute-start(f32[640,1024]{1,0:T(8,128)} %get-tuple-element.35), channel_id=1, source_target_pairs={{0,1},{1,0},{2,3},{3,2},{4,5},{5,4},{6,7},{7,6},{8,9},{9,8},{10,11... | collective-permute-start | bytes 7864328 | tf_op jit(solution)/shard_map/ppermute | solution.py:329
  16.5 10.9 %collective-permute-start.4 = (f32[8,128,128]{2,1,0:T(8,128)S(1)}, f32[8,128,128]{2,1,0:T(8,128)}, u32[]{:S(2)}, u32[]{:S(2)}) collective-permute-start(f32[8,128,128]{2,1,0:T(8,128)S(1)} %bitcast.14), channel_id=1, source_target_pairs={{0,4},{1,5},{10,14},{11,15},{20,16},{21,17},{30,26},{31,27}} | collective-permute-start | bytes 1572872 | tf_op jit(solution)/shard_map/ppermute | solution.py:329
  24.9 49.8 %collective-permute-start.3 = (f32[640,1024]{1,0:T(8,128)}, f32[640,1024]{1,0:T(8,128)}, u32[]{:S(2)}, u32[]{:S(2)}) collective-permute-start(f32[640,1024]{1,0:T(8,128)} %rows_of.9), channel_id=1, source_target_pairs={{0,8},{1,9},{2,10},{3,11},{4,12},{5,13},{6,14},{7,15},{8,0},{9,1},... | collective-permute-start | bytes 7864328 | tf_op jit(solution)/shard_map/ppermute | solution.py:329
  28.3 31.3 %collective-permute-start.5 = (f32[8,128,128]{2,1,0:T(8,128)}, f32[8,128,128]{2,1,0:T(8,128)S(1)}, u32[]{:S(2)}, u32[]{:S(2)}) collective-permute-start(f32[8,128,128]{2,1,0:T(8,128)} %broadcast_select_fusion), channel_id=1, source_target_pairs={{0,2},{1,3},{4,6},{5,7},{10,8},{11,9},{14,12},{15,13},{16,18},{17,... | collective-permute-start | bytes 1572872 | tf_op jit(solution)/shard_map/ppermute | solution.py:329
  35.7 2.1 copy-start.12
  74.8 58.3 %collective-permute-start.7 = (f32[640,1024]{1,0:T(8,128)}, f32[640,1024]{1,0:T(8,128)S(1)}, u32[]{:S(2)}, u32[]{:S(2)}) collective-permute-start(f32[640,1024]{1,0:T(8,128)} %get-tuple-element.44), channel_id=1, source_target_pairs={{0,1},{1,0},{2,3},{3,2},{4,5},{5,4},{6,7},{7,6},{8,9},{9,8},{10,11... | collective-permute-start | bytes 7864328 | tf_op jit(solution)/shard_map/ppermute | solution.py:329
  76.3 61.4 %collective-permute-start.9 = (f32[76,128,128]{2,1,0:T(8,128)}, f32[76,128,128]{2,1,0:T(8,128)}, u32[]{:S(2)}, u32[]{:S(2)}) collective-permute-start(f32[76,128,128]{2,1,0:T(8,128)} %get-tuple-element.49.refs_0_.refs_4_), channel_id=1, source_target_pairs={{0,16},{1,17},{10,26},{11,27},{20,4},{21,5},{30,14},{31,15}} | collective-permute-start | bytes 14942216 | tf_op jit(solution)/shard_map/ppermute | solution.py:329
  85.3 52.4 %collective-permute-start.10 = (f32[76,128,128]{2,1,0:T(8,128)}, f32[76,128,128]{2,1,0:T(8,128)}, u32[]{:S(2)}, u32[]{:S(2)}) collective-permute-start(f32[76,128,128]{2,1,0:T(8,128)} %get-tuple-element.49.refs_0_.refs_4_), channel_id=1, source_target_pairs={{0,8},{1,9},{10,2},{11,3},{20,28},{21,29},{30,22},{31,23}} | collective-permute-start | bytes 14942216 | tf_op jit(solution)/shard_map/ppermute | solution.py:329
  91.5 46.2 %collective-permute-start.8 = (f32[640,640]{1,0:T(8,128)}, f32[640,640]{1,0:T(8,128)}, u32[]{:S(2)}, u32[]{:S(2)}) collective-permute-start(f32[640,640]{1,0:T(8,128)} %constant_dynamic-slice_fusion.5), channel_id=1, source_target_pairs={{0,2},{1,7},{2,4},{3,1},{4,6},{5,3},{6,0},{7,5},{8,10},{9,15},{10,... | collective-permute-start | bytes 4915208 | tf_op jit(solution)/shard_map/ppermute | solution.py:329
  133.0 1.6 copy-start.2
  137.7 3.1 %copy-start.6 = (f32[256,1024]{1,0:T(8,128)S(1)}, f32[256,1024]{1,0:T(8,128)}, u32[]{:S(2)}) copy-start(f32[256,1024]{1,0:T(8,128)} %get-tuple-element.42) | copy-start | bytes 3145732
  137.7 12.6 %collective-permute-start.11 = (f32[76,128,128]{2,1,0:T(8,128)}, f32[76,128,128]{2,1,0:T(8,128)}, u32[]{:S(2)}, u32[]{:S(2)}) collective-permute-start(f32[76,128,128]{2,1,0:T(8,128)} %get-tuple-element.52.refs_2_.refs_6_), channel_id=1, source_target_pairs={{4,12},{5,13},{14,6},{15,7},{16,24},{17,25},{26,18},{27,19}} | collective-permute-start | bytes 14942216 | tf_op jit(solution)/shard_map/ppermute | solution.py:329
  140.8 32.4 %collective-permute-start.6 = (f32[256,1024]{1,0:T(8,128)S(1)}, f32[256,1024]{1,0:T(8,128)S(1)}, u32[]{:S(2)}, u32[]{:S(2)}) collective-permute-start(f32[256,1024]{1,0:T(8,128)S(1)} %copy-done.6), channel_id=1, source_target_pairs={{0,1},{1,0},{2,3},{3,2},{4,5},{5,4},{6,7},{7,6},{8,9},{9,8},{10,11... | collective-permute-start | bytes 3145736 | tf_op jit(solution)/shard_map/ppermute | solution.py:329
  144.0 40.7 %collective-permute-start.15 = (f32[640,640]{1,0:T(8,128)}, f32[640,640]{1,0:T(8,128)}, u32[]{:S(2)}, u32[]{:S(2)}) collective-permute-start(f32[640,640]{1,0:T(8,128)} %constant_dynamic-slice_fusion.2), channel_id=1, source_target_pairs={{0,2},{1,7},{2,4},{3,1},{4,6},{5,3},{6,0},{7,5},{8,10},{9,15},{10,... | collective-permute-start | bytes 4915208 | tf_op jit(solution)/shard_map/ppermute | solution.py:329
  145.4 52.8 %collective-permute-start.14 = (f32[256,1024]{1,0:T(8,128)}, f32[256,1024]{1,0:T(8,128)S(1)}, u32[]{:S(2)}, u32[]{:S(2)}) collective-permute-start(f32[256,1024]{1,0:T(8,128)} %get-tuple-element.58), channel_id=1, source_target_pairs={{0,1},{1,0},{2,3},{3,2},{4,5},{5,4},{6,7},{7,6},{8,9},{9,8},{10,11... | collective-permute-start | bytes 3145736 | tf_op jit(solution)/shard_map/ppermute | solution.py:329
  146.9 2.1 copy-start.13
  174.1 34.8 %collective-permute-start.12 = (f32[256,1024]{1,0:T(8,128)}, f32[256,1024]{1,0:T(8,128)S(1)}, u32[]{:S(2)}, u32[]{:S(2)}) collective-permute-start(f32[256,1024]{1,0:T(8,128)} %get-tuple-element.56), channel_id=1, source_target_pairs={{0,1},{1,0},{2,3},{3,2},{4,5},{5,4},{6,7},{7,6},{8,9},{9,8},{10,11... | collective-permute-start | bytes 3145736 | tf_op jit(solution)/shard_map/ppermute | solution.py:329
  176.4 24.1 %collective-permute-start.13 = (f32[256,640]{1,0:T(8,128)S(1)}, f32[256,640]{1,0:T(8,128)}, u32[]{:S(2)}, u32[]{:S(2)}) collective-permute-start(f32[256,640]{1,0:T(8,128)S(1)} %constant_dynamic-slice_fusion.3), channel_id=1, source_target_pairs={{0,2},{1,7},{2,4},{3,1},{4,6},{5,3},{6,0},{7,5},{8,10},{9,15},{10,... | collective-permute-start | bytes 1966088 | tf_op jit(solution)/shard_map/ppermute | solution.py:329
  200.4 19.5 %collective-permute-start.17 = (f32[256,640]{1,0:T(8,128)S(1)}, f32[256,640]{1,0:T(8,128)S(1)}, u32[]{:S(2)}, u32[]{:S(2)}) collective-permute-start(f32[256,640]{1,0:T(8,128)S(1)} %constant_dynamic-slice_fusion), channel_id=1, source_target_pairs={{0,2},{1,7},{2,4},{3,1},{4,6},{5,3},{6,0},{7,5},{8,10},{9,15},{10,... | collective-permute-start | bytes 1966088 | tf_op jit(solution)/shard_map/ppermute | solution.py:329
  211.1 20.5 %collective-permute-start.16 = (f32[256,640]{1,0:T(8,128)S(1)}, f32[256,640]{1,0:T(8,128)S(1)}, u32[]{:S(2)}, u32[]{:S(2)}) collective-permute-start(f32[256,640]{1,0:T(8,128)S(1)} %constant_dynamic-slice_fusion.1), channel_id=1, source_target_pairs={{0,2},{1,7},{2,4},{3,1},{4,6},{5,3},{6,0},{7,5},{8,10},{9,15},{10,... | collective-permute-start | bytes 1966088 | tf_op jit(solution)/shard_map/ppermute | solution.py:329
  (8 other events, 7.7 us)

commit v6 on v5

--- a/solution.py
+++ b/solution.py
@@ -300,7 +300,7 @@
     step = GROUP * BLOCK
     scalars = jnp.stack([odd, first]).astype(jnp.int32)
     band_rows = pl.BlockSpec((step, WINDOW), lambda g, s: (g, 0))
-    here = pl.BlockSpec((pl.Element(rows), pl.Element(step)), lambda g, s: (pl.multiple_of(s[1], BLOCK), g * step))
+    here = pl.BlockSpec((pl.Element(rows), pl.Element(step)), lambda g, s: (pl.multiple_of(s[1], BLOCK // 2), g * step))
     return pl.pallas_call(
         right_kernel,
         out_shape=jax.ShapeDtypeStruct(total.shape, jnp.float32),
@@ -310,7 +310,7 @@
             in_specs=[
                 pl.BlockSpec((rows, cols), lambda g, s: (0, 0)),
                 pl.BlockSpec((rows, HALO), lambda g, s: (0, 0)),
-                pl.BlockSpec((pl.Element(rows), pl.Element(cols)), lambda g, s: (pl.multiple_of(s[1], BLOCK), 0)),
+                pl.BlockSpec((pl.Element(rows), pl.Element(cols)), lambda g, s: (pl.multiple_of(s[1], BLOCK // 2), 0)),
                 band_rows,
                 band_rows,
                 here,
@@ -339,12 +339,10 @@
 
 def cut(total):
     first = total * 5 // 16 // BLOCK * BLOCK
-    sizes = [first, first]
+    more = BLOCK // 2
     left = total - 2 * first
-    while left:
-        sizes.append(min(left, 2 * BLOCK))
-        left -= sizes[-1]
-    return sizes
+    third = -(-left // (2 * BLOCK)) * BLOCK
+    return [first, first + more, third - more, left - third - BLOCK, BLOCK]
 
 
 def rows_kernel(first, rows, out):

time: 243 us -> 247 us (1.016)
  starting transfers between devices: 35.6 us -> 40 us
  waiting for transfers between devices: 36.2 us -> 33.3 us
    ppermute x18, starting transfers between devices: 35.6 us -> 40 us  [send(): lax.ppermute(value, ('row', 'col'), [(a * cols + b, c * cols + d) for (a,...]
    ppermute x18, waiting for transfers between devices: 36.2 us -> 33.3 us  [send(): lax.ppermute(value, ('row', 'col'), [(a * cols + b, c * cols + d) for (a,...]
  transfers between devices with their start and end apart: 18 -> 18, of which waited for: 7 -> 5; matrix products, arithmetic and copies ran while one was open for 10% -> 11% of each run, Pallas kernels for 51% -> 51%
where the time goes in v6:
time: 247 us; the launch traced here: 245 us
  Pallas kernels  136 us (55%)
  starting transfers between devices  40 us (16%)
  waiting for transfers between devices  33.3 us (13%)
  local copies, waits for them, and re-layouts  23.9 us (10%)
  other arithmetic  11.2 us (5%)
    pallas_call x5, Pallas kernels, right_part(): pl.pallas_call(right_kernel, out_shape=jax.ShapeDtypeStruct(total.shape,...  53.6 us
    ppermute x18, starting transfers between devices, send(): lax.ppermute(value, ('row', 'col'), [(a * cols + b, c * cols + d) for (a,...  40 us
    ppermute x18, waiting for transfers between devices, send(): lax.ppermute(value, ('row', 'col'), [(a * cols + b, c * cols + d) for (a,...  33.3 us
    pallas_call x1, Pallas kernels, left_part(): pl.pallas_call(left_kernel, out_shape=jax.ShapeDtypeStruct((rows, cols),...  28 us
    pallas_call x2, Pallas kernels, band(): pl.pallas_call(functools.partial(band_kernel, sources=len(sources), half=...  24.3 us
    pallas_call x7, Pallas kernels, rows_of(): pl.pallas_call(rows_kernel, out_shape=jax.ShapeDtypeStruct((size, cols),...  20.3 us
    dynamic_slice x5, local copies, waits for them, and re-layouts, hand_strip_on(): lax.dynamic_slice_in_dim(pairs[j], (1 - odd) * (tile_cols - HALO), HALO, 1)  9.77 us
    unnamed x30, local copies, waits for them, and re-layouts  9.32 us
  transfers between devices with their start and end apart: 18, of which 5 were waited for; matrix products, arithmetic and copies ran while one was open for 11% of the time, Pallas kernels for 51%

profile of v6, /device:TPU:0, one launch (start us, length us, event | category | flops | bytes accessed | tf_op | source)
XLA Modules:
  0.0 244.9 jit_solution(11725978515814329176)
XLA Ops:
  0.0 3.0 %packed_diagonal.1 = f32[4,128,128]{2,1,0:T(8,128)} custom-call(s32[1]{0:T(128)} %bitcast.1.first, f32[2048,1024]{1,0:T(8,128)} %own.11, f32[2048,1024]{1,0:T(8,128)} %own.11), custom_call_target="tpu_custom_call" | custom-call | flops 1 | bytes 1 | tf_op jit(solution)/shard_map/packed_diagonal/pallas_call | solution.py:377
  3.0 4.9 %collective-permute-start = (f32[4,128,128]{2,1,0:T(8,128)}, f32[4,128,128]{2,1,0:T(8,128)S(1)}, u32[]{:S(2)}, u32[]{:S(2)}) collective-permute-start(f32[4,128,128]{2,1,0:T(8,128)} %packed_diagonal.1), channel_id=1, source_target_pairs={{0,1},{1,0},{10,11},{11,10},{20,21},{21,20},{30,31},{31,30}} | collective-permute-start | bytes 786440 | tf_op jit(solution)/shard_map/ppermute | solution.py:329
  7.9 3.4 %rows_of.8 = f32[640,1024]{1,0:T(8,128)} custom-call(s32[1]{0:T(128)} %bitcast.2.first, f32[2048,1024]{1,0:T(8,128)} %own.11), custom_call_target="tpu_custom_call" | custom-call | flops 1 | bytes 1 | tf_op jit(solution)/shard_map/rows_of/pallas_call | solution.py:355
  11.3 3.4 %rows_of.7.refs_1_ = f32[640,1024]{1,0:T(8,128)} custom-call(s32[1]{0:T(128)} %constant.103.clone.1.first, f32[2048,1024]{1,0:T(8,128)} %own.11), custom_call_target="tpu_custom_call" | custom-call | flops 1 | bytes 1 | tf_op jit(solution)/shard_map/rows_of/pallas_call | solution.py:355
  16.5 4.9 %collective-permute-start.4 = (f32[8,128,128]{2,1,0:T(8,128)S(1)}, f32[8,128,128]{2,1,0:T(8,128)}, u32[]{:S(2)}, u32[]{:S(2)}) collective-permute-start(f32[8,128,128]{2,1,0:T(8,128)S(1)} %bitcast.14), channel_id=1, source_target_pairs={{0,4},{1,5},{10,14},{11,15},{20,16},{21,17},{30,26},{31,27}} | collective-permute-start | bytes 1572872 | tf_op jit(solution)/shard_map/ppermute | solution.py:329
  21.5 3.4 %rows_of.9 = f32[640,1024]{1,0:T(8,128)} custom-call(s32[1]{0:T(128)} %bitcast.3.first, f32[2048,1024]{1,0:T(8,128)} %own.11), custom_call_target="tpu_custom_call" | custom-call | flops 1 | bytes 1 | tf_op jit(solution)/shard_map/rows_of/pallas_call | solution.py:355
  30.3 3.7 %rows_of.10.refs_5_ = f32[704,1024]{1,0:T(8,128)} custom-call(s32[1]{0:T(128)} %constant.113.clone.1.first, f32[2048,1024]{1,0:T(8,128)} %own.11), custom_call_target="tpu_custom_call" | custom-call | flops 1 | bytes 1 | tf_op jit(solution)/shard_map/rows_of/pallas_call | solution.py:355
  39.6 14.9 %band.2 = (bf16[2048,1536]{1,0:T(8,128)(2,1)}, bf16[2048,1536]{1,0:T(8,128)(2,1)}) custom-call(s32[16,9]{1,0:T(8,128)} %fusion.2.places, f32[16]{0:T(128)} %dynamic_slice.30.gains, s32[3]{0:T(128)} %broadcast_12_scalars.2.scalars, f32[144,128,128]{2,1,0:T(8,128)} %bitcast.11), custom_call_target="tpu_custom_call" | custom-call | flops 1 | bytes 1 | tf_op jit(solution)/shard_map/band/pallas_call | solution.py:176
  63.0 7.1 %add_onsite.1 = (bf16[2048,1536]{1,0:T(8,128)(2,1)}, bf16[2048,1536]{1,0:T(8,128)(2,1)}) custom-call(f32[16]{0:T(128)} %dynamic_slice.30.gains, f32[8,128,128]{2,1,0:T(8,128)} %broadcast_select_fusion.1.refs_0_.refs_1_, f32[8,128,128]{2,1,0:T(8,128)} %broadcast_select_fusion.1.refs_0_.refs_1_, ...), custom_call_target="tpu_custom_call", output_to_operand_aliasing={{0}: (3, {}), {1}: (4, {})} | custom-call | flops 1 | bytes 1 | tf_op jit(solution)/shard_map/add_onsite/pallas_call | solution.py:219
  70.1 3.1 %collective-permute-done.1.refs_0_ = f32[640,1024]{1,0:T(8,128)S(1)} collective-permute-done((f32[640,1024]{1,0:T(8,128)}, f32[640,1024]{1,0:T(8,128)S(1)}, u32[]{:S(2)}, u32[]{:S(2)}) %collective-permute-start.1) | collective-permute-done | bytes 2621472 | tf_op jit(solution)/shard_map/ppermute | solution.py:329
  76.3 9.7 %collective-permute-start.9 = (f32[76,128,128]{2,1,0:T(8,128)}, f32[76,128,128]{2,1,0:T(8,128)}, u32[]{:S(2)}, u32[]{:S(2)}) collective-permute-start(f32[76,128,128]{2,1,0:T(8,128)} %get-tuple-element.49.refs_0_.refs_4_), channel_id=1, source_target_pairs={{0,16},{1,17},{10,26},{11,27},{20,4},{21,5},{30,14},{31,15}} | collective-permute-start | bytes 14942216 | tf_op jit(solution)/shard_map/ppermute | solution.py:329
  86.0 3.5 %collective-permute-start.10 = (f32[76,128,128]{2,1,0:T(8,128)}, f32[76,128,128]{2,1,0:T(8,128)}, u32[]{:S(2)}, u32[]{:S(2)}) collective-permute-start(f32[76,128,128]{2,1,0:T(8,128)} %get-tuple-element.49.refs_0_.refs_4_), channel_id=1, source_target_pairs={{0,8},{1,9},{10,2},{11,3},{20,28},{21,29},{30,22},{31,23}} | collective-permute-start | bytes 14942216 | tf_op jit(solution)/shard_map/ppermute | solution.py:329
  92.2 28.0 %left_part.1.refs_2_ = f32[2048,1024]{1,0:T(8,128)} custom-call(s32[1]{0:T(128)} %bitcast.8.up, f32[640,1024]{1,0:T(8,128)} %get-tuple-element.45.inner, f32[2048,1024]{1,0:T(8,128)} %own.11, f32[640,1024]{1,0:T(8,128)} %get-tuple-element.46.outer, bf16[2048,1536]{1,0:T(8,128)(2,1)} %get-tuple-element.47.high, bf16[2048,1536]{1,0:T(8,128)(2,1)} %get-tuple-element.48.low), custom_call_target="tpu_custom_call" | custom-call | flops 1 | bytes 1 | tf_op jit(solution)/shard_map/left_part/pallas_call | solution.py:254
  120.2 18.4 %collective-permute-done.7.refs_0_ = f32[704,1024]{1,0:T(8,128)S(1)} collective-permute-done((f32[704,1024]{1,0:T(8,128)}, f32[704,1024]{1,0:T(8,128)S(1)}, u32[]{:S(2)}, u32[]{:S(2)}) %collective-permute-start.7) | collective-permute-done | bytes 2883616 | tf_op jit(solution)/shard_map/ppermute | solution.py:329
  140.3 2.9 %collective-permute-start.11 = (f32[76,128,128]{2,1,0:T(8,128)}, f32[76,128,128]{2,1,0:T(8,128)}, u32[]{:S(2)}, u32[]{:S(2)}) collective-permute-start(f32[76,128,128]{2,1,0:T(8,128)} %get-tuple-element.52.refs_2_.refs_6_), channel_id=1, source_target_pairs={{4,12},{5,13},{14,6},{15,7},{16,24},{17,25},{26,18},{27,19}} | collective-permute-start | bytes 14942216 | tf_op jit(solution)/shard_map/ppermute | solution.py:329
  147.8 3.0 %collective-permute-start.15 = (f32[704,640]{1,0:T(8,128)}, f32[704,640]{1,0:T(8,128)}, u32[]{:S(2)}, u32[]{:S(2)}) collective-permute-start(f32[704,640]{1,0:T(8,128)} %constant_dynamic-slice_fusion.2), channel_id=1, source_target_pairs={{0,2},{1,7},{2,4},{3,1},{4,6},{5,3},{6,0},{7,5},{8,10},{9,15},{10,... | collective-permute-start | bytes 5406728 | tf_op jit(solution)/shard_map/ppermute | solution.py:329
  155.5 9.4 %band.3 = (bf16[1024,1536]{1,0:T(8,128)(2,1)}, bf16[1024,1536]{1,0:T(8,128)(2,1)}) custom-call(s32[8,9]{1,0:T(8,128)} %fusion.5.places, f32[8]{0:T(128)} %dynamic_slice.35.gains, s32[3]{0:T(128)} %pad_add_fusion.2.scalars, f32[76,128,128]{2,1,0:T(8,128)} %get-tuple-element.49.refs_0_.refs_4_, f32[76,128,128]{2,1,0:T(8,128)} %get-tuple-element.51.refs_1_.refs_5_, ...), custom_call_target="tpu_custom_call" | custom-call | flops 1 | bytes 1 | tf_op jit(solution)/shard_map/band/pallas_call | solution.py:176
  164.8 13.5 %right_part.5.refs_1_ = f32[2048,1024]{1,0:T(8,128)} custom-call(s32[2]{0:T(128)} %pad_add_fusion.1.scalars, f32[640,1024]{1,0:T(8,128)} %get-tuple-element.43.pair, f32[640,640]{1,0:T(8,128)} %get-tuple-element.50.strip, f32[2048,1024]{1,0:T(8,128)} %own.11, bf16[1024,1536]{1,0:T(8,128)(2,1)} %get-tuple-element.53.high, ...), custom_call_target="tpu_custom_call", output_to_operand_aliasing={{}: (6, {})} | custom-call | flops 1 | bytes 1 | tf_op jit(solution)/shard_map/right_part/pallas_call | solution.py:304
  185.1 6.4 %collective-permute-done.15.strip = f32[704,640]{1,0:T(8,128)} collective-permute-done((f32[704,640]{1,0:T(8,128)}, f32[704,640]{1,0:T(8,128)}, u32[]{:S(2)}, u32[]{:S(2)}) %collective-permute-start.15) | collective-permute-done | bytes 1802272 | tf_op jit(solution)/shard_map/ppermute | solution.py:329
  191.5 14.4 %right_part.6.refs_1_ = f32[2048,1024]{1,0:T(8,128)} custom-call(s32[2]{0:T(128)} %pad_add_fusion.4.scalars, f32[704,1024]{1,0:T(8,128)} %get-tuple-element.59.pair, f32[704,640]{1,0:T(8,128)} %collective-permute-done.15.strip, f32[2048,1024]{1,0:T(8,128)} %own.11, bf16[1024,1536]{1,0:T(8,128)(2,1)} %get-tuple-element.53.high, ...), custom_call_target="tpu_custom_call", output_to_operand_aliasing={{}: (6, {})} | custom-call | flops 1 | bytes 1 | tf_op jit(solution)/shard_map/right_part/pallas_call | solution.py:304
  210.6 9.3 %right_part.7.refs_1_ = f32[2048,1024]{1,0:T(8,128)} custom-call(s32[2]{0:T(128)} %pad_add_fusion.3.scalars, f32[320,1024]{1,0:T(8,128)} %get-tuple-element.57.pair, f32[320,640]{1,0:T(8,128)} %collective-permute-done.13.strip, f32[2048,1024]{1,0:T(8,128)} %own.11, bf16[1024,1536]{1,0:T(8,128)(2,1)} %get-tuple-element.53.high, ...), custom_call_target="tpu_custom_call", output_to_operand_aliasing={{}: (6, {})} | custom-call | flops 1 | bytes 1 | tf_op jit(solution)/shard_map/right_part/pallas_call | solution.py:304
  223.9 3.1 %collective-permute-done.17.strip = f32[256,640]{1,0:T(8,128)S(1)} collective-permute-done((f32[256,640]{1,0:T(8,128)S(1)}, f32[256,640]{1,0:T(8,128)S(1)}, u32[]{:S(2)}, u32[]{:S(2)}) %collective-permute-start.17) | collective-permute-done | bytes 655392 | tf_op jit(solution)/shard_map/ppermute | solution.py:329
  227.8 8.5 %right_part.8.total = f32[2048,1024]{1,0:T(8,128)} custom-call(s32[2]{0:T(128)} %get-tuple-element.66.scalars, f32[256,1024]{1,0:T(8,128)} %get-tuple-element.63.pair, f32[256,640]{1,0:T(8,128)} %copy-done.10, f32[2048,1024]{1,0:T(8,128)} %own.11, bf16[1024,1536]{1,0:T(8,128)(2,1)} %get-tuple-element.53.high, ...), custom_call_target="tpu_custom_call", output_to_operand_aliasing={{}: (6, {})} | custom-call | flops 1 | bytes 1 | tf_op jit(solution)/shard_map/right_part/pallas_call | solution.py:304
  237.1 7.9 %right_part.9 = f32[2048,1024]{1,0:T(8,128)} custom-call(s32[2]{0:T(128)} %get-tuple-element.65.scalars, f32[128,1024]{1,0:T(8,128)} %get-tuple-element.62.pair, f32[128,640]{1,0:T(8,128)} %copy-done.11, f32[2048,1024]{1,0:T(8,128)} %own.11, bf16[1024,1536]{1,0:T(8,128)(2,1)} %get-tuple-element.53.high, ...), custom_call_target="tpu_custom_call", output_to_operand_aliasing={{}: (6, {})} | custom-call | flops 1 | bytes 1 | tf_op jit(solution)/shard_map/right_part/pallas_call | solution.py:304
  (94 shorter events, 55.0 us)
Async XLA Ops:
  0.0 24.9 %copy-start = (s32[64,9]{0,1:T(8,128)S(1)}, s32[64,9]{0,1:T(8,128)}, u32[]{:S(2)}) copy-start(s32[64,9]{0,1:T(8,128)} %param.6) | copy-start | bytes 6916
  3.0 11.7 %collective-permute-start = (f32[4,128,128]{2,1,0:T(8,128)}, f32[4,128,128]{2,1,0:T(8,128)S(1)}, u32[]{:S(2)}, u32[]{:S(2)}) collective-permute-start(f32[4,128,128]{2,1,0:T(8,128)} %packed_diagonal.1), channel_id=1, source_target_pairs={{0,1},{1,0},{10,11},{11,10},{20,21},{21,20},{30,31},{31,30}} | collective-permute-start | bytes 786440 | tf_op jit(solution)/shard_map/ppermute | solution.py:329
  11.3 4.2 %copy-start.7 = (f32[4,128,128]{2,1,0:T(8,128)S(1)}, f32[4,128,128]{2,1,0:T(8,128)}, u32[]{:S(2)}) copy-start(f32[4,128,128]{2,1,0:T(8,128)} %packed_diagonal.1) | copy-start | bytes 786436
  11.3 58.8 %collective-permute-start.2 = (f32[640,1024]{1,0:T(8,128)}, f32[640,1024]{1,0:T(8,128)}, u32[]{:S(2)}, u32[]{:S(2)}) collective-permute-start(f32[640,1024]{1,0:T(8,128)} %rows_of.8), channel_id=1, source_target_pairs={{0,24},{1,25},{2,26},{3,27},{4,28},{5,29},{6,30},{7,31},{8,16},{9,... | collective-permute-start | bytes 7864328 | tf_op jit(solution)/shard_map/ppermute | solution.py:329
  15.4 57.8 %collective-permute-start.1 = (f32[640,1024]{1,0:T(8,128)}, f32[640,1024]{1,0:T(8,128)S(1)}, u32[]{:S(2)}, u32[]{:S(2)}) collective-permute-start(f32[640,1024]{1,0:T(8,128)} %get-tuple-element.35), channel_id=1, source_target_pairs={{0,1},{1,0},{2,3},{3,2},{4,5},{5,4},{6,7},{7,6},{8,9},{9,8},{10,11... | collective-permute-start | bytes 7864328 | tf_op jit(solution)/shard_map/ppermute | solution.py:329
  16.5 10.9 %collective-permute-start.4 = (f32[8,128,128]{2,1,0:T(8,128)S(1)}, f32[8,128,128]{2,1,0:T(8,128)}, u32[]{:S(2)}, u32[]{:S(2)}) collective-permute-start(f32[8,128,128]{2,1,0:T(8,128)S(1)} %bitcast.14), channel_id=1, source_target_pairs={{0,4},{1,5},{10,14},{11,15},{20,16},{21,17},{30,26},{31,27}} | collective-permute-start | bytes 1572872 | tf_op jit(solution)/shard_map/ppermute | solution.py:329
  24.9 49.9 %collective-permute-start.3 = (f32[640,1024]{1,0:T(8,128)}, f32[640,1024]{1,0:T(8,128)}, u32[]{:S(2)}, u32[]{:S(2)}) collective-permute-start(f32[640,1024]{1,0:T(8,128)} %rows_of.9), channel_id=1, source_target_pairs={{0,8},{1,9},{2,10},{3,11},{4,12},{5,13},{6,14},{7,15},{8,0},{9,1},... | collective-permute-start | bytes 7864328 | tf_op jit(solution)/shard_map/ppermute | solution.py:329
  28.3 31.9 %collective-permute-start.5 = (f32[8,128,128]{2,1,0:T(8,128)}, f32[8,128,128]{2,1,0:T(8,128)S(1)}, u32[]{:S(2)}, u32[]{:S(2)}) collective-permute-start(f32[8,128,128]{2,1,0:T(8,128)} %broadcast_select_fusion), channel_id=1, source_target_pairs={{0,2},{1,3},{4,6},{5,7},{10,8},{11,9},{14,12},{15,13},{16,18},{17,... | collective-permute-start | bytes 1572872 | tf_op jit(solution)/shard_map/ppermute | solution.py:329
  36.4 2.1 copy-start.12
  74.8 63.9 %collective-permute-start.7 = (f32[704,1024]{1,0:T(8,128)}, f32[704,1024]{1,0:T(8,128)S(1)}, u32[]{:S(2)}, u32[]{:S(2)}) collective-permute-start(f32[704,1024]{1,0:T(8,128)} %get-tuple-element.44), channel_id=1, source_target_pairs={{0,1},{1,0},{2,3},{3,2},{4,5},{5,4},{6,7},{7,6},{8,9},{9,8},{10,11... | collective-permute-start | bytes 8650760 | tf_op jit(solution)/shard_map/ppermute | solution.py:329
  76.3 64.0 %collective-permute-start.9 = (f32[76,128,128]{2,1,0:T(8,128)}, f32[76,128,128]{2,1,0:T(8,128)}, u32[]{:S(2)}, u32[]{:S(2)}) collective-permute-start(f32[76,128,128]{2,1,0:T(8,128)} %get-tuple-element.49.refs_0_.refs_4_), channel_id=1, source_target_pairs={{0,16},{1,17},{10,26},{11,27},{20,4},{21,5},{30,14},{31,15}} | collective-permute-start | bytes 14942216 | tf_op jit(solution)/shard_map/ppermute | solution.py:329
  86.0 54.4 %collective-permute-start.10 = (f32[76,128,128]{2,1,0:T(8,128)}, f32[76,128,128]{2,1,0:T(8,128)}, u32[]{:S(2)}, u32[]{:S(2)}) collective-permute-start(f32[76,128,128]{2,1,0:T(8,128)} %get-tuple-element.49.refs_0_.refs_4_), channel_id=1, source_target_pairs={{0,8},{1,9},{10,2},{11,3},{20,28},{21,29},{30,22},{31,23}} | collective-permute-start | bytes 14942216 | tf_op jit(solution)/shard_map/ppermute | solution.py:329
  92.2 48.1 %collective-permute-start.8 = (f32[640,640]{1,0:T(8,128)}, f32[640,640]{1,0:T(8,128)}, u32[]{:S(2)}, u32[]{:S(2)}) collective-permute-start(f32[640,640]{1,0:T(8,128)} %constant_dynamic-slice_fusion.5), channel_id=1, source_target_pairs={{0,2},{1,7},{2,4},{3,1},{4,6},{5,3},{6,0},{7,5},{8,10},{9,15},{10,... | collective-permute-start | bytes 4915208 | tf_op jit(solution)/shard_map/ppermute | solution.py:329
  138.7 1.7 copy-start.1
  140.3 15.1 %collective-permute-start.11 = (f32[76,128,128]{2,1,0:T(8,128)}, f32[76,128,128]{2,1,0:T(8,128)}, u32[]{:S(2)}, u32[]{:S(2)}) collective-permute-start(f32[76,128,128]{2,1,0:T(8,128)} %get-tuple-element.52.refs_2_.refs_6_), channel_id=1, source_target_pairs={{4,12},{5,13},{14,6},{15,7},{16,24},{17,25},{26,18},{27,19}} | collective-permute-start | bytes 14942216 | tf_op jit(solution)/shard_map/ppermute | solution.py:329
  143.3 35.0 %collective-permute-start.6 = (f32[320,1024]{1,0:T(8,128)}, f32[320,1024]{1,0:T(8,128)S(1)}, u32[]{:S(2)}, u32[]{:S(2)}) collective-permute-start(f32[320,1024]{1,0:T(8,128)} %get-tuple-element.42), channel_id=1, source_target_pairs={{0,1},{1,0},{2,3},{3,2},{4,5},{5,4},{6,7},{7,6},{8,9},{9,8},{10,11... | collective-permute-start | bytes 3932168 | tf_op jit(solution)/shard_map/ppermute | solution.py:329
  147.8 4.9 %copy-start.13 = (f32[64]{0:T(128)S(1)}, f32[64]{0:T(128)}, u32[]{:S(2)}) copy-start(f32[64]{0:T(128)} %param.7) | copy-start | bytes 772
  147.8 6.3 %copy-start.5 = (f32[256,1024]{1,0:T(8,128)S(1)}, f32[256,1024]{1,0:T(8,128)}, u32[]{:S(2)}) copy-start(f32[256,1024]{1,0:T(8,128)} %get-tuple-element.58) | copy-start | bytes 3145732
  147.8 43.6 %collective-permute-start.15 = (f32[704,640]{1,0:T(8,128)}, f32[704,640]{1,0:T(8,128)}, u32[]{:S(2)}, u32[]{:S(2)}) collective-permute-start(f32[704,640]{1,0:T(8,128)} %constant_dynamic-slice_fusion.2), channel_id=1, source_target_pairs={{0,2},{1,7},{2,4},{3,1},{4,6},{5,3},{6,0},{7,5},{8,10},{9,15},{10,... | collective-permute-start | bytes 5406728 | tf_op jit(solution)/shard_map/ppermute | solution.py:329
  154.2 51.7 %collective-permute-start.14 = (f32[256,1024]{1,0:T(8,128)S(1)}, f32[256,1024]{1,0:T(8,128)S(1)}, u32[]{:S(2)}, u32[]{:S(2)}) collective-permute-start(f32[256,1024]{1,0:T(8,128)S(1)} %copy-done.5), channel_id=1, source_target_pairs={{0,1},{1,0},{2,3},{3,2},{4,5},{5,4},{6,7},{7,6},{8,9},{9,8},{10,11... | collective-permute-start | bytes 3145736 | tf_op jit(solution)/shard_map/ppermute | solution.py:329
  181.5 29.1 %collective-permute-start.13 = (f32[320,640]{1,0:T(8,128)}, f32[320,640]{1,0:T(8,128)}, u32[]{:S(2)}, u32[]{:S(2)}) collective-permute-start(f32[320,640]{1,0:T(8,128)} %constant_dynamic-slice_fusion.3), channel_id=1, source_target_pairs={{0,2},{1,7},{2,4},{3,1},{4,6},{5,3},{6,0},{7,5},{8,10},{9,15},{10,... | collective-permute-start | bytes 2457608 | tf_op jit(solution)/shard_map/ppermute | solution.py:329
  183.0 36.9 %collective-permute-start.12 = (f32[128,1024]{1,0:T(8,128)}, f32[128,1024]{1,0:T(8,128)S(1)}, u32[]{:S(2)}, u32[]{:S(2)}) collective-permute-start(f32[128,1024]{1,0:T(8,128)} %get-tuple-element.56), channel_id=1, source_target_pairs={{0,1},{1,0},{2,3},{3,2},{4,5},{5,4},{6,7},{7,6},{8,9},{9,8},{10,11... | collective-permute-start | bytes 1572872 | tf_op jit(solution)/shard_map/ppermute | solution.py:329
  208.0 19.0 %collective-permute-start.17 = (f32[256,640]{1,0:T(8,128)S(1)}, f32[256,640]{1,0:T(8,128)S(1)}, u32[]{:S(2)}, u32[]{:S(2)}) collective-permute-start(f32[256,640]{1,0:T(8,128)S(1)} %constant_dynamic-slice_fusion), channel_id=1, source_target_pairs={{0,2},{1,7},{2,4},{3,1},{4,6},{5,3},{6,0},{7,5},{8,10},{9,15},{10,... | collective-permute-start | bytes 1966088 | tf_op jit(solution)/shard_map/ppermute | solution.py:329
  221.7 14.6 %collective-permute-start.16 = (f32[128,640]{1,0:T(8,128)S(1)}, f32[128,640]{1,0:T(8,128)S(1)}, u32[]{:S(2)}, u32[]{:S(2)}) collective-permute-start(f32[128,640]{1,0:T(8,128)S(1)} %constant_dynamic-slice_fusion.1), channel_id=1, source_target_pairs={{0,2},{1,7},{2,4},{3,1},{4,6},{5,3},{6,0},{7,5},{8,10},{9,15},{10,... | collective-permute-start | bytes 983048 | tf_op jit(solution)/shard_map/ppermute | solution.py:329
  (8 other events, 7.5 us)
